TPU v7x, 32 devices: a whole 2x2x4 slice. The times are simulated.
32 devices in a mesh: groups: 2 (over y), pool: 4 (over z), tp: 2 (over x), pair: 2 (over core).
Axes of the slice: x: 2, y: 2, z: 4, core: 2. Of those that a mesh axis runs over, the one named last changes fastest.
Arguments:
- tokens: bfloat16 [2048, 4096], P(('groups', 'pool', 'pair'), 'tp'), parts along dimension 0, may hold values from -6 to 6
- routes: int32 [2048, 8], P(('groups', 'pool', 'pair')), parts along dimension 0, may hold values from 0 to 127, as said below
- gate_weights: int32 [2048, 8], P(('groups', 'pool', 'pair')), parts along dimension 0, may hold values from 1 to 255
- w_gate: bfloat16 [8, 4096, 1024], P(('pool', 'pair'), None, 'tp'), may hold values from -0.09375 to 0.09375
- w_up: bfloat16 [8, 4096, 1024], P(('pool', 'pair'), None, 'tp'), may hold values from -0.09375 to 0.09375
- w_down: bfloat16 [8, 1024, 4096], P(('pool', 'pair'), 'tp'), may hold values from -0.75 to 0.75
Outputs:
- mixed: bfloat16 [2048, 4096], P(('groups', 'pool', 'pair'), 'tp'), parts along dimension 0
There are 2 independent parts, one for each index of `groups`. A program takes and returns all parts, laid end to end along the dimension named above; an argument that names none is the same for every part. Nothing has to cross between parts.
Inputs may be any that keep to these rules, and one draw needn't show every extreme that they name: `routes`: each row names 8 different experts; within the rows of one index of pool and pair (aligned blocks of 128 rows) no expert is named by more than 16 rows.
All inputs are finite; a program needn't handle non-finite values.
Results may differ from a plain program's by a relative error of at most 0.0085.
Values may be sent and summed in bfloat16 or wider, within the bound.
No kernel may reach another device: no remote copies, remote signals or barrier semaphores. Data moves between devices by JAX's collectives and lax.ppermute only.
A program may use at most 64 MiB of HBM per device.

v0:
```python
import jax
import jax.numpy as jnp
from jax import lax
from jax.sharding import PartitionSpec as P

D = 4096
CAP = 16


def body(tokens, routes, gate_weights, w_gate, w_up, w_down):
    groups = lax.axis_size(("pool", "pair"))
    parts_tp = lax.axis_size("tp")
    width_local = D // parts_tp
    expert_ids = jnp.arange(groups, dtype=jnp.int32)
    match = routes[:, :, None] == expert_ids[None, None, :]
    hits = jnp.sum(match.astype(jnp.int32), axis=1)
    totals = jnp.sum(gate_weights, axis=1).astype(jnp.float32)
    weighted = jnp.sum(match.astype(jnp.int32) * gate_weights[:, :, None], axis=1)
    share = weighted.astype(jnp.float32) / totals[:, None]
    hits_t = hits.T
    slot_t = (jnp.cumsum(hits, axis=0) - hits).T
    slot_ids = jnp.arange(CAP, dtype=jnp.int32)
    picked = (hits_t[:, None, :] == 1) & (slot_t[:, None, :] == slot_ids[None, :, None])
    select = picked.astype(jnp.bfloat16)
    mixing = picked.astype(jnp.float32) * share.T[:, None, :]
    gate_mat = w_gate[0]
    up_mat = w_up[0]
    down_mat = w_down[0]
    whole = lax.all_gather(tokens, "tp", axis=1, tiled=True)
    outgoing = jnp.einsum("gcr,rd->gcd", select, whole, preferred_element_type=jnp.float32).astype(
        jnp.bfloat16
    )
    block_rows = lax.all_to_all(outgoing, ("pool", "pair"), split_axis=0, concat_axis=0, tiled=True)
    gate = jnp.einsum("gnd,df->gnf", block_rows, gate_mat, preferred_element_type=jnp.float32)
    up = jnp.einsum("gnd,df->gnf", block_rows, up_mat, preferred_element_type=jnp.float32)
    hidden = (jax.nn.silu(gate) * up).astype(jnp.bfloat16)
    hidden_rows = hidden.reshape(groups * CAP, hidden.shape[2])
    highest = lax.Precision.HIGHEST
    summed = lax.psum_scatter(
        lax.dot_general(
            down_mat, hidden_rows, (((0,), (1,)), ((), ())), preferred_element_type=jnp.float32
        ).astype(jnp.bfloat16),
        "tp",
        scatter_dimension=0,
        tiled=True,
    )
    outcome = summed.reshape(width_local, groups, CAP)
    returned = lax.all_to_all(outcome, ("pool", "pair"), split_axis=1, concat_axis=1, tiled=True)
    mixed = jnp.einsum("gcr,dgc->rd", mixing, returned.astype(jnp.float32), precision=highest)
    return mixed.astype(jnp.bfloat16)


def solution(mesh):
    in_specs = (
        P(("groups", "pool", "pair"), "tp"),
        P(("groups", "pool", "pair"), None),
        P(("groups", "pool", "pair"), None),
        P(("pool", "pair"), None, "tp"),
        P(("pool", "pair"), None, "tp"),
        P(("pool", "pair"), "tp", None),
    )
    out_specs = P(("groups", "pool", "pair"), "tp")
    return jax.shard_map(body, mesh=mesh, in_specs=in_specs, out_specs=out_specs, check_vma=False)
```

profile of v0, /device:TPU:0, one launch (start us, length us, event | category | flops | bytes accessed | tf_op | source)
XLA Modules:
  0.0 117.3 jit_solution(12629188055976460437)
XLA Ops:
  6.5 0.0 all-gather.2.cloned.1.call-start
  6.5 0.7 all-gather.2.cloned.1.call-update
  7.3 0.0 reduce-scatter.2.cloned.1.call-start
  7.3 0.7 select_reduce_fusion
  8.0 0.1 copy.11
  8.1 0.2 reduce_window_sum.11
  8.4 24.6 %all-gather.2.cloned.1.call-done = bf16[128,4096]{1,0:T(8,128)(2,1)} async-done(((bf16[128,2048]{1,0:T(8,128)(2,1)}), bf16[128,4096]{1,0:T(8,128)(2,1)}) %all-gather.2.cloned.1.call-update) | async-done | bytes 1048592 | tf_op jit(solution)/shard_map/all_gather | solution.py:29
  32.9 1.8 %convolution_convert_fusion.1 = bf16[8,16,4096]{2,1,0:T(8,128)(2,1)S(1)} fusion(bf16[128,4096]{1,0:T(8,128)(2,1)} %all-gather.2.cloned.1.call-done, s32[8,128]{1,0:T(8,128)S(1)} %copy.13, pred[8,128]{1,0:T(8,128)(4,1)S(1)} %compare_bitcast_fusion), kind=kOutput, calls=%fused_computation.1 | convolution fusion | flops 134774784 | bytes 2102272 | tf_op jit(solution)/shard_map/gcr,rd->gcd/dot_general | solution.py:30
  34.7 0.0 copy-start.3
  34.8 31.3 %all_to_all.10 = bf16[8,16,4096]{2,1,0:T(8,128)(2,1)S(1)} all-to-all(bf16[8,16,4096]{2,1,0:T(8,128)(2,1)S(1)} %convolution_convert_fusion.1), channel_id=1, replica_groups=mesh['groups'=2,'pool'=4,'tp'=2,'pair'=2] {'pool','pair'}, dimensions={0} | all-to-all | bytes 2097152 | tf_op jit(solution)/shard_map/all_to_all | solution.py:33
  66.0 0.0 copy-done
  66.0 0.7 fusion.4
  66.7 0.0 copy-done.3
  66.8 0.0 copy-start.1
  66.8 0.7 fusion.10
  67.5 0.0 copy-start.2
  67.5 1.4 %copy-done.1 = bf16[1,512,4096]{2,1,0:T(8,128)(2,1)S(1)} copy-done((bf16[1,512,4096]{2,1,0:T(8,128)(2,1)S(1)}, bf16[1,512,4096]{2,1,0:T(8,128)(2,1)}, u32[]{:S(2)}) %copy-start.1) | copy-done | bytes 4194328
  68.9 1.7 %fusion = bf16[4096,128]{0,1:T(8,128)(2,1)} fusion(bf16[128,512]{1,0:T(8,128)(2,1)S(1)} %bitcast.37, bf16[1,512,4096]{2,1,0:T(8,128)(2,1)S(1)} %copy-done.1), kind=kOutput, calls=%fused_computation.2 | convolution fusion | flops 537395200 | bytes 5373952 | tf_op jit(solution)/shard_map/dot_general | solution.py:40
  70.7 0.0 reduce-scatter.2.cloned.1.call-update
  70.7 18.4 %reduce-scatter.2.cloned.1.call-done = bf16[2048,128]{0,1:T(8,128)(2,1)} async-done(((bf16[4096,128]{0,1:T(8,128)(2,1)}), bf16[2048,128]{0,1:T(8,128)(2,1)}) %reduce-scatter.2.cloned.1.call-update) | async-done | bytes 524304 | tf_op jit(solution)/shard_map/reduce_scatter | solution.py:39
  89.1 4.6 %all-to-all-start.1 = ((bf16[2048,8,16]{0,2,1:T(8,128)(2,1)}), bf16[2048,8,16]{0,2,1:T(8,128)(2,1)S(1)}, u32[]{:S(2)}, u32[]{:S(2)}) async-start(bf16[2048,8,16]{0,2,1:T(8,128)(2,1)} %bitcast.36), calls=%async_computation.2 | async-start | bytes 1048576 | tf_op jit(solution)/shard_map/all_to_all | solution.py:48
  93.7 0.0 copy-done.2
  93.7 15.3 %all-to-all-done.1 = bf16[2048,8,16]{0,2,1:T(8,128)(2,1)S(1)} async-done(((bf16[2048,8,16]{0,2,1:T(8,128)(2,1)}), bf16[2048,8,16]{0,2,1:T(8,128)(2,1)S(1)}, u32[]{:S(2)}, u32[]{:S(2)}) %all-to-all-start.1) | async-done | bytes 524320 | tf_op jit(solution)/shard_map/all_to_all | solution.py:48
  109.1 1.4 %fusion.6 = bf16[128,2048]{1,0:T(8,128)(2,1)} fusion(bf16[2048,8,16]{0,2,1:T(8,128)(2,1)S(1)} %all-to-all-done.1, f32[8,128]{1,0:T(8,128)S(1)} %divide_bitcast_fusion, s32[8,128]{1,0:T(8,128)S(1)} %copy.13, pred[8,128]{1,0:T(8,128)(4,1)S(1)} %compare_bitcast_fusion), kind=kOutput, calls=%fused_computation.9 | convolution fusion | flops 402964480 | bytes 1057792 | tf_op jit(solution)/shard_map/gcr,dgc->rd/dot_general | solution.py:49
  (7 shorter events, 0.1 us)
Async XLA Ops:
  6.5 26.4 %all-gather.2.cloned.1.call-start = ((), (), s32[]{:S(2)}) async-start(), calls=%async_computation.3 | async-start | bytes 1572864 | tf_op jit(solution)/shard_map/all_gather | solution.py:29
  7.3 81.8 %reduce-scatter.2.cloned.1.call-start = ((), (), s32[]{:S(2)}) async-start(), calls=%async_computation.4 | async-start | bytes 1572864 | tf_op jit(solution)/shard_map/reduce_scatter | solution.py:39
  32.9 33.1 %copy-start = (bf16[1,4096,512]{2,1,0:T(8,128)(2,1)S(1)}, bf16[1,4096,512]{2,1,0:T(8,128)(2,1)}, u32[]{:S(2)}) copy-start(bf16[1,4096,512]{2,1,0:T(8,128)(2,1)} %param.9) | copy-start | bytes 12582916
  34.7 32.0 %copy-start.3 = (bf16[1,4096,512]{2,1,0:T(8,128)(2,1)S(1)}, bf16[1,4096,512]{2,1,0:T(8,128)(2,1)}, u32[]{:S(2)}) copy-start(bf16[1,4096,512]{2,1,0:T(8,128)(2,1)} %param.10) | copy-start | bytes 12582916
  66.8 2.2 %copy-start.1 = (bf16[1,512,4096]{2,1,0:T(8,128)(2,1)S(1)}, bf16[1,512,4096]{2,1,0:T(8,128)(2,1)}, u32[]{:S(2)}) copy-start(bf16[1,512,4096]{2,1,0:T(8,128)(2,1)} %param.11) | copy-start | bytes 12582916
  67.5 26.2 %copy-start.2 = (s32[128,8]{0,1:T(8,128)S(1)}, s32[128,8]{0,1:T(8,128)}, u32[]{:S(2)}) copy-start(s32[128,8]{0,1:T(8,128)} %param.8) | copy-start | bytes 12292
  89.1 20.0 %all-to-all-start.1 = ((bf16[2048,8,16]{0,2,1:T(8,128)(2,1)}), bf16[2048,8,16]{0,2,1:T(8,128)(2,1)S(1)}, u32[]{:S(2)}, u32[]{:S(2)}) async-start(bf16[2048,8,16]{0,2,1:T(8,128)(2,1)} %bitcast.36), calls=%async_computation.2 | async-start | bytes 1048576 | tf_op jit(solution)/shard_map/all_to_all | solution.py:48
Sparse Core Ops, SparseCore 0:
  8.9 23.9 all-gather.1
  70.8 18.2 reduce-scatter.1
where the time goes:
time: 118 us; the launch traced here: 117 us
  waiting for transfers between devices  59 us (50%)
  blocking collectives  31.3 us (27%)
  between operations  13.5 us (11%)
  matrix products  6.36 us (5%)
  starting transfers between devices  4.65 us (4%)
  local copies, waits for them, and re-layouts  1.61 us (1%)
    all_to_all x1, blocking collectives, body(): lax.all_to_all(outgoing, ('pool', 'pair'), split_axis=0, concat_axis=0, t...  31.3 us
    all_gather x1, waiting for transfers between devices, body(): whole = lax.all_gather(tokens, 'tp', axis=1, tiled=True)  24.6 us
    reduce_scatter x1, waiting for transfers between devices, body(): lax.psum_scatter(lax.dot_general(down_mat, hidden_rows, (((0,), (1,)), ((...  18.4 us
    all_to_all x1, waiting for transfers between devices, body(): lax.all_to_all(outcome, ('pool', 'pair'), split_axis=1, concat_axis=1, ti...  15.3 us
    all_to_all x1, starting transfers between devices, body(): lax.all_to_all(outcome, ('pool', 'pair'), split_axis=1, concat_axis=1, ti...  4.61 us
  transfers between devices with their start and end apart: 3, of which 3 were waited for; matrix products, arithmetic and copies ran while one was open for 1% of the time, Pallas kernels for 0%

commit v1 on v0

v1 whole, which is shorter than its diff:
```python
import functools

import jax
import jax.numpy as jnp
from jax import lax
from jax.experimental import pallas as pl
from jax.experimental.pallas import tpu as pltpu
from jax.sharding import PartitionSpec as P

CAP = 16
VMEM = pl.BlockSpec(memory_space=pltpu.VMEM)
SMEM = pl.BlockSpec(memory_space=pltpu.SMEM)
PARAMS = pltpu.CompilerParams(vmem_limit_bytes=24 * 2**20)
BF16, F32 = jnp.bfloat16, jnp.float32


def picks(routes_t, experts):
    hits = [
        jnp.max((routes_t == e).astype(F32), axis=0, keepdims=True) for e in experts
    ]
    hits = jnp.concatenate(hits, axis=0)
    streams = hits.shape[1]
    earlier = lax.broadcasted_iota(jnp.int32, (streams, streams), 0)
    later = lax.broadcasted_iota(jnp.int32, (streams, streams), 1)
    before = (earlier < later).astype(BF16)
    slots = jnp.dot(hits.astype(BF16), before, preferred_element_type=F32)
    return hits, slots


def one_hot(hits, slots, row):
    streams = hits.shape[1]
    slot = lax.broadcasted_iota(jnp.int32, (CAP, streams), 0).astype(F32)
    return jnp.where((slots[row : row + 1] == slot) & (hits[row : row + 1] > 0), 1.0, 0.0)


def select_kernel(n_pool, n_pair, chunks, pos_ref, *refs):
    tokens, routes, outs = refs[:n_pair], refs[n_pair : 2 * n_pair], refs[2 * n_pair :]
    pool, pair = pos_ref[0], pos_ref[1]
    experts = [lax.rem(pool + s, n_pool) * n_pair + pair for s in range(n_pool)]
    for u in range(n_pair):
        hits, slots = picks(routes[u][...], experts)
        sel = jnp.concatenate([one_hot(hits, slots, s) for s in range(n_pool)], axis=0)
        rows = jnp.dot(sel.astype(BF16), tokens[u][...], preferred_element_type=F32).astype(BF16)
        for s in range(n_pool):
            outs[s][u * CAP : (u + 1) * CAP, :] = rows[s * CAP : (s + 1) * CAP]


def mixing_kernel(n_pool, n_pair, pos_ref, routes_ref, weights_ref, hi_ref, lo_ref):
    pool, pair = pos_ref[0], pos_ref[1]
    routes, weights = routes_ref[...], weights_ref[...]
    totals = jnp.sum(weights.astype(F32), axis=0, keepdims=True)
    experts = [
        lax.rem(pool + s, n_pool) * n_pair + lax.rem(pair - u + n_pair, n_pair)
        for u in range(n_pair)
        for s in range(n_pool)
    ]
    hits, slots = picks(routes, experts)
    for i, e in enumerate(experts):
        chosen = jnp.where(routes == e, weights, 0).astype(F32)
        share = jnp.sum(chosen, axis=0, keepdims=True) / totals
        mixing = one_hot(hits, slots, i) * share
        hi = mixing.astype(BF16)
        hi_ref[i * CAP : (i + 1) * CAP, :] = hi
        lo_ref[i * CAP : (i + 1) * CAP, :] = (mixing - hi.astype(F32)).astype(BF16)


def expert_kernel(n_tp, pos_ref, gate_ref, up_ref, down_ref, *refs):
    rows, outs = refs[:n_tp], refs[n_tp:]
    width = rows[0].shape[1]
    tp = pos_ref[2]
    gate = up = None
    for k in range(n_tp):
        at = pl.ds(pl.multiple_of(lax.rem(tp - k + n_tp, n_tp) * width, width), width)
        block = rows[k][...]
        g = jnp.dot(block, gate_ref[at, :], preferred_element_type=F32)
        u = jnp.dot(block, up_ref[at, :], preferred_element_type=F32)
        gate, up = (g, u) if gate is None else (gate + g, up + u)
    hidden = (gate / (1.0 + jnp.exp(-gate)) * up).astype(BF16)
    for k in range(n_tp):
        at = pl.ds(pl.multiple_of(lax.rem(tp + k, n_tp) * width, width), width)
        outs[k][...] = jnp.dot(hidden, down_ref[:, at], preferred_element_type=F32).astype(BF16)


def mix_kernel(n_pool, n_pair, hi_ref, lo_ref, *refs):
    home, away, out = refs[:n_pool], refs[n_pool:-1], refs[-1]
    rows = [r[:CAP, :] for r in home] + [r[...] for r in away]
    rows = jnp.concatenate(rows, axis=0)
    dims = (((0,), (0,)), ((), ()))
    total = lax.dot_general(hi_ref[...], rows, dims, preferred_element_type=F32)
    total += lax.dot_general(lo_ref[...], rows, dims, preferred_element_type=F32)
    out[...] = total.astype(BF16)


def turn(x, axis, shift):
    n = lax.axis_size(axis)
    return lax.ppermute(x, axis, [(i, (i + shift) % n) for i in range(n)])


def body(tokens, routes, gate_weights, w_gate, w_up, w_down):
    n_pool, n_tp, n_pair = (lax.axis_size(a) for a in ("pool", "tp", "pair"))
    streams, width = tokens.shape
    pos = jnp.stack([lax.axis_index(a) for a in ("pool", "pair", "tp")]).astype(jnp.int32)
    gate_mat, up_mat, down_mat = w_gate[0], w_up[0], w_down[0]
    routes_t = routes.T
    weights_t = gate_weights.T
    chunks = [[0], [1], [3], [2]] if n_pool == 4 else [list(range(n_pool))]

    all_tokens = [tokens] + [turn(tokens, "pair", -u) for u in range(1, n_pair)]
    all_routes = [routes_t] + [turn(routes_t, "pair", -u) for u in range(1, n_pair)]
    rows = n_pair * CAP
    leaving = pl.pallas_call(
        functools.partial(select_kernel, n_pool, n_pair, chunks),
        out_shape=[jax.ShapeDtypeStruct((rows, width), BF16)] * n_pool,
        in_specs=[SMEM] + [VMEM] * (2 * n_pair),
        out_specs=[VMEM] * n_pool,
        compiler_params=PARAMS,
        name="select",
    )(pos, *all_tokens, *all_routes)
    slots = n_pool * n_pair * CAP
    hi, lo = pl.pallas_call(
        functools.partial(mixing_kernel, n_pool, n_pair),
        out_shape=[jax.ShapeDtypeStruct((slots, streams), BF16)] * 2,
        in_specs=[SMEM, VMEM, VMEM],
        out_specs=[VMEM] * 2,
        compiler_params=PARAMS,
        name="mixing",
    )(pos, routes_t, weights_t)

    arrived = [turn(leaving[s], "pool", s) if s else leaving[0] for s in range(n_pool)]
    home = [None] * n_pool
    for chunk in chunks:
        block = arrived[chunk[0]] if len(chunk) == 1 else jnp.concatenate([arrived[s] for s in chunk])
        blocks = [block] + [turn(block, "tp", k) for k in range(1, n_tp)]
        parts = pl.pallas_call(
            functools.partial(expert_kernel, n_tp),
            out_shape=[jax.ShapeDtypeStruct((block.shape[0], width), BF16)] * n_tp,
            in_specs=[SMEM] + [VMEM] * (3 + n_tp),
            out_specs=[VMEM] * n_tp,
            compiler_params=PARAMS,
            name="expert",
        )(pos, gate_mat, up_mat, down_mat, *blocks)
        total = parts[0].astype(F32)
        for k in range(1, n_tp):
            total = total + turn(parts[k], "tp", k).astype(F32)
        total = total.astype(BF16)
        for i, s in enumerate(chunk):
            mine = total[i * rows : (i + 1) * rows]
            home[s] = turn(mine, "pool", -s) if s else mine
    away = [turn(home[s][u * CAP : (u + 1) * CAP], "pair", u) for u in range(1, n_pair) for s in range(n_pool)]
    return pl.pallas_call(
        functools.partial(mix_kernel, n_pool, n_pair),
        out_shape=jax.ShapeDtypeStruct((streams, width), BF16),
        in_specs=[VMEM] * (2 + n_pool * n_pair),
        out_specs=VMEM,
        compiler_params=PARAMS,
        name="mix",
    )(hi, lo, *home, *away)


def solution(mesh):
    in_specs = (
        P(("groups", "pool", "pair"), "tp"),
        P(("groups", "pool", "pair"), None),
        P(("groups", "pool", "pair"), None),
        P(("pool", "pair"), None, "tp"),
        P(("pool", "pair"), None, "tp"),
        P(("pool", "pair"), "tp", None),
    )
    out_specs = P(("groups", "pool", "pair"), "tp")
    return jax.shard_map(body, mesh=mesh, in_specs=in_specs, out_specs=out_specs, check_vma=False)
```

time: 118 us -> 61.8 us (0.52)
  waiting for transfers between devices: 59 us -> 14 us
  blocking collectives: 31.3 us -> 0 us
  starting transfers between devices: 4.65 us -> 24.3 us
  Pallas kernels: 0 us -> 14.5 us
  between operations: 13.5 us -> 0.13 us
  local copies, waits for them, and re-layouts: 1.61 us -> 8.33 us
  matrix products: 6.36 us -> 0 us
    all_to_all x1 -> x0, blocking collectives: 31.3 us -> none  [body(): lax.all_to_all(outgoing, ('pool', 'pair'), split_axis=0, concat_axis=0, t...]
    all_gather x1 -> x0, waiting for transfers between devices: 24.6 us -> none  [body(): whole = lax.all_gather(tokens, 'tp', axis=1, tiled=True)]
    ppermute x0 -> x20, starting transfers between devices: none -> 24.3 us  [turn(): return lax.ppermute(x, axis, [(i, (i + shift) % n) for i in range(n)])]
    reduce_scatter x1 -> x0, waiting for transfers between devices: 18.4 us -> none  [body(): lax.psum_scatter(lax.dot_general(down_mat, hidden_rows, (((0,), (1,)), ((...]
    all_to_all x1 -> x0, waiting for transfers between devices: 15.3 us -> none  [body(): lax.all_to_all(outcome, ('pool', 'pair'), split_axis=1, concat_axis=1, ti...]
    pallas_call x0 -> x7, Pallas kernels: none -> 14.5 us  [the longest x4 11.5 us: body(): pl.pallas_call(functools.partial(expert_kernel, n_tp), out_shape=[jax.Sha...]
    ppermute x0 -> x20, waiting for transfers between devices: none -> 14 us  [turn(): return lax.ppermute(x, axis, [(i, (i + shift) % n) for i in range(n)])]
    unnamed x8 -> x14, local copies, waits for them, and re-layouts: 1.46 us -> 8.31 us
  transfers between devices with their start and end apart: 3 -> 20, of which waited for: 3 -> 6; matrix products, arithmetic and copies ran while one was open for 1% -> 0% of each run, Pallas kernels for 0% -> 20%
where the time goes in v1:
time: 61.8 us; the launch traced here: 61.5 us
  starting transfers between devices  24.3 us (39%)
  Pallas kernels  14.5 us (23%)
  waiting for transfers between devices  14 us (23%)
  local copies, waits for them, and re-layouts  8.33 us (13%)
    ppermute x20, starting transfers between devices, turn(): return lax.ppermute(x, axis, [(i, (i + shift) % n) for i in range(n)])  24.3 us
    ppermute x20, waiting for transfers between devices, turn(): return lax.ppermute(x, axis, [(i, (i + shift) % n) for i in range(n)])  14 us
    pallas_call x4, Pallas kernels, body(): pl.pallas_call(functools.partial(expert_kernel, n_tp), out_shape=[jax.Sha...  11.5 us
    unnamed x14, local copies, waits for them, and re-layouts  8.31 us
    pallas_call x1, Pallas kernels, body(): pl.pallas_call(functools.partial(mix_kernel, n_pool, n_pair), out_shape=j...  1.25 us
  transfers between devices with their start and end apart: 20, of which 6 were waited for; matrix products, arithmetic and copies ran while one was open for 0% of the time, Pallas kernels for 20%

profile of v1, /device:TPU:0, one launch (start us, length us, event | category | flops | bytes accessed | tf_op | source)
XLA Modules:
  0.0 61.5 jit_solution(2636768913409809407)
XLA Ops:
  0.6 1.6 %collective-permute-done.1.refs_3_ = s32[8,128]{1,0:T(8,128)S(1)} collective-permute-done((s32[8,128]{1,0:T(8,128)}, s32[8,128]{1,0:T(8,128)S(1)}, u32[]{:S(2)}, u32[]{:S(2)}) %collective-permute-start.1) | collective-permute-done | bytes 4128 | tf_op jit(solution)/shard_map/ppermute | solution.py:96
  2.2 1.0 %copy-done.4 = bf16[128,2048]{1,0:T(8,128)(2,1)S(1)} copy-done((bf16[128,2048]{1,0:T(8,128)(2,1)S(1)}, bf16[128,2048]{1,0:T(8,128)(2,1)}, u32[]{:S(2)}) %copy-start.4) | copy-done | bytes 524312
  3.9 1.1 %select.1 = (bf16[32,2048]{1,0:T(8,128)(2,1)S(1)}, bf16[32,2048]{1,0:T(8,128)(2,1)S(1)}, bf16[32,2048]{1,0:T(8,128)(2,1)S(1)}, bf16[32,2048]{1,0:T(8,128)(2,1)S(1)}) custom-call(s32[3]{0:T(128)S(1)} %pad_add_fusion.pos_ref, bf16[128,2048]{1,0:T(8,128)(2,1)S(1)} %copy-done.4, bf16[128,2048]{1,0:T(8,128)(2,1)S(1)} %collective-permute-done.refs_1_, ...), custom_call_target="tpu_custom_call" | custom-call | tf_op jit(solution)/shard_map/select/pallas_call | solution.py:111
  5.0 3.0 %collective-permute-start.4 = (bf16[32,2048]{1,0:T(8,128)(2,1)S(1)}, bf16[32,2048]{1,0:T(8,128)(2,1)S(1)}, u32[]{:S(2)}, u32[]{:S(2)}) collective-permute-start(bf16[32,2048]{1,0:T(8,128)(2,1)S(1)} %get-tuple-element.24), channel_id=1, source_target_pairs={{0,4},{4,8},{8,12},{12,0},{1,5},{5,9},{9,13},{13,1},{2,6},{6,10},{... | collective-permute-start | bytes 393224 | tf_op jit(solution)/shard_map/ppermute | solution.py:96
  8.0 2.6 %collective-permute-start.8 = (bf16[32,2048]{1,0:T(8,128)(2,1)S(1)}, bf16[32,2048]{1,0:T(8,128)(2,1)S(1)}, u32[]{:S(2)}, u32[]{:S(2)}) collective-permute-start(bf16[32,2048]{1,0:T(8,128)(2,1)S(1)} %get-tuple-element.27), channel_id=1, source_target_pairs={{0,8},{4,12},{8,0},{12,4},{1,9},{5,13},{9,1},{13,5},{2,10},{6,14},... | collective-permute-start | bytes 393224 | tf_op jit(solution)/shard_map/ppermute | solution.py:96
  10.6 1.3 %collective-permute-start.12 = (bf16[32,2048]{1,0:T(8,128)(2,1)S(1)}, bf16[32,2048]{1,0:T(8,128)(2,1)S(1)}, u32[]{:S(2)}, u32[]{:S(2)}) collective-permute-start(bf16[32,2048]{1,0:T(8,128)(2,1)S(1)} %get-tuple-element.30), channel_id=1, source_target_pairs={{0,12},{4,0},{8,4},{12,8},{1,13},{5,1},{9,5},{13,9},{2,14},{6,2},{... | collective-permute-start | bytes 393224 | tf_op jit(solution)/shard_map/ppermute | solution.py:96
  12.0 2.5 %collective-permute-done.4.refs_0_ = bf16[32,2048]{1,0:T(8,128)(2,1)S(1)} collective-permute-done((bf16[32,2048]{1,0:T(8,128)(2,1)S(1)}, bf16[32,2048]{1,0:T(8,128)(2,1)S(1)}, u32[]{:S(2)}, u32[]{:S(2)}) %collective-permute-start.4) | collective-permute-done | bytes 131104 | tf_op jit(solution)/shard_map/ppermute | solution.py:96
  14.4 1.7 %collective-permute-start.5 = (bf16[32,2048]{1,0:T(8,128)(2,1)S(1)}, bf16[32,2048]{1,0:T(8,128)(2,1)S(1)}, u32[]{:S(2)}, u32[]{:S(2)}) collective-permute-start(bf16[32,2048]{1,0:T(8,128)(2,1)S(1)} %collective-permute-done.4.refs_0_), channel_id=1, source_target_pairs={{0,2},{2,0},{1,3},{3,1},{4,6},{6,4},{5,7},{7,5},{8,10},{10,8},{9,1... | collective-permute-start | bytes 393224 | tf_op jit(solution)/shard_map/ppermute | solution.py:96
  16.5 3.1 %collective-permute-done.8.refs_0_ = bf16[32,2048]{1,0:T(8,128)(2,1)S(1)} collective-permute-done((bf16[32,2048]{1,0:T(8,128)(2,1)S(1)}, bf16[32,2048]{1,0:T(8,128)(2,1)S(1)}, u32[]{:S(2)}, u32[]{:S(2)}) %collective-permute-start.8) | collective-permute-done | bytes 131104 | tf_op jit(solution)/shard_map/ppermute | solution.py:96
  19.6 1.5 %collective-permute-start.9 = (bf16[32,2048]{1,0:T(8,128)(2,1)S(1)}, bf16[32,2048]{1,0:T(8,128)(2,1)S(1)}, u32[]{:S(2)}, u32[]{:S(2)}) collective-permute-start(bf16[32,2048]{1,0:T(8,128)(2,1)S(1)} %collective-permute-done.8.refs_0_), channel_id=1, source_target_pairs={{0,2},{2,0},{1,3},{3,1},{4,6},{6,4},{5,7},{7,5},{8,10},{10,8},{9,1... | collective-permute-start | bytes 393224 | tf_op jit(solution)/shard_map/ppermute | solution.py:96
  21.6 2.2 %copy-done = bf16[1,4096,512]{2,1,0:T(8,128)(2,1)S(1)} copy-done((bf16[1,4096,512]{2,1,0:T(8,128)(2,1)S(1)}, bf16[1,4096,512]{2,1,0:T(8,128)(2,1)}, u32[]{:S(2)}) %copy-start) | copy-done | bytes 4194328
  23.8 2.2 %copy-done.2 = bf16[1,4096,512]{2,1,0:T(8,128)(2,1)S(1)} copy-done((bf16[1,4096,512]{2,1,0:T(8,128)(2,1)S(1)}, bf16[1,4096,512]{2,1,0:T(8,128)(2,1)}, u32[]{:S(2)}) %copy-start.2) | copy-done | bytes 4194328
  26.0 2.2 %copy-done.3 = bf16[1,512,4096]{2,1,0:T(8,128)(2,1)S(1)} copy-done((bf16[1,512,4096]{2,1,0:T(8,128)(2,1)S(1)}, bf16[1,512,4096]{2,1,0:T(8,128)(2,1)}, u32[]{:S(2)}) %copy-start.3) | copy-done | bytes 4194328
  28.2 2.9 %expert.5 = (bf16[32,2048]{1,0:T(8,128)(2,1)S(1)}, bf16[32,2048]{1,0:T(8,128)(2,1)S(1)}) custom-call(s32[3]{0:T(128)S(1)} %pad_add_fusion.pos_ref, bf16[4096,512]{1,0:T(8,128)(2,1)S(1)} %bitcast.8, bf16[4096,512]{1,0:T(8,128)(2,1)S(1)} %bitcast.12, bf16[512,4096]{1,0:T(8,128)(2,1)S(1)} %bitcast.16, bf16[32,2048]{1,0:T(8,128)(2,1)S(1)} %collective-permute-done.4.refs_0_, ...), custom_call_target="tpu_custom_call" | custom-call | tf_op jit(solution)/shard_map/expert/pallas_call | solution.py:134
  31.0 1.5 %collective-permute-start.6 = (bf16[32,2048]{1,0:T(8,128)(2,1)S(1)}, bf16[32,2048]{1,0:T(8,128)(2,1)S(1)}, u32[]{:S(2)}, u32[]{:S(2)}) collective-permute-start(bf16[32,2048]{1,0:T(8,128)(2,1)S(1)} %get-tuple-element.26), channel_id=1, source_target_pairs={{0,2},{2,0},{1,3},{3,1},{4,6},{6,4},{5,7},{7,5},{8,10},{10,8},{9,1... | collective-permute-start | bytes 393224 | tf_op jit(solution)/shard_map/ppermute | solution.py:96
  32.6 2.9 %expert.4 = (bf16[32,2048]{1,0:T(8,128)(2,1)S(1)}, bf16[32,2048]{1,0:T(8,128)(2,1)S(1)}) custom-call(s32[3]{0:T(128)S(1)} %pad_add_fusion.pos_ref, bf16[4096,512]{1,0:T(8,128)(2,1)S(1)} %bitcast.9, bf16[4096,512]{1,0:T(8,128)(2,1)S(1)} %bitcast.13, bf16[512,4096]{1,0:T(8,128)(2,1)S(1)} %bitcast.17, bf16[32,2048]{1,0:T(8,128)(2,1)S(1)} %get-tuple-element.21.refs_0_, ...), custom_call_target="tpu_custom_call" | custom-call | tf_op jit(solution)/shard_map/expert/pallas_call | solution.py:134
  36.0 2.9 %expert.6 = (bf16[32,2048]{1,0:T(8,128)(2,1)S(1)}, bf16[32,2048]{1,0:T(8,128)(2,1)S(1)}) custom-call(s32[3]{0:T(128)S(1)} %pad_add_fusion.pos_ref, bf16[4096,512]{1,0:T(8,128)(2,1)S(1)} %bitcast.10, bf16[4096,512]{1,0:T(8,128)(2,1)S(1)} %bitcast.14, bf16[512,4096]{1,0:T(8,128)(2,1)S(1)} %bitcast.18, bf16[32,2048]{1,0:T(8,128)(2,1)S(1)} %collective-permute-done.8.refs_0_, ...), custom_call_target="tpu_custom_call" | custom-call | tf_op jit(solution)/shard_map/expert/pallas_call | solution.py:134
  38.9 1.6 %collective-permute-start.10 = (bf16[32,2048]{1,0:T(8,128)(2,1)S(1)}, bf16[32,2048]{1,0:T(8,128)(2,1)S(1)}, u32[]{:S(2)}, u32[]{:S(2)}) collective-permute-start(bf16[32,2048]{1,0:T(8,128)(2,1)S(1)} %get-tuple-element.29), channel_id=1, source_target_pairs={{0,2},{2,0},{1,3},{3,1},{4,6},{6,4},{5,7},{7,5},{8,10},{10,8},{9,1... | collective-permute-start | bytes 393224 | tf_op jit(solution)/shard_map/ppermute | solution.py:96
  40.5 2.9 %expert.7 = (bf16[32,2048]{1,0:T(8,128)(2,1)S(1)}, bf16[32,2048]{1,0:T(8,128)(2,1)S(1)}) custom-call(s32[3]{0:T(128)S(1)} %pad_add_fusion.pos_ref, bf16[4096,512]{1,0:T(8,128)(2,1)S(1)} %bitcast.11, bf16[4096,512]{1,0:T(8,128)(2,1)S(1)} %bitcast.15, bf16[512,4096]{1,0:T(8,128)(2,1)S(1)} %bitcast.19, bf16[32,2048]{1,0:T(8,128)(2,1)S(1)} %collective-permute-done.12.refs_0_, ...), custom_call_target="tpu_custom_call" | custom-call | tf_op jit(solution)/shard_map/expert/pallas_call | solution.py:134
  44.0 4.4 %collective-permute-start.7 = (bf16[32,2048]{1,0:T(8,128)(2,1)S(1)}, bf16[32,2048]{1,0:T(8,128)(2,1)S(1)}, u32[]{:S(2)}, u32[]{:S(2)}) collective-permute-start(bf16[32,2048]{1,0:T(8,128)(2,1)S(1)} %add_convert_fusion.2), channel_id=1, source_target_pairs={{0,12},{4,0},{8,4},{12,8},{1,13},{5,1},{9,5},{13,9},{2,14},{6,2},{... | collective-permute-start | bytes 393224 | tf_op jit(solution)/shard_map/ppermute | solution.py:96
  48.4 1.4 %collective-permute-start.11 = (bf16[32,2048]{1,0:T(8,128)(2,1)S(1)}, bf16[32,2048]{1,0:T(8,128)(2,1)S(1)}, u32[]{:S(2)}, u32[]{:S(2)}) collective-permute-start(bf16[32,2048]{1,0:T(8,128)(2,1)S(1)} %add_convert_fusion.1), channel_id=1, source_target_pairs={{0,8},{4,12},{8,0},{12,4},{1,9},{5,13},{9,1},{13,5},{2,10},{6,14},... | collective-permute-start | bytes 393224 | tf_op jit(solution)/shard_map/ppermute | solution.py:96
  49.9 2.1 %collective-permute-start.15 = (bf16[32,2048]{1,0:T(8,128)(2,1)S(1)}, bf16[32,2048]{1,0:T(8,128)(2,1)S(1)}, u32[]{:S(2)}, u32[]{:S(2)}) collective-permute-start(bf16[32,2048]{1,0:T(8,128)(2,1)S(1)} %add_convert_fusion), channel_id=1, source_target_pairs={{0,4},{4,8},{8,12},{12,0},{1,5},{5,9},{9,13},{13,1},{2,6},{6,10},{... | collective-permute-start | bytes 393224 | tf_op jit(solution)/shard_map/ppermute | solution.py:96
  53.1 5.6 %collective-permute-done.11.refs_2_ = bf16[32,2048]{1,0:T(8,128)(2,1)S(1)} collective-permute-done((bf16[32,2048]{1,0:T(8,128)(2,1)S(1)}, bf16[32,2048]{1,0:T(8,128)(2,1)S(1)}, u32[]{:S(2)}, u32[]{:S(2)}) %collective-permute-start.11) | collective-permute-done | bytes 131104 | tf_op jit(solution)/shard_map/ppermute | solution.py:96
  60.2 1.3 %mix.1 = bf16[128,2048]{1,0:T(8,128)(2,1)} custom-call(bf16[128,128]{1,0:T(8,128)(2,1)S(1)} %get-tuple-element.19.hi_ref, bf16[128,128]{1,0:T(8,128)(2,1)S(1)} %get-tuple-element.20.lo_ref, bf16[32,2048]{1,0:T(8,128)(2,1)S(1)} %add_convert_fusion.3.refs_0_, bf16[32,2048]{1,0:T(8,128)(2,1)S(1)} %collective-permute-done.7.refs_1_, ...), custom_call_target="tpu_custom_call" | custom-call | tf_op jit(solution)/shard_map/mix/pallas_call | solution.py:150
  (46 shorter events, 6.0 us)
Async XLA Ops:
  0.0 2.2 %collective-permute-start = (bf16[128,2048]{1,0:T(8,128)(2,1)}, bf16[128,2048]{1,0:T(8,128)(2,1)S(1)}, u32[]{:S(2)}, u32[]{:S(2)}) collective-permute-start(bf16[128,2048]{1,0:T(8,128)(2,1)} %refs_0_.1), channel_id=1, source_target_pairs={{0,1},{1,0},{2,3},{3,2},{4,5},{5,4},{6,7},{7,6},{8,9},{9,8},{10,11... | collective-permute-start | bytes 1572872 | tf_op jit(solution)/shard_map/ppermute | solution.py:96
  0.5 1.8 %collective-permute-start.1 = (s32[8,128]{1,0:T(8,128)}, s32[8,128]{1,0:T(8,128)S(1)}, u32[]{:S(2)}, u32[]{:S(2)}) collective-permute-start(s32[8,128]{1,0:T(8,128)} %bitcast.20), channel_id=1, source_target_pairs={{0,1},{1,0},{2,3},{3,2},{4,5},{5,4},{6,7},{7,6},{8,9},{9,8},{10,11... | collective-permute-start | bytes 12296 | tf_op jit(solution)/shard_map/ppermute | solution.py:96
  5.0 9.4 %collective-permute-start.4 = (bf16[32,2048]{1,0:T(8,128)(2,1)S(1)}, bf16[32,2048]{1,0:T(8,128)(2,1)S(1)}, u32[]{:S(2)}, u32[]{:S(2)}) collective-permute-start(bf16[32,2048]{1,0:T(8,128)(2,1)S(1)} %get-tuple-element.24), channel_id=1, source_target_pairs={{0,4},{4,8},{8,12},{12,0},{1,5},{5,9},{9,13},{13,1},{2,6},{6,10},{... | collective-permute-start | bytes 393224 | tf_op jit(solution)/shard_map/ppermute | solution.py:96
  8.0 11.5 %collective-permute-start.8 = (bf16[32,2048]{1,0:T(8,128)(2,1)S(1)}, bf16[32,2048]{1,0:T(8,128)(2,1)S(1)}, u32[]{:S(2)}, u32[]{:S(2)}) collective-permute-start(bf16[32,2048]{1,0:T(8,128)(2,1)S(1)} %get-tuple-element.27), channel_id=1, source_target_pairs={{0,8},{4,12},{8,0},{12,4},{1,9},{5,13},{9,1},{13,5},{2,10},{6,14},... | collective-permute-start | bytes 393224 | tf_op jit(solution)/shard_map/ppermute | solution.py:96
  10.6 10.4 %collective-permute-start.12 = (bf16[32,2048]{1,0:T(8,128)(2,1)S(1)}, bf16[32,2048]{1,0:T(8,128)(2,1)S(1)}, u32[]{:S(2)}, u32[]{:S(2)}) collective-permute-start(bf16[32,2048]{1,0:T(8,128)(2,1)S(1)} %get-tuple-element.30), channel_id=1, source_target_pairs={{0,12},{4,0},{8,4},{12,8},{1,13},{5,1},{9,5},{13,9},{2,14},{6,2},{... | collective-permute-start | bytes 393224 | tf_op jit(solution)/shard_map/ppermute | solution.py:96
  14.4 7.2 %collective-permute-start.5 = (bf16[32,2048]{1,0:T(8,128)(2,1)S(1)}, bf16[32,2048]{1,0:T(8,128)(2,1)S(1)}, u32[]{:S(2)}, u32[]{:S(2)}) collective-permute-start(bf16[32,2048]{1,0:T(8,128)(2,1)S(1)} %collective-permute-done.4.refs_0_), channel_id=1, source_target_pairs={{0,2},{2,0},{1,3},{3,1},{4,6},{6,4},{5,7},{7,5},{8,10},{10,8},{9,1... | collective-permute-start | bytes 393224 | tf_op jit(solution)/shard_map/ppermute | solution.py:96
  16.2 16.4 %collective-permute-start.2 = (bf16[32,2048]{1,0:T(8,128)(2,1)S(1)}, bf16[32,2048]{1,0:T(8,128)(2,1)S(1)}, u32[]{:S(2)}, u32[]{:S(2)}) collective-permute-start(bf16[32,2048]{1,0:T(8,128)(2,1)S(1)} %get-tuple-element.21.refs_0_), channel_id=1, source_target_pairs={{0,2},{2,0},{1,3},{3,1},{4,6},{6,4},{5,7},{7,5},{8,10},{10,8},{9,1... | collective-permute-start | bytes 393224 | tf_op jit(solution)/shard_map/ppermute | solution.py:96
  19.6 16.5 %collective-permute-start.9 = (bf16[32,2048]{1,0:T(8,128)(2,1)S(1)}, bf16[32,2048]{1,0:T(8,128)(2,1)S(1)}, u32[]{:S(2)}, u32[]{:S(2)}) collective-permute-start(bf16[32,2048]{1,0:T(8,128)(2,1)S(1)} %collective-permute-done.8.refs_0_), channel_id=1, source_target_pairs={{0,2},{2,0},{1,3},{3,1},{4,6},{6,4},{5,7},{7,5},{8,10},{10,8},{9,1... | collective-permute-start | bytes 393224 | tf_op jit(solution)/shard_map/ppermute | solution.py:96
  21.1 19.4 %collective-permute-start.13 = (bf16[32,2048]{1,0:T(8,128)(2,1)S(1)}, bf16[32,2048]{1,0:T(8,128)(2,1)S(1)}, u32[]{:S(2)}, u32[]{:S(2)}) collective-permute-start(bf16[32,2048]{1,0:T(8,128)(2,1)S(1)} %collective-permute-done.12.refs_0_), channel_id=1, source_target_pairs={{0,2},{2,0},{1,3},{3,1},{4,6},{6,4},{5,7},{7,5},{8,10},{10,8},{9,1... | collective-permute-start | bytes 393224 | tf_op jit(solution)/shard_map/ppermute | solution.py:96
  21.6 2.2 %copy-start = (bf16[1,4096,512]{2,1,0:T(8,128)(2,1)S(1)}, bf16[1,4096,512]{2,1,0:T(8,128)(2,1)}, u32[]{:S(2)}) copy-start(bf16[1,4096,512]{2,1,0:T(8,128)(2,1)} %param.9) | copy-start | bytes 12582916
  23.8 2.2 %copy-start.2 = (bf16[1,4096,512]{2,1,0:T(8,128)(2,1)S(1)}, bf16[1,4096,512]{2,1,0:T(8,128)(2,1)}, u32[]{:S(2)}) copy-start(bf16[1,4096,512]{2,1,0:T(8,128)(2,1)} %param.10) | copy-start | bytes 12582916
  28.2 4.4 %copy-start.1 = (bf16[1,4096,512]{2,1,0:T(8,128)(2,1)S(1)}, bf16[1,4096,512]{2,1,0:T(8,128)(2,1)}, u32[]{:S(2)}) copy-start(bf16[1,4096,512]{2,1,0:T(8,128)(2,1)} %param.9) | copy-start | bytes 12582916
  31.0 12.9 %collective-permute-start.6 = (bf16[32,2048]{1,0:T(8,128)(2,1)S(1)}, bf16[32,2048]{1,0:T(8,128)(2,1)S(1)}, u32[]{:S(2)}, u32[]{:S(2)}) collective-permute-start(bf16[32,2048]{1,0:T(8,128)(2,1)S(1)} %get-tuple-element.26), channel_id=1, source_target_pairs={{0,2},{2,0},{1,3},{3,1},{4,6},{6,4},{5,7},{7,5},{8,10},{10,8},{9,1... | collective-permute-start | bytes 393224 | tf_op jit(solution)/shard_map/ppermute | solution.py:96
  35.5 16.5 %collective-permute-start.3 = (bf16[32,2048]{1,0:T(8,128)(2,1)S(1)}, bf16[32,2048]{1,0:T(8,128)(2,1)S(1)}, u32[]{:S(2)}, u32[]{:S(2)}) collective-permute-start(bf16[32,2048]{1,0:T(8,128)(2,1)S(1)} %get-tuple-element.23), channel_id=1, source_target_pairs={{0,2},{2,0},{1,3},{3,1},{4,6},{6,4},{5,7},{7,5},{8,10},{10,8},{9,1... | collective-permute-start | bytes 393224 | tf_op jit(solution)/shard_map/ppermute | solution.py:96
  38.9 20.4 %copy-start.6 = (s32[128,8]{0,1:T(8,128)S(1)}, s32[128,8]{0,1:T(8,128)}, u32[]{:S(2)}) copy-start(s32[128,8]{0,1:T(8,128)} %param.8) | copy-start | bytes 12292
  38.9 9.5 %collective-permute-start.10 = (bf16[32,2048]{1,0:T(8,128)(2,1)S(1)}, bf16[32,2048]{1,0:T(8,128)(2,1)S(1)}, u32[]{:S(2)}, u32[]{:S(2)}) collective-permute-start(bf16[32,2048]{1,0:T(8,128)(2,1)S(1)} %get-tuple-element.29), channel_id=1, source_target_pairs={{0,2},{2,0},{1,3},{3,1},{4,6},{6,4},{5,7},{7,5},{8,10},{10,8},{9,1... | collective-permute-start | bytes 393224 | tf_op jit(solution)/shard_map/ppermute | solution.py:96
  43.4 6.5 %collective-permute-start.14 = (bf16[32,2048]{1,0:T(8,128)(2,1)S(1)}, bf16[32,2048]{1,0:T(8,128)(2,1)S(1)}, u32[]{:S(2)}, u32[]{:S(2)}) collective-permute-start(bf16[32,2048]{1,0:T(8,128)(2,1)S(1)} %get-tuple-element.32), channel_id=1, source_target_pairs={{0,2},{2,0},{1,3},{3,1},{4,6},{6,4},{5,7},{7,5},{8,10},{10,8},{9,1... | collective-permute-start | bytes 393224 | tf_op jit(solution)/shard_map/ppermute | solution.py:96
  44.0 9.1 %collective-permute-start.7 = (bf16[32,2048]{1,0:T(8,128)(2,1)S(1)}, bf16[32,2048]{1,0:T(8,128)(2,1)S(1)}, u32[]{:S(2)}, u32[]{:S(2)}) collective-permute-start(bf16[32,2048]{1,0:T(8,128)(2,1)S(1)} %add_convert_fusion.2), channel_id=1, source_target_pairs={{0,12},{4,0},{8,4},{12,8},{1,13},{5,1},{9,5},{13,9},{2,14},{6,2},{... | collective-permute-start | bytes 393224 | tf_op jit(solution)/shard_map/ppermute | solution.py:96
  48.4 10.3 %collective-permute-start.11 = (bf16[32,2048]{1,0:T(8,128)(2,1)S(1)}, bf16[32,2048]{1,0:T(8,128)(2,1)S(1)}, u32[]{:S(2)}, u32[]{:S(2)}) collective-permute-start(bf16[32,2048]{1,0:T(8,128)(2,1)S(1)} %add_convert_fusion.1), channel_id=1, source_target_pairs={{0,8},{4,12},{8,0},{12,4},{1,9},{5,13},{9,1},{13,5},{2,10},{6,14},... | collective-permute-start | bytes 393224 | tf_op jit(solution)/shard_map/ppermute | solution.py:96
  49.9 8.9 %collective-permute-start.15 = (bf16[32,2048]{1,0:T(8,128)(2,1)S(1)}, bf16[32,2048]{1,0:T(8,128)(2,1)S(1)}, u32[]{:S(2)}, u32[]{:S(2)}) collective-permute-start(bf16[32,2048]{1,0:T(8,128)(2,1)S(1)} %add_convert_fusion), channel_id=1, source_target_pairs={{0,4},{4,8},{8,12},{12,0},{1,5},{5,9},{9,13},{13,1},{2,6},{6,10},{... | collective-permute-start | bytes 393224 | tf_op jit(solution)/shard_map/ppermute | solution.py:96
  52.1 8.0 %collective-permute-start.16 = (bf16[16,2048]{1,0:T(8,128)(2,1)S(1)}, bf16[16,2048]{1,0:T(8,128)(2,1)S(1)}, u32[]{:S(2)}, u32[]{:S(2)}) collective-permute-start(bf16[16,2048]{1,0:T(8,128)(2,1)S(1)} %slice.16), channel_id=1, source_target_pairs={{0,1},{1,0},{2,3},{3,2},{4,5},{5,4},{6,7},{7,6},{8,9},{9,8},{10,11... | collective-permute-start | bytes 196616 | tf_op jit(solution)/shard_map/ppermute | solution.py:96
  53.1 6.9 %collective-permute-start.17 = (bf16[16,2048]{1,0:T(8,128)(2,1)S(1)}, bf16[16,2048]{1,0:T(8,128)(2,1)S(1)}, u32[]{:S(2)}, u32[]{:S(2)}) collective-permute-start(bf16[16,2048]{1,0:T(8,128)(2,1)S(1)} %slice.17), channel_id=1, source_target_pairs={{0,1},{1,0},{2,3},{3,2},{4,5},{5,4},{6,7},{7,6},{8,9},{9,8},{10,11... | collective-permute-start | bytes 196616 | tf_op jit(solution)/shard_map/ppermute | solution.py:96
  58.7 1.3 %collective-permute-start.18 = (bf16[16,2048]{1,0:T(8,128)(2,1)S(1)}, bf16[16,2048]{1,0:T(8,128)(2,1)S(1)}, u32[]{:S(2)}, u32[]{:S(2)}) collective-permute-start(bf16[16,2048]{1,0:T(8,128)(2,1)S(1)} %slice.18), channel_id=1, source_target_pairs={{0,1},{1,0},{2,3},{3,2},{4,5},{5,4},{6,7},{7,6},{8,9},{9,8},{10,11... | collective-permute-start | bytes 196616 | tf_op jit(solution)/shard_map/ppermute | solution.py:96
  58.8 1.5 %collective-permute-start.19 = (bf16[16,2048]{1,0:T(8,128)(2,1)S(1)}, bf16[16,2048]{1,0:T(8,128)(2,1)S(1)}, u32[]{:S(2)}, u32[]{:S(2)}) collective-permute-start(bf16[16,2048]{1,0:T(8,128)(2,1)S(1)} %slice.19), channel_id=1, source_target_pairs={{0,1},{1,0},{2,3},{3,2},{4,5},{5,4},{6,7},{7,6},{8,9},{9,8},{10,11... | collective-permute-start | bytes 196616 | tf_op jit(solution)/shard_map/ppermute | solution.py:96
  (3 other events, 3.9 us)

commit v2 on v0

v2 whole, which is shorter than its diff:
```python
import functools

import jax
import jax.numpy as jnp
from jax import lax
from jax.experimental import pallas as pl
from jax.experimental.pallas import tpu as pltpu
from jax.sharding import PartitionSpec as P

CAP = 16
VMEM = pl.BlockSpec(memory_space=pltpu.VMEM)
SMEM = pl.BlockSpec(memory_space=pltpu.SMEM)
HBM = pl.BlockSpec(memory_space=pltpu.HBM)
BF16, F32 = jnp.bfloat16, jnp.float32


def call(kernel, name, outs, in_specs, args, nbytes, flops=0, scratch=(), alias=None, vmem=24):
    return pl.pallas_call(
        kernel,
        out_shape=outs,
        in_specs=in_specs,
        out_specs=[VMEM] * len(outs),
        scratch_shapes=scratch,
        input_output_aliases=alias or {},
        compiler_params=pltpu.CompilerParams(vmem_limit_bytes=vmem * 2**20),
        cost_estimate=pl.CostEstimate(flops=flops, bytes_accessed=nbytes, transcendentals=0),
        name=name,
    )(*args)


def picks(routes_t, experts):
    hits = [
        jnp.max((routes_t == e).astype(F32), axis=0, keepdims=True) for e in experts
    ]
    hits = jnp.concatenate(hits, axis=0)
    streams = hits.shape[1]
    earlier = lax.broadcasted_iota(jnp.int32, (streams, streams), 0)
    later = lax.broadcasted_iota(jnp.int32, (streams, streams), 1)
    before = (earlier < later).astype(BF16)
    slots = jnp.dot(hits.astype(BF16), before, preferred_element_type=F32)
    return hits, slots


def one_hot(hits, slots, row):
    streams = hits.shape[1]
    slot = lax.broadcasted_iota(jnp.int32, (CAP, streams), 0).astype(F32)
    return jnp.where((slots[row : row + 1] == slot) & (hits[row : row + 1] > 0), 1.0, 0.0)


def select(pos_ref, routes, tokens, outs, n_pool, n_pair, u):
    pool, pair = pos_ref[0], pos_ref[1]
    experts = [lax.rem(pool + s, n_pool) * n_pair + pair for s in range(n_pool)]
    hits, slots = picks(routes[...], experts)
    sel = jnp.concatenate([one_hot(hits, slots, s) for s in range(n_pool)], axis=0)
    rows = jnp.dot(sel.astype(BF16), tokens[...], preferred_element_type=F32).astype(BF16)
    for s in range(n_pool):
        outs[s][u * CAP : (u + 1) * CAP, :] = rows[s * CAP : (s + 1) * CAP]


def select_own_kernel(n_pool, n_pair, pos_ref, routes, tokens, *refs):
    outs, held, sem = refs[:n_pool], refs[n_pool], refs[n_pool + 1]
    copy = pltpu.make_async_copy(tokens, held, sem)
    copy.start()
    copy.wait()
    select(pos_ref, routes, held, outs, n_pool, n_pair, 0)


def select_other_kernel(n_pool, n_pair, pos_ref, *refs):
    others = n_pair - 1
    routes, tokens = refs[:others], refs[others : 2 * others]
    outs = refs[2 * others + n_pool :]
    held = refs[2 * others : 2 * others + n_pool]
    for s in range(n_pool):
        outs[s][:CAP, :] = held[s][:CAP, :]
    for u in range(1, n_pair):
        select(pos_ref, routes[u - 1], tokens[u - 1], outs, n_pool, n_pair, u)


def mixing_kernel(n_pool, n_pair, pos_ref, after_ref, routes_ref, weights_ref, out_ref):
    pool, pair = pos_ref[0], pos_ref[1]
    routes, weights = routes_ref[...], weights_ref[...]
    totals = jnp.sum(weights.astype(F32), axis=0, keepdims=True)
    experts = [
        lax.rem(pool + s, n_pool) * n_pair + lax.rem(pair - u + n_pair, n_pair)
        for u in range(n_pair)
        for s in range(n_pool)
    ]
    hits, slots = picks(routes, experts)
    mixing = []
    for i, e in enumerate(experts):
        chosen = jnp.where(routes == e, weights, 0).astype(F32)
        share = jnp.sum(chosen, axis=0, keepdims=True) / totals
        mixing.append(one_hot(hits, slots, i) * share)
    mixing = jnp.concatenate(mixing, axis=0).T
    n = mixing.shape[1]
    hi = mixing.astype(BF16)
    out_ref[:, :n] = hi
    out_ref[:, n:] = (mixing - hi.astype(F32)).astype(BF16)


def load_kernel(after_ref, gate, up, gate_out, up_out, sems):
    pairs = ((gate, gate_out), (up, up_out))
    copies = [pltpu.make_async_copy(a, b, sems.at[i]) for i, (a, b) in enumerate(pairs)]
    for c in copies:
        c.start()
    for c in copies:
        c.wait()


def stacked(refs):
    return jnp.concatenate([r[...] for r in refs], axis=0)


def near_kernel(n_tp, pos_ref, gate_ref, up_ref, *refs):
    rows, gate_out, up_out = refs[:-2], refs[-2], refs[-1]
    width = rows[0].shape[1]
    at = pl.ds(pl.multiple_of(pos_ref[2] * width, width), width)
    block = stacked(rows)
    gate_out[...] = jnp.dot(block, gate_ref[at, :], preferred_element_type=F32)
    up_out[...] = jnp.dot(block, up_ref[at, :], preferred_element_type=F32)


def far_kernel(n_tp, n_chunks, pos_ref, gate_ref, up_ref, down_ref, gate_in, up_in, *refs):
    far = n_tp - 1
    rows = [refs[k * n_chunks : (k + 1) * n_chunks] for k in range(far)]
    hidden_ref, outs = refs[far * n_chunks], refs[far * n_chunks + 1 :]
    width = down_ref.shape[1] // n_tp
    tp = pos_ref[2]
    gate, up = gate_in[...], up_in[...]
    for k in range(1, n_tp):
        at = pl.ds(pl.multiple_of(lax.rem(tp - k + n_tp, n_tp) * width, width), width)
        block = stacked(rows[k - 1])
        gate += jnp.dot(block, gate_ref[at, :], preferred_element_type=F32)
        up += jnp.dot(block, up_ref[at, :], preferred_element_type=F32)
    hidden = (gate / (1.0 + jnp.exp(-gate)) * up).astype(BF16)
    hidden_ref[...] = hidden
    for k in range(1, n_tp):
        at = pl.ds(pl.multiple_of(lax.rem(tp + k, n_tp) * width, width), width)
        part = jnp.dot(hidden, down_ref[:, at], preferred_element_type=F32).astype(BF16)
        put(outs[(k - 1) * n_chunks : k * n_chunks], part)


def put(outs, part):
    at = 0
    for o in outs:
        o[...] = part[at : at + o.shape[0]]
        at += o.shape[0]


def keep_kernel(n_tp, pos_ref, down_ref, hidden_ref, *outs):
    width = outs[0].shape[1]
    at = pl.ds(pl.multiple_of(pos_ref[2] * width, width), width)
    put(outs, jnp.dot(hidden_ref[...], down_ref[:, at], preferred_element_type=F32).astype(BF16))


def mix_kernel(n_pool, n_pair, layout, mixing_ref, *refs):
    parts, out = refs[:-1], refs[-1]
    at, rows = 0, []
    for n, first in layout:
        total = parts[at][first : first + CAP, :].astype(F32)
        for r in parts[at + 1 : at + n]:
            total += r[first : first + CAP, :].astype(F32)
        rows.append(total.astype(BF16))
        at += n
    rows = jnp.concatenate(rows + rows, axis=0)
    out[...] = jnp.dot(mixing_ref[...], rows, preferred_element_type=F32).astype(BF16)


def turn(x, axis, shift):
    n = lax.axis_size(axis)
    return lax.ppermute(x, axis, [(i, (i + shift) % n) for i in range(n)])


def cross(x, shift, k):
    n, m = lax.axis_size("pool"), lax.axis_size("tp")
    pairs = [(i * m + j, (i + shift) % n * m + (j + k) % m) for i in range(n) for j in range(m)]
    return lax.ppermute(x, ("pool", "tp"), pairs)


def add(parts):
    total = parts[0].astype(F32)
    for p in parts[1:]:
        total += p.astype(F32)
    return total.astype(BF16)


def body(tokens, routes, gate_weights, w_gate, w_up, w_down):
    n_pool, n_tp, n_pair = (lax.axis_size(a) for a in ("pool", "tp", "pair"))
    streams, width = tokens.shape
    hidden_units = w_gate.shape[2]
    pos = jnp.stack([lax.axis_index(a) for a in ("pool", "pair", "tp")]).astype(jnp.int32)
    routes_t, weights_t = routes.T, gate_weights.T
    rows = n_pair * CAP
    small = n_pool <= 4 and n_tp == 2
    direct = [1] if small else []

    def shape(r, c, t=BF16):
        return jax.ShapeDtypeStruct((r, c), t)

    far_tokens = [turn(tokens, "pair", -u) for u in range(1, n_pair)]
    far_routes = [turn(routes_t, "pair", -u) for u in range(1, n_pair)]
    leaving = call(
        functools.partial(select_own_kernel, n_pool, n_pair),
        "select_own",
        [shape(rows, width)] * n_pool,
        [SMEM, VMEM, HBM],
        (pos, routes_t, tokens),
        2 * 2 * streams * width,
        scratch=[pltpu.VMEM((streams, width), BF16), pltpu.SemaphoreType.DMA],
    )
    leaving = call(
        functools.partial(select_other_kernel, n_pool, n_pair),
        "select_other",
        [shape(rows, width)] * n_pool,
        [SMEM] + [VMEM] * (2 * (n_pair - 1) + n_pool),
        (pos, *far_routes, *far_tokens, *leaving),
        2 * 2 * streams * width,
        alias={1 + 2 * (n_pair - 1) + s: s for s in range(n_pool)},
    )
    gate_mat, up_mat = call(
        load_kernel,
        "load",
        [jax.ShapeDtypeStruct(w.shape[1:], BF16) for w in (w_gate, w_up)],
        [VMEM] + [HBM] * 2,
        (leaving[0], w_gate[0], w_up[0]),
        2 * 2 * (w_gate.size + w_up.size),
        scratch=[pltpu.SemaphoreType.DMA((2,))],
        vmem=44,
    )
    down_mat = w_down[0]
    slots = n_pool * rows
    (mixing,) = call(
        functools.partial(mixing_kernel, n_pool, n_pair),
        "mixing",
        [shape(streams, 2 * slots)],
        [SMEM, VMEM, VMEM, VMEM],
        (pos, leaving[0], routes_t, weights_t),
        4 * 10 * streams * slots,
    )

    near = [turn(leaving[s], "pool", s) if s else leaving[0] for s in range(n_pool)]
    first = 1 if n_pool > 1 else 0
    near[first], gate_mat, up_mat, mixing = lax.optimization_barrier((near[first], gate_mat, up_mat, mixing))
    far = [[turn(b, "tp", k) for b in near] for k in range(1, n_tp)]
    gate, up = call(
        functools.partial(near_kernel, n_tp),
        "near",
        [shape(slots, hidden_units, F32)] * 2,
        [SMEM] + [VMEM] * (2 + n_pool),
        (pos, gate_mat, up_mat, *near),
        4 * width * hidden_units,
        4 * slots * width * hidden_units,
    )
    hidden, *sent = call(
        functools.partial(far_kernel, n_tp, n_pool),
        "far",
        [shape(slots, hidden_units)] + [shape(rows, width)] * (n_pool * (n_tp - 1)),
        [SMEM] + [VMEM] * (5 + n_pool * (n_tp - 1)),
        (pos, gate_mat, up_mat, down_mat, gate, up, *sum(far, [])),
        8 * width * hidden_units,
        6 * slots * width * hidden_units,
    )
    sent = [sent[k * n_pool : (k + 1) * n_pool] for k in range(n_tp - 1)]
    kept = call(
        functools.partial(keep_kernel, n_tp),
        "keep",
        [shape(rows, width)] * n_pool,
        [SMEM] + [VMEM] * 2,
        (pos, down_mat, hidden),
        2 * width * hidden_units,
        2 * slots * width * hidden_units,
    )

    home = []
    for s in range(n_pool):
        if s in direct:
            home.append([cross(kept[s], -s, 0)] + [cross(sent[k - 1][s], -s, k) for k in range(1, n_tp)])
        else:
            total = add([kept[s]] + [turn(sent[k - 1][s], "tp", k) for k in range(1, n_tp)])
            home.append([turn(total, "pool", -s) if s else total])
    layout, parts = [], []
    for s in range(n_pool):
        layout.append((len(home[s]), 0))
        parts += home[s]
    for u in range(1, n_pair):
        for s in range(n_pool):
            part = add([h[u * CAP : (u + 1) * CAP] for h in home[s]])
            layout.append((1, 0))
            parts.append(turn(part, "pair", u))
    (out,) = call(
        functools.partial(mix_kernel, n_pool, n_pair, layout),
        "mix",
        [shape(streams, width)],
        [VMEM] * (1 + len(parts)),
        (mixing, *parts),
        2 * 3 * streams * width,
    )
    return out


def solution(mesh):
    in_specs = (
        P(("groups", "pool", "pair"), "tp"),
        P(("groups", "pool", "pair"), None),
        P(("groups", "pool", "pair"), None),
        P(("pool", "pair"), None, "tp"),
        P(("pool", "pair"), None, "tp"),
        P(("pool", "pair"), "tp", None),
    )
    out_specs = P(("groups", "pool", "pair"), "tp")
    return jax.shard_map(body, mesh=mesh, in_specs=in_specs, out_specs=out_specs, check_vma=False)
```

time: 118 us -> 56.1 us (0.48)
  waiting for transfers between devices: 59 us -> 18.8 us
  blocking collectives: 31.3 us -> 0 us
  starting transfers between devices: 4.65 us -> 23.1 us
  between operations: 13.5 us -> 0.18 us
  Pallas kernels: 0 us -> 11.1 us
  matrix products: 6.36 us -> 0 us
    all_to_all x1 -> x0, blocking collectives: 31.3 us -> none  [body(): lax.all_to_all(outgoing, ('pool', 'pair'), split_axis=0, concat_axis=0, t...]
    all_gather x1 -> x0, waiting for transfers between devices: 24.6 us -> none  [body(): whole = lax.all_gather(tokens, 'tp', axis=1, tiled=True)]
    ppermute x0 -> x20, starting transfers between devices: none -> 23.1 us  [the longest x18 19.4 us: turn(): return lax.ppermute(x, axis, [(i, (i + shift) % n) for i in range(n)])]
    ppermute x0 -> x20, waiting for transfers between devices: none -> 18.8 us  [the longest x18 18.8 us: turn(): return lax.ppermute(x, axis, [(i, (i + shift) % n) for i in range(n)])]
    reduce_scatter x1 -> x0, waiting for transfers between devices: 18.4 us -> none  [body(): lax.psum_scatter(lax.dot_general(down_mat, hidden_rows, (((0,), (1,)), ((...]
    all_to_all x1 -> x0, waiting for transfers between devices: 15.3 us -> none  [body(): lax.all_to_all(outcome, ('pool', 'pair'), split_axis=1, concat_axis=1, ti...]
    pallas_call x0 -> x8, Pallas kernels: none -> 11.1 us  [call(): pl.pallas_call(kernel, out_shape=outs, in_specs=in_specs, out_specs=[VMEM...]
    dot_general x5 -> x0, matrix products: 6.36 us -> none  [the longest x1 1.8 us: body(): jnp.einsum('gcr,rd->gcd', select, whole, preferred_element_type=jnp.float32)]
  transfers between devices with their start and end apart: 3 -> 20, of which waited for: 3 -> 10; matrix products, arithmetic and copies ran while one was open for 1% -> 0% of each run, Pallas kernels for 0% -> 13%
where the time goes in v2:
time: 56.1 us; the launch traced here: 55.8 us
  starting transfers between devices  23.1 us (41%)
  waiting for transfers between devices  18.8 us (34%)
  Pallas kernels  11.1 us (20%)
  local copies, waits for them, and re-layouts  2.44 us (4%)
    ppermute x18, starting transfers between devices, turn(): return lax.ppermute(x, axis, [(i, (i + shift) % n) for i in range(n)])  19.4 us
    ppermute x18, waiting for transfers between devices, turn(): return lax.ppermute(x, axis, [(i, (i + shift) % n) for i in range(n)])  18.8 us
    pallas_call x8, Pallas kernels, call(): pl.pallas_call(kernel, out_shape=outs, in_specs=in_specs, out_specs=[VMEM...  11.1 us
    ppermute x2, starting transfers between devices, cross(): return lax.ppermute(x, ('pool', 'tp'), pairs)  3.62 us
    unnamed x8, local copies, waits for them, and re-layouts  2.42 us
  transfers between devices with their start and end apart: 20, of which 10 were waited for; matrix products, arithmetic and copies ran while one was open for 0% of the time, Pallas kernels for 13%

profile of v2, /device:TPU:0, one launch (start us, length us, event | category | flops | bytes accessed | tf_op | source)
XLA Modules:
  0.0 55.8 jit_solution(4417904902410609620)
XLA Ops:
  0.6 1.0 %copy-done.1 = bf16[128,2048]{1,0:T(8,128)(2,1)S(1)} copy-done((bf16[128,2048]{1,0:T(8,128)(2,1)S(1)}, bf16[128,2048]{1,0:T(8,128)(2,1)}, u32[]{:S(2)}) %copy-start.1) | copy-done | bytes 524312
  2.3 0.9 %select_own.1 = (bf16[32,2048]{1,0:T(8,128)(2,1)S(1)}, bf16[32,2048]{1,0:T(8,128)(2,1)S(1)}, bf16[32,2048]{1,0:T(8,128)(2,1)S(1)}, bf16[32,2048]{1,0:T(8,128)(2,1)S(1)}) custom-call(s32[3]{0:T(128)S(1)} %pad_add_fusion.pos_ref, s32[8,128]{1,0:T(8,128)S(1)} %bitcast.11, bf16[128,2048]{1,0:T(8,128)(2,1)S(1)} %copy-done.1), custom_call_target="tpu_custom_call" | custom-call | bytes 1048576 | tf_op jit(solution)/shard_map/select_own/pallas_call | solution.py:18
  4.2 3.1 %collective-permute-start.2 = (bf16[32,2048]{1,0:T(8,128)(2,1)S(1)}, bf16[32,2048]{1,0:T(8,128)(2,1)S(1)}, u32[]{:S(2)}, u32[]{:S(2)}) collective-permute-start(bf16[32,2048]{1,0:T(8,128)(2,1)S(1)} %get-tuple-element.34), channel_id=1, source_target_pairs={{0,4},{4,8},{8,12},{12,0},{1,5},{5,9},{9,13},{13,1},{2,6},{6,10},{... | collective-permute-start | bytes 393224 | tf_op jit(solution)/shard_map/ppermute | solution.py:171
  7.3 2.6 %collective-permute-start.3 = (bf16[32,2048]{1,0:T(8,128)(2,1)S(1)}, bf16[32,2048]{1,0:T(8,128)(2,1)S(1)}, u32[]{:S(2)}, u32[]{:S(2)}) collective-permute-start(bf16[32,2048]{1,0:T(8,128)(2,1)S(1)} %get-tuple-element.42), channel_id=1, source_target_pairs={{0,8},{4,12},{8,0},{12,4},{1,9},{5,13},{9,1},{13,5},{2,10},{6,14},... | collective-permute-start | bytes 393224 | tf_op jit(solution)/shard_map/ppermute | solution.py:171
  9.9 1.3 %collective-permute-start.4 = (bf16[32,2048]{1,0:T(8,128)(2,1)S(1)}, bf16[32,2048]{1,0:T(8,128)(2,1)S(1)}, u32[]{:S(2)}, u32[]{:S(2)}) collective-permute-start(bf16[32,2048]{1,0:T(8,128)(2,1)S(1)} %get-tuple-element.43), channel_id=1, source_target_pairs={{0,12},{4,0},{8,4},{12,8},{1,13},{5,1},{9,5},{13,9},{2,14},{6,2},{... | collective-permute-start | bytes 393224 | tf_op jit(solution)/shard_map/ppermute | solution.py:171
  11.2 1.5 %collective-permute-start.5 = (bf16[32,2048]{1,0:T(8,128)(2,1)S(1)}, bf16[32,2048]{1,0:T(8,128)(2,1)S(1)}, u32[]{:S(2)}, u32[]{:S(2)}) collective-permute-start(bf16[32,2048]{1,0:T(8,128)(2,1)S(1)} %get-tuple-element.35.after_ref.refs_0_), channel_id=1, source_target_pairs={{0,2},{2,0},{1,3},{3,1},{4,6},{6,4},{5,7},{7,5},{8,10},{10,8},{9,1... | collective-permute-start | bytes 393224 | tf_op jit(solution)/shard_map/ppermute | solution.py:171
  14.2 3.5 %load.1 = (bf16[4096,512]{1,0:T(8,128)(2,1)S(1)}, bf16[4096,512]{1,0:T(8,128)(2,1)S(1)}) custom-call(bf16[32,2048]{1,0:T(8,128)(2,1)S(1)} %get-tuple-element.35.after_ref.refs_0_, bf16[4096,512]{1,0:T(8,128)(2,1)} %bitcast.14, bf16[4096,512]{1,0:T(8,128)(2,1)} %bitcast.15), custom_call_target="tpu_custom_call" | custom-call | bytes 16777216 | tf_op jit(solution)/shard_map/load/pallas_call | solution.py:18
  17.7 1.0 %collective-permute-done.3.refs_2_ = bf16[32,2048]{1,0:T(8,128)(2,1)S(1)} collective-permute-done((bf16[32,2048]{1,0:T(8,128)(2,1)S(1)}, bf16[32,2048]{1,0:T(8,128)(2,1)S(1)}, u32[]{:S(2)}, u32[]{:S(2)}) %collective-permute-start.3) | collective-permute-done | bytes 131104 | tf_op jit(solution)/shard_map/ppermute | solution.py:171
  18.7 1.5 %collective-permute-start.7 = (bf16[32,2048]{1,0:T(8,128)(2,1)S(1)}, bf16[32,2048]{1,0:T(8,128)(2,1)S(1)}, u32[]{:S(2)}, u32[]{:S(2)}) collective-permute-start(bf16[32,2048]{1,0:T(8,128)(2,1)S(1)} %collective-permute-done.3.refs_2_), channel_id=1, source_target_pairs={{0,2},{2,0},{1,3},{3,1},{4,6},{6,4},{5,7},{7,5},{8,10},{10,8},{9,1... | collective-permute-start | bytes 393224 | tf_op jit(solution)/shard_map/ppermute | solution.py:171
  20.7 1.5 %collective-permute-start.6 = (bf16[32,2048]{1,0:T(8,128)(2,1)S(1)}, bf16[32,2048]{1,0:T(8,128)(2,1)S(1)}, u32[]{:S(2)}, u32[]{:S(2)}) collective-permute-start(bf16[32,2048]{1,0:T(8,128)(2,1)S(1)} %collective-permute-done.2.refs_1_), channel_id=1, source_target_pairs={{0,2},{2,0},{1,3},{3,1},{4,6},{6,4},{5,7},{7,5},{8,10},{10,8},{9,1... | collective-permute-start | bytes 393224 | tf_op jit(solution)/shard_map/ppermute | solution.py:171
  22.2 1.3 %near.1 = (f32[128,512]{1,0:T(8,128)S(1)}, f32[128,512]{1,0:T(8,128)S(1)}) custom-call(s32[3]{0:T(128)S(1)} %pad_add_fusion.pos_ref, bf16[4096,512]{1,0:T(8,128)(2,1)S(1)} %get-tuple-element.39.gate_ref, bf16[4096,512]{1,0:T(8,128)(2,1)S(1)} %get-tuple-element.40.up_ref, bf16[32,2048]{1,0:T(8,128)(2,1)S(1)} %get-tuple-element.35.after_ref.refs_0_, ...), custom_call_target="tpu_custom_call" | custom-call | flops 536870912 | bytes 4194304 | tf_op jit(solution)/shard_map/near/pallas_call | solution.py:18
  23.5 1.6 %collective-permute-done.7.refs_2_ = bf16[32,2048]{1,0:T(8,128)(2,1)S(1)} collective-permute-done((bf16[32,2048]{1,0:T(8,128)(2,1)S(1)}, bf16[32,2048]{1,0:T(8,128)(2,1)S(1)}, u32[]{:S(2)}, u32[]{:S(2)}) %collective-permute-start.7) | collective-permute-done | bytes 131104 | tf_op jit(solution)/shard_map/ppermute | solution.py:171
  25.0 2.8 %collective-permute-done.8.refs_3_ = bf16[32,2048]{1,0:T(8,128)(2,1)S(1)} collective-permute-done((bf16[32,2048]{1,0:T(8,128)(2,1)S(1)}, bf16[32,2048]{1,0:T(8,128)(2,1)S(1)}, u32[]{:S(2)}, u32[]{:S(2)}) %collective-permute-start.8) | collective-permute-done | bytes 131104 | tf_op jit(solution)/shard_map/ppermute | solution.py:171
  27.9 1.8 %collective-permute-done.6.refs_1_ = bf16[32,2048]{1,0:T(8,128)(2,1)S(1)} collective-permute-done((bf16[32,2048]{1,0:T(8,128)(2,1)S(1)}, bf16[32,2048]{1,0:T(8,128)(2,1)S(1)}, u32[]{:S(2)}, u32[]{:S(2)}) %collective-permute-start.6) | collective-permute-done | bytes 131104 | tf_op jit(solution)/shard_map/ppermute | solution.py:171
  29.6 1.7 %far.1 = (bf16[128,512]{1,0:T(8,128)(2,1)S(1)}, bf16[32,2048]{1,0:T(8,128)(2,1)S(1)}, bf16[32,2048]{1,0:T(8,128)(2,1)S(1)}, bf16[32,2048]{1,0:T(8,128)(2,1)S(1)}, bf16[32,2048]{1,0:T(8,128)(2,1)S(1)}) custom-call(s32[3]{0:T(128)S(1)} %pad_add_fusion.pos_ref, bf16[4096,512]{1,0:T(8,128)(2,1)S(1)} %get-tuple-element.39.gate_ref, ...), custom_call_target="tpu_custom_call" | custom-call | flops 805306368 | bytes 8388608 | tf_op jit(solution)/shard_map/far/pallas_call | solution.py:18
  31.3 1.6 %collective-permute-start.9 = (bf16[32,2048]{1,0:T(8,128)(2,1)S(1)}, bf16[32,2048]{1,0:T(8,128)(2,1)S(1)}, u32[]{:S(2)}, u32[]{:S(2)}) collective-permute-start(bf16[32,2048]{1,0:T(8,128)(2,1)S(1)} %get-tuple-element.48), channel_id=1, source_target_pairs={{0,2},{2,0},{1,3},{3,1},{4,6},{6,4},{5,7},{7,5},{8,10},{10,8},{9,1... | collective-permute-start | bytes 393224 | tf_op jit(solution)/shard_map/ppermute | solution.py:171
  32.9 3.5 %collective-permute-start.11 = (bf16[32,2048]{1,0:T(8,128)(2,1)S(1)}, bf16[32,2048]{1,0:T(8,128)(2,1)S(1)}, u32[]{:S(2)}, u32[]{:S(2)}) collective-permute-start(bf16[32,2048]{1,0:T(8,128)(2,1)S(1)} %get-tuple-element.50), channel_id=1, source_target_pairs={{0,14},{2,12},{4,2},{6,0},{8,6},{10,4},{12,10},{14,8},{1,15},{3,13... | collective-permute-start | bytes 393224 | tf_op jit(solution)/shard_map/ppermute | solution.py:177
  36.4 1.5 %collective-permute-start.12 = (bf16[32,2048]{1,0:T(8,128)(2,1)S(1)}, bf16[32,2048]{1,0:T(8,128)(2,1)S(1)}, u32[]{:S(2)}, u32[]{:S(2)}) collective-permute-start(bf16[32,2048]{1,0:T(8,128)(2,1)S(1)} %get-tuple-element.52), channel_id=1, source_target_pairs={{0,2},{2,0},{1,3},{3,1},{4,6},{6,4},{5,7},{7,5},{8,10},{10,8},{9,1... | collective-permute-start | bytes 393224 | tf_op jit(solution)/shard_map/ppermute | solution.py:171
  38.4 1.0 %keep.1 = (bf16[32,2048]{1,0:T(8,128)(2,1)S(1)}, bf16[32,2048]{1,0:T(8,128)(2,1)S(1)}, bf16[32,2048]{1,0:T(8,128)(2,1)S(1)}, bf16[32,2048]{1,0:T(8,128)(2,1)S(1)}) custom-call(s32[3]{0:T(128)S(1)} %pad_add_fusion.pos_ref, bf16[512,4096]{1,0:T(8,128)(2,1)S(1)} %bitcast.9, bf16[128,512]{1,0:T(8,128)(2,1)S(1)} %get-tuple-element.46.hidden_ref), custom_call_target="tpu_custom_call" | custom-call | flops 268435456 | bytes 2097152 | tf_op jit(solution)/shard_map/keep/pallas_call | solution.py:18
  40.4 2.7 %collective-permute-done.12 = bf16[32,2048]{1,0:T(8,128)(2,1)S(1)} collective-permute-done((bf16[32,2048]{1,0:T(8,128)(2,1)S(1)}, bf16[32,2048]{1,0:T(8,128)(2,1)S(1)}, u32[]{:S(2)}, u32[]{:S(2)}) %collective-permute-start.12) | collective-permute-done | bytes 131104 | tf_op jit(solution)/shard_map/ppermute | solution.py:171
  43.1 1.1 %collective-permute-start.13 = (bf16[32,2048]{1,0:T(8,128)(2,1)S(1)}, bf16[32,2048]{1,0:T(8,128)(2,1)S(1)}, u32[]{:S(2)}, u32[]{:S(2)}) collective-permute-start(bf16[32,2048]{1,0:T(8,128)(2,1)S(1)} %add_convert_fusion.1), channel_id=1, source_target_pairs={{0,8},{4,12},{8,0},{12,4},{1,9},{5,13},{9,1},{13,5},{2,10},{6,14},... | collective-permute-start | bytes 393224 | tf_op jit(solution)/shard_map/ppermute | solution.py:171
  44.8 1.5 %collective-permute-start.15 = (bf16[32,2048]{1,0:T(8,128)(2,1)S(1)}, bf16[32,2048]{1,0:T(8,128)(2,1)S(1)}, u32[]{:S(2)}, u32[]{:S(2)}) collective-permute-start(bf16[32,2048]{1,0:T(8,128)(2,1)S(1)} %add_convert_fusion), channel_id=1, source_target_pairs={{0,4},{4,8},{8,12},{12,0},{1,5},{5,9},{9,13},{13,1},{2,6},{6,10},{... | collective-permute-start | bytes 393224 | tf_op jit(solution)/shard_map/ppermute | solution.py:171
  46.4 6.8 %collective-permute-done.13.refs_3_ = bf16[32,2048]{1,0:T(8,128)(2,1)S(1)} collective-permute-done((bf16[32,2048]{1,0:T(8,128)(2,1)S(1)}, bf16[32,2048]{1,0:T(8,128)(2,1)S(1)}, u32[]{:S(2)}, u32[]{:S(2)}) %collective-permute-start.13) | collective-permute-done | bytes 131104 | tf_op jit(solution)/shard_map/ppermute | solution.py:171
  54.7 1.1 %mix.1 = bf16[128,2048]{1,0:T(8,128)(2,1)} custom-call(bf16[128,256]{1,0:T(8,128)(2,1)S(1)} %mixing.1.mixing_ref, bf16[32,2048]{1,0:T(8,128)(2,1)S(1)} %add_convert_fusion.2.refs_0_, bf16[32,2048]{1,0:T(8,128)(2,1)S(1)} %collective-permute-done.10.refs_1_, bf16[32,2048]{1,0:T(8,128)(2,1)S(1)} %collective-permute-done.11.refs_2_, ...), custom_call_target="tpu_custom_call" | custom-call | bytes 1572864 | tf_op jit(solution)/shard_map/mix/pallas_call | solution.py:18
  (40 shorter events, 7.9 us)
Async XLA Ops:
  0.0 3.3 %collective-permute-start.1 = (bf16[128,2048]{1,0:T(8,128)(2,1)}, bf16[128,2048]{1,0:T(8,128)(2,1)S(1)}, u32[]{:S(2)}, u32[]{:S(2)}) collective-permute-start(bf16[128,2048]{1,0:T(8,128)(2,1)} %tokens.1), channel_id=1, source_target_pairs={{0,1},{1,0},{2,3},{3,2},{4,5},{5,4},{6,7},{7,6},{8,9},{9,8},{10,11... | collective-permute-start | bytes 1572872 | tf_op jit(solution)/shard_map/ppermute | solution.py:171
  0.5 2.8 %collective-permute-start = (s32[8,128]{1,0:T(8,128)}, s32[8,128]{1,0:T(8,128)S(1)}, u32[]{:S(2)}, u32[]{:S(2)}) collective-permute-start(s32[8,128]{1,0:T(8,128)} %bitcast.10), channel_id=1, source_target_pairs={{0,1},{1,0},{2,3},{3,2},{4,5},{5,4},{6,7},{7,6},{8,9},{9,8},{10,11... | collective-permute-start | bytes 12296 | tf_op jit(solution)/shard_map/ppermute | solution.py:171
  0.6 1.0 %copy-start.1 = (bf16[128,2048]{1,0:T(8,128)(2,1)S(1)}, bf16[128,2048]{1,0:T(8,128)(2,1)}, u32[]{:S(2)}) copy-start(bf16[128,2048]{1,0:T(8,128)(2,1)} %tokens.1) | copy-start | bytes 1572868
  1.6 0.7 %copy-start.2 = (s32[128,8]{0,1:T(8,128)S(1)}, s32[128,8]{0,1:T(8,128)}, u32[]{:S(2)}) copy-start(s32[128,8]{0,1:T(8,128)} %param.7) | copy-start | bytes 12292
  4.2 13.5 %collective-permute-start.2 = (bf16[32,2048]{1,0:T(8,128)(2,1)S(1)}, bf16[32,2048]{1,0:T(8,128)(2,1)S(1)}, u32[]{:S(2)}, u32[]{:S(2)}) collective-permute-start(bf16[32,2048]{1,0:T(8,128)(2,1)S(1)} %get-tuple-element.34), channel_id=1, source_target_pairs={{0,4},{4,8},{8,12},{12,0},{1,5},{5,9},{9,13},{13,1},{2,6},{6,10},{... | collective-permute-start | bytes 393224 | tf_op jit(solution)/shard_map/ppermute | solution.py:171
  7.3 11.4 %collective-permute-start.3 = (bf16[32,2048]{1,0:T(8,128)(2,1)S(1)}, bf16[32,2048]{1,0:T(8,128)(2,1)S(1)}, u32[]{:S(2)}, u32[]{:S(2)}) collective-permute-start(bf16[32,2048]{1,0:T(8,128)(2,1)S(1)} %get-tuple-element.42), channel_id=1, source_target_pairs={{0,8},{4,12},{8,0},{12,4},{1,9},{5,13},{9,1},{13,5},{2,10},{6,14},... | collective-permute-start | bytes 393224 | tf_op jit(solution)/shard_map/ppermute | solution.py:171
  9.9 10.3 %collective-permute-start.4 = (bf16[32,2048]{1,0:T(8,128)(2,1)S(1)}, bf16[32,2048]{1,0:T(8,128)(2,1)S(1)}, u32[]{:S(2)}, u32[]{:S(2)}) collective-permute-start(bf16[32,2048]{1,0:T(8,128)(2,1)S(1)} %get-tuple-element.43), channel_id=1, source_target_pairs={{0,12},{4,0},{8,4},{12,8},{1,13},{5,1},{9,5},{13,9},{2,14},{6,2},{... | collective-permute-start | bytes 393224 | tf_op jit(solution)/shard_map/ppermute | solution.py:171
  11.2 12.2 %collective-permute-start.5 = (bf16[32,2048]{1,0:T(8,128)(2,1)S(1)}, bf16[32,2048]{1,0:T(8,128)(2,1)S(1)}, u32[]{:S(2)}, u32[]{:S(2)}) collective-permute-start(bf16[32,2048]{1,0:T(8,128)(2,1)S(1)} %get-tuple-element.35.after_ref.refs_0_), channel_id=1, source_target_pairs={{0,2},{2,0},{1,3},{3,1},{4,6},{6,4},{5,7},{7,5},{8,10},{10,8},{9,1... | collective-permute-start | bytes 393224 | tf_op jit(solution)/shard_map/ppermute | solution.py:171
  12.7 0.7 %copy-start.3 = (s32[128,8]{0,1:T(8,128)S(1)}, s32[128,8]{0,1:T(8,128)}, u32[]{:S(2)}) copy-start(s32[128,8]{0,1:T(8,128)} %param.8) | copy-start | bytes 12292
  17.7 11.9 %copy-start = (bf16[1,512,4096]{2,1,0:T(8,128)(2,1)S(1)}, bf16[1,512,4096]{2,1,0:T(8,128)(2,1)}, u32[]{:S(2)}) copy-start(bf16[1,512,4096]{2,1,0:T(8,128)(2,1)} %param.11) | copy-start | bytes 12582916
  18.7 6.4 %collective-permute-start.7 = (bf16[32,2048]{1,0:T(8,128)(2,1)S(1)}, bf16[32,2048]{1,0:T(8,128)(2,1)S(1)}, u32[]{:S(2)}, u32[]{:S(2)}) collective-permute-start(bf16[32,2048]{1,0:T(8,128)(2,1)S(1)} %collective-permute-done.3.refs_2_), channel_id=1, source_target_pairs={{0,2},{2,0},{1,3},{3,1},{4,6},{6,4},{5,7},{7,5},{8,10},{10,8},{9,1... | collective-permute-start | bytes 393224 | tf_op jit(solution)/shard_map/ppermute | solution.py:171
  20.2 7.7 %collective-permute-start.8 = (bf16[32,2048]{1,0:T(8,128)(2,1)S(1)}, bf16[32,2048]{1,0:T(8,128)(2,1)S(1)}, u32[]{:S(2)}, u32[]{:S(2)}) collective-permute-start(bf16[32,2048]{1,0:T(8,128)(2,1)S(1)} %collective-permute-done.4.refs_3_), channel_id=1, source_target_pairs={{0,2},{2,0},{1,3},{3,1},{4,6},{6,4},{5,7},{7,5},{8,10},{10,8},{9,1... | collective-permute-start | bytes 393224 | tf_op jit(solution)/shard_map/ppermute | solution.py:171
  20.7 8.9 %collective-permute-start.6 = (bf16[32,2048]{1,0:T(8,128)(2,1)S(1)}, bf16[32,2048]{1,0:T(8,128)(2,1)S(1)}, u32[]{:S(2)}, u32[]{:S(2)}) collective-permute-start(bf16[32,2048]{1,0:T(8,128)(2,1)S(1)} %collective-permute-done.2.refs_1_), channel_id=1, source_target_pairs={{0,2},{2,0},{1,3},{3,1},{4,6},{6,4},{5,7},{7,5},{8,10},{10,8},{9,1... | collective-permute-start | bytes 393224 | tf_op jit(solution)/shard_map/ppermute | solution.py:171
  31.3 8.9 %collective-permute-start.9 = (bf16[32,2048]{1,0:T(8,128)(2,1)S(1)}, bf16[32,2048]{1,0:T(8,128)(2,1)S(1)}, u32[]{:S(2)}, u32[]{:S(2)}) collective-permute-start(bf16[32,2048]{1,0:T(8,128)(2,1)S(1)} %get-tuple-element.48), channel_id=1, source_target_pairs={{0,2},{2,0},{1,3},{3,1},{4,6},{6,4},{5,7},{7,5},{8,10},{10,8},{9,1... | collective-permute-start | bytes 393224 | tf_op jit(solution)/shard_map/ppermute | solution.py:171
  32.9 13.5 %collective-permute-start.11 = (bf16[32,2048]{1,0:T(8,128)(2,1)S(1)}, bf16[32,2048]{1,0:T(8,128)(2,1)S(1)}, u32[]{:S(2)}, u32[]{:S(2)}) collective-permute-start(bf16[32,2048]{1,0:T(8,128)(2,1)S(1)} %get-tuple-element.50), channel_id=1, source_target_pairs={{0,14},{2,12},{4,2},{6,0},{8,6},{10,4},{12,10},{14,8},{1,15},{3,13... | collective-permute-start | bytes 393224 | tf_op jit(solution)/shard_map/ppermute | solution.py:177
  36.4 6.6 %collective-permute-start.12 = (bf16[32,2048]{1,0:T(8,128)(2,1)S(1)}, bf16[32,2048]{1,0:T(8,128)(2,1)S(1)}, u32[]{:S(2)}, u32[]{:S(2)}) collective-permute-start(bf16[32,2048]{1,0:T(8,128)(2,1)S(1)} %get-tuple-element.52), channel_id=1, source_target_pairs={{0,2},{2,0},{1,3},{3,1},{4,6},{6,4},{5,7},{7,5},{8,10},{10,8},{9,1... | collective-permute-start | bytes 393224 | tf_op jit(solution)/shard_map/ppermute | solution.py:171
  37.9 6.9 %collective-permute-start.14 = (bf16[32,2048]{1,0:T(8,128)(2,1)S(1)}, bf16[32,2048]{1,0:T(8,128)(2,1)S(1)}, u32[]{:S(2)}, u32[]{:S(2)}) collective-permute-start(bf16[32,2048]{1,0:T(8,128)(2,1)S(1)} %get-tuple-element.54), channel_id=1, source_target_pairs={{0,2},{2,0},{1,3},{3,1},{4,6},{6,4},{5,7},{7,5},{8,10},{10,8},{9,1... | collective-permute-start | bytes 393224 | tf_op jit(solution)/shard_map/ppermute | solution.py:171
  39.4 6.9 %collective-permute-start.10 = (bf16[32,2048]{1,0:T(8,128)(2,1)S(1)}, bf16[32,2048]{1,0:T(8,128)(2,1)S(1)}, u32[]{:S(2)}, u32[]{:S(2)}) collective-permute-start(bf16[32,2048]{1,0:T(8,128)(2,1)S(1)} %get-tuple-element.49), channel_id=1, source_target_pairs={{0,12},{2,14},{4,0},{6,2},{8,4},{10,6},{12,8},{14,10},{1,13},{3,15... | collective-permute-start | bytes 393224 | tf_op jit(solution)/shard_map/ppermute | solution.py:177
  40.3 13.5 %collective-permute-start.16 = (bf16[16,2048]{1,0:T(8,128)(2,1)S(1)}, bf16[16,2048]{1,0:T(8,128)(2,1)S(1)}, u32[]{:S(2)}, u32[]{:S(2)}) collective-permute-start(bf16[16,2048]{1,0:T(8,128)(2,1)S(1)} %slice.20), channel_id=1, source_target_pairs={{0,1},{1,0},{2,3},{3,2},{4,5},{5,4},{6,7},{7,6},{8,9},{9,8},{10,11... | collective-permute-start | bytes 196616 | tf_op jit(solution)/shard_map/ppermute | solution.py:171
  43.1 10.1 %collective-permute-start.13 = (bf16[32,2048]{1,0:T(8,128)(2,1)S(1)}, bf16[32,2048]{1,0:T(8,128)(2,1)S(1)}, u32[]{:S(2)}, u32[]{:S(2)}) collective-permute-start(bf16[32,2048]{1,0:T(8,128)(2,1)S(1)} %add_convert_fusion.1), channel_id=1, source_target_pairs={{0,8},{4,12},{8,0},{12,4},{1,9},{5,13},{9,1},{13,5},{2,10},{6,14},... | collective-permute-start | bytes 393224 | tf_op jit(solution)/shard_map/ppermute | solution.py:171
  44.8 8.4 %collective-permute-start.15 = (bf16[32,2048]{1,0:T(8,128)(2,1)S(1)}, bf16[32,2048]{1,0:T(8,128)(2,1)S(1)}, u32[]{:S(2)}, u32[]{:S(2)}) collective-permute-start(bf16[32,2048]{1,0:T(8,128)(2,1)S(1)} %add_convert_fusion), channel_id=1, source_target_pairs={{0,4},{4,8},{8,12},{12,0},{1,5},{5,9},{9,13},{13,1},{2,6},{6,10},{... | collective-permute-start | bytes 393224 | tf_op jit(solution)/shard_map/ppermute | solution.py:171
  46.4 7.5 %collective-permute-start.17 = (bf16[16,2048]{1,0:T(8,128)(2,1)S(1)}, bf16[16,2048]{1,0:T(8,128)(2,1)S(1)}, u32[]{:S(2)}, u32[]{:S(2)}) collective-permute-start(bf16[16,2048]{1,0:T(8,128)(2,1)S(1)} %add_convert_fusion.3), channel_id=1, source_target_pairs={{0,1},{1,0},{2,3},{3,2},{4,5},{5,4},{6,7},{7,6},{8,9},{9,8},{10,11... | collective-permute-start | bytes 196616 | tf_op jit(solution)/shard_map/ppermute | solution.py:171
  53.2 1.3 %collective-permute-start.18 = (bf16[16,2048]{1,0:T(8,128)(2,1)S(1)}, bf16[16,2048]{1,0:T(8,128)(2,1)S(1)}, u32[]{:S(2)}, u32[]{:S(2)}) collective-permute-start(bf16[16,2048]{1,0:T(8,128)(2,1)S(1)} %slice.23), channel_id=1, source_target_pairs={{0,1},{1,0},{2,3},{3,2},{4,5},{5,4},{6,7},{7,6},{8,9},{9,8},{10,11... | collective-permute-start | bytes 196616 | tf_op jit(solution)/shard_map/ppermute | solution.py:171
  53.3 1.5 %collective-permute-start.19 = (bf16[16,2048]{1,0:T(8,128)(2,1)S(1)}, bf16[16,2048]{1,0:T(8,128)(2,1)S(1)}, u32[]{:S(2)}, u32[]{:S(2)}) collective-permute-start(bf16[16,2048]{1,0:T(8,128)(2,1)S(1)} %slice.24), channel_id=1, source_target_pairs={{0,1},{1,0},{2,3},{3,2},{4,5},{5,4},{6,7},{7,6},{8,9},{9,8},{10,11... | collective-permute-start | bytes 196616 | tf_op jit(solution)/shard_map/ppermute | solution.py:171

commit v3 on v2

--- a/solution.py
+++ b/solution.py
@@ -98,26 +98,45 @@
     out_ref[:, n:] = (mixing - hi.astype(F32)).astype(BF16)
 
 
-def load_kernel(after_ref, gate, up, gate_out, up_out, sems):
-    pairs = ((gate, gate_out), (up, up_out))
-    copies = [pltpu.make_async_copy(a, b, sems.at[i]) for i, (a, b) in enumerate(pairs)]
-    for c in copies:
-        c.start()
-    for c in copies:
-        c.wait()
-
-
 def stacked(refs):
     return jnp.concatenate([r[...] for r in refs], axis=0)
 
 
-def near_kernel(n_tp, pos_ref, gate_ref, up_ref, *refs):
-    rows, gate_out, up_out = refs[:-2], refs[-2], refs[-1]
+def near_kernel(n_tp, tiles, pos_ref, gate_ref, up_ref, *refs):
+    rows = refs[:-7]
+    gate_out, up_out, gate_far, up_far, gate_near, up_near, sems = refs[-7:]
     width = rows[0].shape[1]
-    at = pl.ds(pl.multiple_of(pos_ref[2] * width, width), width)
+    tp = pos_ref[2]
+    depth = width // tiles
+    pairs = ((gate_ref, gate_near, gate_far), (up_ref, up_near, up_far))
+    near, far = [], []
+    for i in range(tiles):
+        at = pl.ds(pl.multiple_of(tp * width + i * depth, depth), depth)
+        for j, (ref, held, _) in enumerate(pairs):
+            near.append(pltpu.make_async_copy(ref.at[at, :], held.at[pl.ds(i * depth, depth), :], sems.at[i * 2 + j]))
+    for k in range(1, n_tp):
+        for i in range(2):
+            half = width // 2
+            at = pl.ds(pl.multiple_of(lax.rem(tp - k + n_tp, n_tp) * width + i * half, half), half)
+            to = pl.ds((k - 1) * width + i * half, half)
+            for j, (ref, _, out) in enumerate(pairs):
+                sem = sems.at[2 * tiles + ((k - 1) * 2 + i) * 2 + j]
+                far.append(pltpu.make_async_copy(ref.at[at, :], out.at[to, :], sem))
+    for c in near + far:
+        c.start()
     block = stacked(rows)
-    gate_out[...] = jnp.dot(block, gate_ref[at, :], preferred_element_type=F32)
-    up_out[...] = jnp.dot(block, up_ref[at, :], preferred_element_type=F32)
+    gate = up = None
+    for i in range(tiles):
+        cut = block[:, i * depth : (i + 1) * depth]
+        near[2 * i].wait()
+        g = jnp.dot(cut, gate_near[i * depth : (i + 1) * depth, :], preferred_element_type=F32)
+        near[2 * i + 1].wait()
+        u = jnp.dot(cut, up_near[i * depth : (i + 1) * depth, :], preferred_element_type=F32)
+        gate, up = (g, u) if gate is None else (gate + g, up + u)
+    gate_out[...] = gate
+    up_out[...] = up
+    for c in far:
+        c.wait()
 
 
 def far_kernel(n_tp, n_chunks, pos_ref, gate_ref, up_ref, down_ref, gate_in, up_in, *refs):
@@ -128,7 +147,7 @@
     tp = pos_ref[2]
     gate, up = gate_in[...], up_in[...]
     for k in range(1, n_tp):
-        at = pl.ds(pl.multiple_of(lax.rem(tp - k + n_tp, n_tp) * width, width), width)
+        at = pl.ds((k - 1) * width, width)
         block = stacked(rows[k - 1])
         gate += jnp.dot(block, gate_ref[at, :], preferred_element_type=F32)
         up += jnp.dot(block, up_ref[at, :], preferred_element_type=F32)
@@ -191,7 +210,7 @@
     pos = jnp.stack([lax.axis_index(a) for a in ("pool", "pair", "tp")]).astype(jnp.int32)
     routes_t, weights_t = routes.T, gate_weights.T
     rows = n_pair * CAP
-    small = n_pool <= 4 and n_tp == 2
+    small = n_pool == 4 and n_tp == 2
     direct = [1] if small else []
 
     def shape(r, c, t=BF16):
@@ -217,17 +236,7 @@
         2 * 2 * streams * width,
         alias={1 + 2 * (n_pair - 1) + s: s for s in range(n_pool)},
     )
-    gate_mat, up_mat = call(
-        load_kernel,
-        "load",
-        [jax.ShapeDtypeStruct(w.shape[1:], BF16) for w in (w_gate, w_up)],
-        [VMEM] + [HBM] * 2,
-        (leaving[0], w_gate[0], w_up[0]),
-        2 * 2 * (w_gate.size + w_up.size),
-        scratch=[pltpu.SemaphoreType.DMA((2,))],
-        vmem=44,
-    )
-    down_mat = w_down[0]
+    gate_mat, up_mat, down_mat = w_gate[0], w_up[0], w_down[0]
     slots = n_pool * rows
     (mixing,) = call(
         functools.partial(mixing_kernel, n_pool, n_pair),
@@ -240,23 +249,28 @@
 
     near = [turn(leaving[s], "pool", s) if s else leaving[0] for s in range(n_pool)]
     first = 1 if n_pool > 1 else 0
-    near[first], gate_mat, up_mat, mixing = lax.optimization_barrier((near[first], gate_mat, up_mat, mixing))
+    near[first], mixing = lax.optimization_barrier((near[first], mixing))
     far = [[turn(b, "tp", k) for b in near] for k in range(1, n_tp)]
-    gate, up = call(
-        functools.partial(near_kernel, n_tp),
+    tiles = 4 if width % 1024 == 0 else 1
+    rest = (n_tp - 1) * width
+    gate, up, gate_far, up_far = call(
+        functools.partial(near_kernel, n_tp, tiles),
         "near",
-        [shape(slots, hidden_units, F32)] * 2,
-        [SMEM] + [VMEM] * (2 + n_pool),
+        [shape(slots, hidden_units, F32)] * 2 + [shape(rest, hidden_units)] * 2,
+        [SMEM] + [HBM] * 2 + [VMEM] * n_pool,
         (pos, gate_mat, up_mat, *near),
-        4 * width * hidden_units,
+        2 * 2 * (w_gate.size + w_up.size),
         4 * slots * width * hidden_units,
+        scratch=[pltpu.VMEM((width, hidden_units), BF16)] * 2
+        + [pltpu.SemaphoreType.DMA((2 * tiles + 4 * (n_tp - 1),))],
+        vmem=48,
     )
     hidden, *sent = call(
         functools.partial(far_kernel, n_tp, n_pool),
         "far",
         [shape(slots, hidden_units)] + [shape(rows, width)] * (n_pool * (n_tp - 1)),
         [SMEM] + [VMEM] * (5 + n_pool * (n_tp - 1)),
-        (pos, gate_mat, up_mat, down_mat, gate, up, *sum(far, [])),
+        (pos, gate_far, up_far, down_mat, gate, up, *sum(far, [])),
         8 * width * hidden_units,
         6 * slots * width * hidden_units,
     )
@@ -271,13 +285,18 @@
         2 * slots * width * hidden_units,
     )
 
-    home = []
-    for s in range(n_pool):
+    home = [None] * n_pool
+    for s in [2, 1, 3, 0] if small else range(n_pool):
         if s in direct:
-            home.append([cross(kept[s], -s, 0)] + [cross(sent[k - 1][s], -s, k) for k in range(1, n_tp)])
+            home[s] = [cross(kept[s], -s, 0)] + [cross(sent[k - 1][s], -s, k) for k in range(1, n_tp)]
         else:
-            total = add([kept[s]] + [turn(sent[k - 1][s], "tp", k) for k in range(1, n_tp)])
-            home.append([turn(total, "pool", -s) if s else total])
+            come = [turn(sent[k - 1][s], "tp", k) for k in range(1, n_tp)]
+            total = add([kept[s]] + come)
+            if small and s == 3:
+                total, sent[0][0] = lax.optimization_barrier((total, sent[0][0]))
+            home[s] = [turn(total, "pool", -s) if s else total]
+    if small:
+        home[1], home[0] = lax.optimization_barrier((home[1], home[0]))
     layout, parts = [], []
     for s in range(n_pool):
         layout.append((len(home[s]), 0))

time: 56.1 us -> 50.9 us (0.907)
  waiting for transfers between devices: 18.8 us -> 12.2 us
  starting transfers between devices: 23.1 us -> 25 us
    ppermute x18, waiting for transfers between devices: 18.8 us -> 12.1 us  [turn(): return lax.ppermute(x, axis, [(i, (i + shift) % n) for i in range(n)])]
    ppermute x18, starting transfers between devices: 19.4 us -> 21.2 us  [turn(): return lax.ppermute(x, axis, [(i, (i + shift) % n) for i in range(n)])]
    pallas_call x8 -> x7, Pallas kernels: 11.1 us -> 10.7 us  [call(): pl.pallas_call(kernel, out_shape=outs, in_specs=in_specs, out_specs=[VMEM...]
  transfers between devices with their start and end apart: 20 -> 20, of which waited for: 10 -> 6; matrix products, arithmetic and copies ran while one was open for 0% -> 0% of each run, Pallas kernels for 13% -> 14%
where the time goes in v3:
time: 50.9 us; the launch traced here: 50.7 us
  starting transfers between devices  25 us (49%)
  waiting for transfers between devices  12.2 us (24%)
  Pallas kernels  10.7 us (21%)
  local copies, waits for them, and re-layouts  2.44 us (5%)
    ppermute x18, starting transfers between devices, turn(): return lax.ppermute(x, axis, [(i, (i + shift) % n) for i in range(n)])  21.2 us
    ppermute x18, waiting for transfers between devices, turn(): return lax.ppermute(x, axis, [(i, (i + shift) % n) for i in range(n)])  12.1 us
    pallas_call x7, Pallas kernels, call(): pl.pallas_call(kernel, out_shape=outs, in_specs=in_specs, out_specs=[VMEM...  10.7 us
    ppermute x2, starting transfers between devices, cross(): return lax.ppermute(x, ('pool', 'tp'), pairs)  3.86 us
    unnamed x8, local copies, waits for them, and re-layouts  2.42 us
  transfers between devices with their start and end apart: 20, of which 6 were waited for; matrix products, arithmetic and copies ran while one was open for 0% of the time, Pallas kernels for 14%

profile of v3, /device:TPU:0, one launch (start us, length us, event | category | flops | bytes accessed | tf_op | source)
XLA Modules:
  0.0 50.7 jit_solution(3030422771082410406)
XLA Ops:
  0.6 1.0 %copy-done.1 = bf16[128,2048]{1,0:T(8,128)(2,1)S(1)} copy-done((bf16[128,2048]{1,0:T(8,128)(2,1)S(1)}, bf16[128,2048]{1,0:T(8,128)(2,1)}, u32[]{:S(2)}) %copy-start.1) | copy-done | bytes 524312
  2.3 0.9 %select_own.1 = (bf16[32,2048]{1,0:T(8,128)(2,1)S(1)}, bf16[32,2048]{1,0:T(8,128)(2,1)S(1)}, bf16[32,2048]{1,0:T(8,128)(2,1)S(1)}, bf16[32,2048]{1,0:T(8,128)(2,1)S(1)}) custom-call(s32[3]{0:T(128)S(1)} %pad_add_fusion.pos_ref, s32[8,128]{1,0:T(8,128)S(1)} %bitcast.11, bf16[128,2048]{1,0:T(8,128)(2,1)S(1)} %copy-done.1), custom_call_target="tpu_custom_call" | custom-call | bytes 1048576 | tf_op jit(solution)/shard_map/select_own/pallas_call | solution.py:18
  3.3 0.9 %select_other.1 = (bf16[32,2048]{1,0:T(8,128)(2,1)S(1)}, bf16[32,2048]{1,0:T(8,128)(2,1)S(1)}, bf16[32,2048]{1,0:T(8,128)(2,1)S(1)}, bf16[32,2048]{1,0:T(8,128)(2,1)S(1)}) custom-call(s32[3]{0:T(128)S(1)} %pad_add_fusion.pos_ref, s32[8,128]{1,0:T(8,128)S(1)} %collective-permute-done.refs_0_, ...), custom_call_target="tpu_custom_call", output_to_operand_aliasing={{0}: (3, {}), {1}: (4, {}), {2}: (5, {}), {3}: (6, {})} | custom-call | bytes 1048576 | tf_op jit(solution)/shard_map/select_other/pallas_call | solution.py:18
  4.2 3.1 %collective-permute-start.2 = (bf16[32,2048]{1,0:T(8,128)(2,1)S(1)}, bf16[32,2048]{1,0:T(8,128)(2,1)S(1)}, u32[]{:S(2)}, u32[]{:S(2)}) collective-permute-start(bf16[32,2048]{1,0:T(8,128)(2,1)S(1)} %get-tuple-element.37), channel_id=1, source_target_pairs={{0,4},{4,8},{8,12},{12,0},{1,5},{5,9},{9,13},{13,1},{2,6},{6,10},{... | collective-permute-start | bytes 393224 | tf_op jit(solution)/shard_map/ppermute | solution.py:190
  7.3 2.6 %collective-permute-start.3 = (bf16[32,2048]{1,0:T(8,128)(2,1)S(1)}, bf16[32,2048]{1,0:T(8,128)(2,1)S(1)}, u32[]{:S(2)}, u32[]{:S(2)}) collective-permute-start(bf16[32,2048]{1,0:T(8,128)(2,1)S(1)} %get-tuple-element.41), channel_id=1, source_target_pairs={{0,8},{4,12},{8,0},{12,4},{1,9},{5,13},{9,1},{13,5},{2,10},{6,14},... | collective-permute-start | bytes 393224 | tf_op jit(solution)/shard_map/ppermute | solution.py:190
  9.9 1.3 %collective-permute-start.4 = (bf16[32,2048]{1,0:T(8,128)(2,1)S(1)}, bf16[32,2048]{1,0:T(8,128)(2,1)S(1)}, u32[]{:S(2)}, u32[]{:S(2)}) collective-permute-start(bf16[32,2048]{1,0:T(8,128)(2,1)S(1)} %get-tuple-element.42), channel_id=1, source_target_pairs={{0,12},{4,0},{8,4},{12,8},{1,13},{5,1},{9,5},{13,9},{2,14},{6,2},{... | collective-permute-start | bytes 393224 | tf_op jit(solution)/shard_map/ppermute | solution.py:190
  11.2 1.5 %collective-permute-start.5 = (bf16[32,2048]{1,0:T(8,128)(2,1)S(1)}, bf16[32,2048]{1,0:T(8,128)(2,1)S(1)}, u32[]{:S(2)}, u32[]{:S(2)}) collective-permute-start(bf16[32,2048]{1,0:T(8,128)(2,1)S(1)} %get-tuple-element.38.after_ref.refs_0_), channel_id=1, source_target_pairs={{0,2},{2,0},{1,3},{3,1},{4,6},{6,4},{5,7},{7,5},{8,10},{10,8},{9,1... | collective-permute-start | bytes 393224 | tf_op jit(solution)/shard_map/ppermute | solution.py:190
  14.2 1.3 %collective-permute-start.6 = (bf16[32,2048]{1,0:T(8,128)(2,1)S(1)}, bf16[32,2048]{1,0:T(8,128)(2,1)S(1)}, u32[]{:S(2)}, u32[]{:S(2)}) collective-permute-start(bf16[32,2048]{1,0:T(8,128)(2,1)S(1)} %collective-permute-done.2.refs_1_), channel_id=1, source_target_pairs={{0,2},{2,0},{1,3},{3,1},{4,6},{6,4},{5,7},{7,5},{8,10},{10,8},{9,1... | collective-permute-start | bytes 393224 | tf_op jit(solution)/shard_map/ppermute | solution.py:190
  15.4 3.2 %collective-permute-done.3.refs_2_ = bf16[32,2048]{1,0:T(8,128)(2,1)S(1)} collective-permute-done((bf16[32,2048]{1,0:T(8,128)(2,1)S(1)}, bf16[32,2048]{1,0:T(8,128)(2,1)S(1)}, u32[]{:S(2)}, u32[]{:S(2)}) %collective-permute-start.3) | collective-permute-done | bytes 131104 | tf_op jit(solution)/shard_map/ppermute | solution.py:190
  18.7 1.5 %collective-permute-start.7 = (bf16[32,2048]{1,0:T(8,128)(2,1)S(1)}, bf16[32,2048]{1,0:T(8,128)(2,1)S(1)}, u32[]{:S(2)}, u32[]{:S(2)}) collective-permute-start(bf16[32,2048]{1,0:T(8,128)(2,1)S(1)} %collective-permute-done.3.refs_2_), channel_id=1, source_target_pairs={{0,2},{2,0},{1,3},{3,1},{4,6},{6,4},{5,7},{7,5},{8,10},{10,8},{9,1... | collective-permute-start | bytes 393224 | tf_op jit(solution)/shard_map/ppermute | solution.py:190
  20.7 4.3 %near.1 = (f32[128,512]{1,0:T(8,128)S(1)}, f32[128,512]{1,0:T(8,128)S(1)}, bf16[2048,512]{1,0:T(8,128)(2,1)S(1)}, bf16[2048,512]{1,0:T(8,128)(2,1)S(1)}) custom-call(s32[3]{0:T(128)S(1)} %pad_add_fusion.pos_ref, bf16[4096,512]{1,0:T(8,128)(2,1)} %bitcast.14, bf16[4096,512]{1,0:T(8,128)(2,1)} %bitcast.15, ...), custom_call_target="tpu_custom_call" | custom-call | flops 536870912 | bytes 16777216 | tf_op jit(solution)/shard_map/near/pallas_call | solution.py:18
  25.1 1.7 %collective-permute-done.8.refs_3_ = bf16[32,2048]{1,0:T(8,128)(2,1)S(1)} collective-permute-done((bf16[32,2048]{1,0:T(8,128)(2,1)S(1)}, bf16[32,2048]{1,0:T(8,128)(2,1)S(1)}, u32[]{:S(2)}, u32[]{:S(2)}) %collective-permute-start.8) | collective-permute-done | bytes 131104 | tf_op jit(solution)/shard_map/ppermute | solution.py:190
  26.8 1.6 %far.1 = (bf16[128,512]{1,0:T(8,128)(2,1)S(1)}, bf16[32,2048]{1,0:T(8,128)(2,1)S(1)}, bf16[32,2048]{1,0:T(8,128)(2,1)S(1)}, bf16[32,2048]{1,0:T(8,128)(2,1)S(1)}, bf16[32,2048]{1,0:T(8,128)(2,1)S(1)}) custom-call(s32[3]{0:T(128)S(1)} %pad_add_fusion.pos_ref, bf16[2048,512]{1,0:T(8,128)(2,1)S(1)} %get-tuple-element.43.gate_ref, ...), custom_call_target="tpu_custom_call" | custom-call | flops 805306368 | bytes 8388608 | tf_op jit(solution)/shard_map/far/pallas_call | solution.py:18
  28.5 1.6 %collective-permute-start.11 = (bf16[32,2048]{1,0:T(8,128)(2,1)S(1)}, bf16[32,2048]{1,0:T(8,128)(2,1)S(1)}, u32[]{:S(2)}, u32[]{:S(2)}) collective-permute-start(bf16[32,2048]{1,0:T(8,128)(2,1)S(1)} %get-tuple-element.52), channel_id=1, source_target_pairs={{0,2},{2,0},{1,3},{3,1},{4,6},{6,4},{5,7},{7,5},{8,10},{10,8},{9,1... | collective-permute-start | bytes 393224 | tf_op jit(solution)/shard_map/ppermute | solution.py:190
  30.0 3.5 %collective-permute-start.10 = (bf16[32,2048]{1,0:T(8,128)(2,1)S(1)}, bf16[32,2048]{1,0:T(8,128)(2,1)S(1)}, u32[]{:S(2)}, u32[]{:S(2)}) collective-permute-start(bf16[32,2048]{1,0:T(8,128)(2,1)S(1)} %get-tuple-element.49), channel_id=1, source_target_pairs={{0,14},{2,12},{4,2},{6,0},{8,6},{10,4},{12,10},{14,8},{1,15},{3,13... | collective-permute-start | bytes 393224 | tf_op jit(solution)/shard_map/ppermute | solution.py:196
  33.6 1.5 %collective-permute-start.13 = (bf16[32,2048]{1,0:T(8,128)(2,1)S(1)}, bf16[32,2048]{1,0:T(8,128)(2,1)S(1)}, u32[]{:S(2)}, u32[]{:S(2)}) collective-permute-start(bf16[32,2048]{1,0:T(8,128)(2,1)S(1)} %get-tuple-element.59), channel_id=1, source_target_pairs={{0,2},{2,0},{1,3},{3,1},{4,6},{6,4},{5,7},{7,5},{8,10},{10,8},{9,1... | collective-permute-start | bytes 393224 | tf_op jit(solution)/shard_map/ppermute | solution.py:190
  35.0 1.0 %keep.1 = (bf16[32,2048]{1,0:T(8,128)(2,1)S(1)}, bf16[32,2048]{1,0:T(8,128)(2,1)S(1)}, bf16[32,2048]{1,0:T(8,128)(2,1)S(1)}, bf16[32,2048]{1,0:T(8,128)(2,1)S(1)}) custom-call(s32[3]{0:T(128)S(1)} %pad_add_fusion.pos_ref, bf16[512,4096]{1,0:T(8,128)(2,1)S(1)} %bitcast.9, bf16[128,512]{1,0:T(8,128)(2,1)S(1)} %get-tuple-element.47.hidden_ref), custom_call_target="tpu_custom_call" | custom-call | flops 268435456 | bytes 2097152 | tf_op jit(solution)/shard_map/keep/pallas_call | solution.py:18
  36.4 1.0 %collective-permute-done.11 = bf16[32,2048]{1,0:T(8,128)(2,1)S(1)} collective-permute-done((bf16[32,2048]{1,0:T(8,128)(2,1)S(1)}, bf16[32,2048]{1,0:T(8,128)(2,1)S(1)}, u32[]{:S(2)}, u32[]{:S(2)}) %collective-permute-start.11) | collective-permute-done | bytes 131104 | tf_op jit(solution)/shard_map/ppermute | solution.py:190
  38.0 2.7 %collective-permute-start.15 = (bf16[32,2048]{1,0:T(8,128)(2,1)S(1)}, bf16[32,2048]{1,0:T(8,128)(2,1)S(1)}, u32[]{:S(2)}, u32[]{:S(2)}) collective-permute-start(bf16[32,2048]{1,0:T(8,128)(2,1)S(1)} %add_convert_fusion.2), channel_id=1, source_target_pairs={{0,4},{4,8},{8,12},{12,0},{1,5},{5,9},{9,13},{13,1},{2,6},{6,10},{... | collective-permute-start | bytes 393224 | tf_op jit(solution)/shard_map/ppermute | solution.py:190
  40.7 2.0 %collective-permute-start.14 = (bf16[32,2048]{1,0:T(8,128)(2,1)S(1)}, bf16[32,2048]{1,0:T(8,128)(2,1)S(1)}, u32[]{:S(2)}, u32[]{:S(2)}) collective-permute-start(bf16[32,2048]{1,0:T(8,128)(2,1)S(1)} %add_convert_fusion), channel_id=1, source_target_pairs={{0,8},{4,12},{8,0},{12,4},{1,9},{5,13},{9,1},{13,5},{2,10},{6,14},... | collective-permute-start | bytes 393224 | tf_op jit(solution)/shard_map/ppermute | solution.py:190
  42.7 2.4 %collective-permute-done.15.refs_4_ = bf16[32,2048]{1,0:T(8,128)(2,1)S(1)} collective-permute-done((bf16[32,2048]{1,0:T(8,128)(2,1)S(1)}, bf16[32,2048]{1,0:T(8,128)(2,1)S(1)}, u32[]{:S(2)}, u32[]{:S(2)}) %collective-permute-start.15) | collective-permute-done | bytes 131104 | tf_op jit(solution)/shard_map/ppermute | solution.py:190
  45.8 2.5 %collective-permute-done.14.refs_3_ = bf16[32,2048]{1,0:T(8,128)(2,1)S(1)} collective-permute-done((bf16[32,2048]{1,0:T(8,128)(2,1)S(1)}, bf16[32,2048]{1,0:T(8,128)(2,1)S(1)}, u32[]{:S(2)}, u32[]{:S(2)}) %collective-permute-start.14) | collective-permute-done | bytes 131104 | tf_op jit(solution)/shard_map/ppermute | solution.py:190
  48.4 1.2 %collective-permute-done.18.refs_7_ = bf16[16,2048]{1,0:T(8,128)(2,1)S(1)} collective-permute-done((bf16[16,2048]{1,0:T(8,128)(2,1)S(1)}, bf16[16,2048]{1,0:T(8,128)(2,1)S(1)}, u32[]{:S(2)}, u32[]{:S(2)}) %collective-permute-start.18) | collective-permute-done | bytes 65568 | tf_op jit(solution)/shard_map/ppermute | solution.py:190
  49.6 1.1 %mix.1 = bf16[128,2048]{1,0:T(8,128)(2,1)} custom-call(bf16[128,256]{1,0:T(8,128)(2,1)S(1)} %mixing.1.mixing_ref, bf16[32,2048]{1,0:T(8,128)(2,1)S(1)} %add_convert_fusion.1.refs_0_, bf16[32,2048]{1,0:T(8,128)(2,1)S(1)} %collective-permute-done.9.refs_1_, bf16[32,2048]{1,0:T(8,128)(2,1)S(1)} %collective-permute-done.10.refs_2_, ...), custom_call_target="tpu_custom_call" | custom-call | bytes 1572864 | tf_op jit(solution)/shard_map/mix/pallas_call | solution.py:18
  (39 shorter events, 4.9 us)
Async XLA Ops:
  0.0 3.3 %collective-permute-start.1 = (bf16[128,2048]{1,0:T(8,128)(2,1)}, bf16[128,2048]{1,0:T(8,128)(2,1)S(1)}, u32[]{:S(2)}, u32[]{:S(2)}) collective-permute-start(bf16[128,2048]{1,0:T(8,128)(2,1)} %tokens.1), channel_id=1, source_target_pairs={{0,1},{1,0},{2,3},{3,2},{4,5},{5,4},{6,7},{7,6},{8,9},{9,8},{10,11... | collective-permute-start | bytes 1572872 | tf_op jit(solution)/shard_map/ppermute | solution.py:190
  0.5 2.8 %collective-permute-start = (s32[8,128]{1,0:T(8,128)}, s32[8,128]{1,0:T(8,128)S(1)}, u32[]{:S(2)}, u32[]{:S(2)}) collective-permute-start(s32[8,128]{1,0:T(8,128)} %bitcast.10), channel_id=1, source_target_pairs={{0,1},{1,0},{2,3},{3,2},{4,5},{5,4},{6,7},{7,6},{8,9},{9,8},{10,11... | collective-permute-start | bytes 12296 | tf_op jit(solution)/shard_map/ppermute | solution.py:190
  0.6 1.0 %copy-start.1 = (bf16[128,2048]{1,0:T(8,128)(2,1)S(1)}, bf16[128,2048]{1,0:T(8,128)(2,1)}, u32[]{:S(2)}) copy-start(bf16[128,2048]{1,0:T(8,128)(2,1)} %tokens.1) | copy-start | bytes 1572868
  1.6 0.7 %copy-start.2 = (s32[128,8]{0,1:T(8,128)S(1)}, s32[128,8]{0,1:T(8,128)}, u32[]{:S(2)}) copy-start(s32[128,8]{0,1:T(8,128)} %param.7) | copy-start | bytes 12292
  4.2 10.0 %collective-permute-start.2 = (bf16[32,2048]{1,0:T(8,128)(2,1)S(1)}, bf16[32,2048]{1,0:T(8,128)(2,1)S(1)}, u32[]{:S(2)}, u32[]{:S(2)}) collective-permute-start(bf16[32,2048]{1,0:T(8,128)(2,1)S(1)} %get-tuple-element.37), channel_id=1, source_target_pairs={{0,4},{4,8},{8,12},{12,0},{1,5},{5,9},{9,13},{13,1},{2,6},{6,10},{... | collective-permute-start | bytes 393224 | tf_op jit(solution)/shard_map/ppermute | solution.py:190
  7.3 11.4 %collective-permute-start.3 = (bf16[32,2048]{1,0:T(8,128)(2,1)S(1)}, bf16[32,2048]{1,0:T(8,128)(2,1)S(1)}, u32[]{:S(2)}, u32[]{:S(2)}) collective-permute-start(bf16[32,2048]{1,0:T(8,128)(2,1)S(1)} %get-tuple-element.41), channel_id=1, source_target_pairs={{0,8},{4,12},{8,0},{12,4},{1,9},{5,13},{9,1},{13,5},{2,10},{6,14},... | collective-permute-start | bytes 393224 | tf_op jit(solution)/shard_map/ppermute | solution.py:190
  9.9 10.3 %collective-permute-start.4 = (bf16[32,2048]{1,0:T(8,128)(2,1)S(1)}, bf16[32,2048]{1,0:T(8,128)(2,1)S(1)}, u32[]{:S(2)}, u32[]{:S(2)}) collective-permute-start(bf16[32,2048]{1,0:T(8,128)(2,1)S(1)} %get-tuple-element.42), channel_id=1, source_target_pairs={{0,12},{4,0},{8,4},{12,8},{1,13},{5,1},{9,5},{13,9},{2,14},{6,2},{... | collective-permute-start | bytes 393224 | tf_op jit(solution)/shard_map/ppermute | solution.py:190
  11.2 13.8 %collective-permute-start.5 = (bf16[32,2048]{1,0:T(8,128)(2,1)S(1)}, bf16[32,2048]{1,0:T(8,128)(2,1)S(1)}, u32[]{:S(2)}, u32[]{:S(2)}) collective-permute-start(bf16[32,2048]{1,0:T(8,128)(2,1)S(1)} %get-tuple-element.38.after_ref.refs_0_), channel_id=1, source_target_pairs={{0,2},{2,0},{1,3},{3,1},{4,6},{6,4},{5,7},{7,5},{8,10},{10,8},{9,1... | collective-permute-start | bytes 393224 | tf_op jit(solution)/shard_map/ppermute | solution.py:190
  12.7 0.7 %copy-start.3 = (s32[128,8]{0,1:T(8,128)S(1)}, s32[128,8]{0,1:T(8,128)}, u32[]{:S(2)}) copy-start(s32[128,8]{0,1:T(8,128)} %param.8) | copy-start | bytes 12292
  14.2 10.9 %collective-permute-start.6 = (bf16[32,2048]{1,0:T(8,128)(2,1)S(1)}, bf16[32,2048]{1,0:T(8,128)(2,1)S(1)}, u32[]{:S(2)}, u32[]{:S(2)}) collective-permute-start(bf16[32,2048]{1,0:T(8,128)(2,1)S(1)} %collective-permute-done.2.refs_1_), channel_id=1, source_target_pairs={{0,2},{2,0},{1,3},{3,1},{4,6},{6,4},{5,7},{7,5},{8,10},{10,8},{9,1... | collective-permute-start | bytes 393224 | tf_op jit(solution)/shard_map/ppermute | solution.py:190
  18.7 6.4 %collective-permute-start.7 = (bf16[32,2048]{1,0:T(8,128)(2,1)S(1)}, bf16[32,2048]{1,0:T(8,128)(2,1)S(1)}, u32[]{:S(2)}, u32[]{:S(2)}) collective-permute-start(bf16[32,2048]{1,0:T(8,128)(2,1)S(1)} %collective-permute-done.3.refs_2_), channel_id=1, source_target_pairs={{0,2},{2,0},{1,3},{3,1},{4,6},{6,4},{5,7},{7,5},{8,10},{10,8},{9,1... | collective-permute-start | bytes 393224 | tf_op jit(solution)/shard_map/ppermute | solution.py:190
  20.2 6.6 %collective-permute-start.8 = (bf16[32,2048]{1,0:T(8,128)(2,1)S(1)}, bf16[32,2048]{1,0:T(8,128)(2,1)S(1)}, u32[]{:S(2)}, u32[]{:S(2)}) collective-permute-start(bf16[32,2048]{1,0:T(8,128)(2,1)S(1)} %collective-permute-done.4.refs_3_), channel_id=1, source_target_pairs={{0,2},{2,0},{1,3},{3,1},{4,6},{6,4},{5,7},{7,5},{8,10},{10,8},{9,1... | collective-permute-start | bytes 393224 | tf_op jit(solution)/shard_map/ppermute | solution.py:190
  20.7 6.1 %copy-start = (bf16[1,512,4096]{2,1,0:T(8,128)(2,1)S(1)}, bf16[1,512,4096]{2,1,0:T(8,128)(2,1)}, u32[]{:S(2)}) copy-start(bf16[1,512,4096]{2,1,0:T(8,128)(2,1)} %param.11) | copy-start | bytes 12582916
  28.5 8.9 %collective-permute-start.11 = (bf16[32,2048]{1,0:T(8,128)(2,1)S(1)}, bf16[32,2048]{1,0:T(8,128)(2,1)S(1)}, u32[]{:S(2)}, u32[]{:S(2)}) collective-permute-start(bf16[32,2048]{1,0:T(8,128)(2,1)S(1)} %get-tuple-element.52), channel_id=1, source_target_pairs={{0,2},{2,0},{1,3},{3,1},{4,6},{6,4},{5,7},{7,5},{8,10},{10,8},{9,1... | collective-permute-start | bytes 393224 | tf_op jit(solution)/shard_map/ppermute | solution.py:190
  30.0 15.1 %collective-permute-start.10 = (bf16[32,2048]{1,0:T(8,128)(2,1)S(1)}, bf16[32,2048]{1,0:T(8,128)(2,1)S(1)}, u32[]{:S(2)}, u32[]{:S(2)}) collective-permute-start(bf16[32,2048]{1,0:T(8,128)(2,1)S(1)} %get-tuple-element.49), channel_id=1, source_target_pairs={{0,14},{2,12},{4,2},{6,0},{8,6},{10,4},{12,10},{14,8},{1,15},{3,13... | collective-permute-start | bytes 393224 | tf_op jit(solution)/shard_map/ppermute | solution.py:196
  33.6 7.1 %collective-permute-start.13 = (bf16[32,2048]{1,0:T(8,128)(2,1)S(1)}, bf16[32,2048]{1,0:T(8,128)(2,1)S(1)}, u32[]{:S(2)}, u32[]{:S(2)}) collective-permute-start(bf16[32,2048]{1,0:T(8,128)(2,1)S(1)} %get-tuple-element.59), channel_id=1, source_target_pairs={{0,2},{2,0},{1,3},{3,1},{4,6},{6,4},{5,7},{7,5},{8,10},{10,8},{9,1... | collective-permute-start | bytes 393224 | tf_op jit(solution)/shard_map/ppermute | solution.py:190
  36.0 9.1 %collective-permute-start.9 = (bf16[32,2048]{1,0:T(8,128)(2,1)S(1)}, bf16[32,2048]{1,0:T(8,128)(2,1)S(1)}, u32[]{:S(2)}, u32[]{:S(2)}) collective-permute-start(bf16[32,2048]{1,0:T(8,128)(2,1)S(1)} %get-tuple-element.48), channel_id=1, source_target_pairs={{0,12},{2,14},{4,0},{6,2},{8,4},{10,6},{12,8},{14,10},{1,13},{3,15... | collective-permute-start | bytes 393224 | tf_op jit(solution)/shard_map/ppermute | solution.py:196
  37.4 7.6 %collective-permute-start.12 = (bf16[32,2048]{1,0:T(8,128)(2,1)S(1)}, bf16[32,2048]{1,0:T(8,128)(2,1)S(1)}, u32[]{:S(2)}, u32[]{:S(2)}) collective-permute-start(bf16[32,2048]{1,0:T(8,128)(2,1)S(1)} %get-tuple-element.54), channel_id=1, source_target_pairs={{0,2},{2,0},{1,3},{3,1},{4,6},{6,4},{5,7},{7,5},{8,10},{10,8},{9,1... | collective-permute-start | bytes 393224 | tf_op jit(solution)/shard_map/ppermute | solution.py:190
  38.0 7.1 %collective-permute-start.15 = (bf16[32,2048]{1,0:T(8,128)(2,1)S(1)}, bf16[32,2048]{1,0:T(8,128)(2,1)S(1)}, u32[]{:S(2)}, u32[]{:S(2)}) collective-permute-start(bf16[32,2048]{1,0:T(8,128)(2,1)S(1)} %add_convert_fusion.2), channel_id=1, source_target_pairs={{0,4},{4,8},{8,12},{12,0},{1,5},{5,9},{9,13},{13,1},{2,6},{6,10},{... | collective-permute-start | bytes 393224 | tf_op jit(solution)/shard_map/ppermute | solution.py:190
  40.7 7.6 %collective-permute-start.14 = (bf16[32,2048]{1,0:T(8,128)(2,1)S(1)}, bf16[32,2048]{1,0:T(8,128)(2,1)S(1)}, u32[]{:S(2)}, u32[]{:S(2)}) collective-permute-start(bf16[32,2048]{1,0:T(8,128)(2,1)S(1)} %add_convert_fusion), channel_id=1, source_target_pairs={{0,8},{4,12},{8,0},{12,4},{1,9},{5,13},{9,1},{13,5},{2,10},{6,14},... | collective-permute-start | bytes 393224 | tf_op jit(solution)/shard_map/ppermute | solution.py:190
  45.1 3.3 %collective-permute-start.19 = (bf16[16,2048]{1,0:T(8,128)(2,1)S(1)}, bf16[16,2048]{1,0:T(8,128)(2,1)S(1)}, u32[]{:S(2)}, u32[]{:S(2)}) collective-permute-start(bf16[16,2048]{1,0:T(8,128)(2,1)S(1)} %slice.21), channel_id=1, source_target_pairs={{0,1},{1,0},{2,3},{3,2},{4,5},{5,4},{6,7},{7,6},{8,9},{9,8},{10,11... | collective-permute-start | bytes 196616 | tf_op jit(solution)/shard_map/ppermute | solution.py:190
  45.2 3.2 %collective-permute-start.17 = (bf16[16,2048]{1,0:T(8,128)(2,1)S(1)}, bf16[16,2048]{1,0:T(8,128)(2,1)S(1)}, u32[]{:S(2)}, u32[]{:S(2)}) collective-permute-start(bf16[16,2048]{1,0:T(8,128)(2,1)S(1)} %add_convert_fusion.3), channel_id=1, source_target_pairs={{0,1},{1,0},{2,3},{3,2},{4,5},{5,4},{6,7},{7,6},{8,9},{9,8},{10,11... | collective-permute-start | bytes 196616 | tf_op jit(solution)/shard_map/ppermute | solution.py:190
  45.8 2.6 %collective-permute-start.16 = (bf16[16,2048]{1,0:T(8,128)(2,1)S(1)}, bf16[16,2048]{1,0:T(8,128)(2,1)S(1)}, u32[]{:S(2)}, u32[]{:S(2)}) collective-permute-start(bf16[16,2048]{1,0:T(8,128)(2,1)S(1)} %slice.15), channel_id=1, source_target_pairs={{0,1},{1,0},{2,3},{3,2},{4,5},{5,4},{6,7},{7,6},{8,9},{9,8},{10,11... | collective-permute-start | bytes 196616 | tf_op jit(solution)/shard_map/ppermute | solution.py:190
  48.4 1.3 %collective-permute-start.18 = (bf16[16,2048]{1,0:T(8,128)(2,1)S(1)}, bf16[16,2048]{1,0:T(8,128)(2,1)S(1)}, u32[]{:S(2)}, u32[]{:S(2)}) collective-permute-start(bf16[16,2048]{1,0:T(8,128)(2,1)S(1)} %slice.20), channel_id=1, source_target_pairs={{0,1},{1,0},{2,3},{3,2},{4,5},{5,4},{6,7},{7,6},{8,9},{9,8},{10,11... | collective-permute-start | bytes 196616 | tf_op jit(solution)/shard_map/ppermute | solution.py:190

commit v4 on v3

--- a/solution.py
+++ b/solution.py
@@ -47,22 +47,26 @@
     return jnp.where((slots[row : row + 1] == slot) & (hits[row : row + 1] > 0), 1.0, 0.0)
 
 
-def select(pos_ref, routes, tokens, outs, n_pool, n_pair, u):
+def select(pos_ref, routes, tokens, outs, n_pool, n_pair, u, copy=None):
     pool, pair = pos_ref[0], pos_ref[1]
     experts = [lax.rem(pool + s, n_pool) * n_pair + pair for s in range(n_pool)]
     hits, slots = picks(routes[...], experts)
     sel = jnp.concatenate([one_hot(hits, slots, s) for s in range(n_pool)], axis=0)
+    if copy is not None:
+        copy.wait()
     rows = jnp.dot(sel.astype(BF16), tokens[...], preferred_element_type=F32).astype(BF16)
     for s in range(n_pool):
         outs[s][u * CAP : (u + 1) * CAP, :] = rows[s * CAP : (s + 1) * CAP]
 
 
 def select_own_kernel(n_pool, n_pair, pos_ref, routes, tokens, *refs):
-    outs, held, sem = refs[:n_pool], refs[n_pool], refs[n_pool + 1]
-    copy = pltpu.make_async_copy(tokens, held, sem)
-    copy.start()
-    copy.wait()
-    select(pos_ref, routes, held, outs, n_pool, n_pair, 0)
+    outs, held, held_routes, sems = refs[:n_pool], refs[n_pool], refs[n_pool + 1], refs[n_pool + 2]
+    first = pltpu.make_async_copy(routes, held_routes, sems.at[0])
+    second = pltpu.make_async_copy(tokens, held, sems.at[1])
+    first.start()
+    second.start()
+    first.wait()
+    select(pos_ref, held_routes, held, outs, n_pool, n_pair, 0, second)
 
 
 def select_other_kernel(n_pool, n_pair, pos_ref, *refs):
@@ -211,7 +215,7 @@
     routes_t, weights_t = routes.T, gate_weights.T
     rows = n_pair * CAP
     small = n_pool == 4 and n_tp == 2
-    direct = [1] if small else []
+    direct = []
 
     def shape(r, c, t=BF16):
         return jax.ShapeDtypeStruct((r, c), t)
@@ -222,10 +226,14 @@
         functools.partial(select_own_kernel, n_pool, n_pair),
         "select_own",
         [shape(rows, width)] * n_pool,
-        [SMEM, VMEM, HBM],
-        (pos, routes_t, tokens),
+        [SMEM, HBM, HBM],
+        (pos, pltpu.with_memory_space_constraint(routes_t, pltpu.HBM), pltpu.with_memory_space_constraint(tokens, pltpu.HBM)),
         2 * 2 * streams * width,
-        scratch=[pltpu.VMEM((streams, width), BF16), pltpu.SemaphoreType.DMA],
+        scratch=[
+            pltpu.VMEM((streams, width), BF16),
+            pltpu.VMEM(routes_t.shape, routes.dtype),
+            pltpu.SemaphoreType.DMA((2,)),
+        ],
     )
     leaving = call(
         functools.partial(select_other_kernel, n_pool, n_pair),
@@ -247,8 +255,10 @@
         4 * 10 * streams * slots,
     )
 
-    near = [turn(leaving[s], "pool", s) if s else leaving[0] for s in range(n_pool)]
-    first = 1 if n_pool > 1 else 0
+    near = [leaving[0]] * n_pool
+    for s in [3, 2, 1] if small else range(1, n_pool):
+        near[s] = turn(leaving[s], "pool", s)
+    first = 3 if small else 0
     near[first], mixing = lax.optimization_barrier((near[first], mixing))
     far = [[turn(b, "tp", k) for b in near] for k in range(1, n_tp)]
     tiles = 4 if width % 1024 == 0 else 1
@@ -286,17 +296,16 @@
     )
 
     home = [None] * n_pool
-    for s in [2, 1, 3, 0] if small else range(n_pool):
+    totals = [None] * n_pool
+    for s in [2, 3, 1, 0] if small else range(n_pool):
         if s in direct:
             home[s] = [cross(kept[s], -s, 0)] + [cross(sent[k - 1][s], -s, k) for k in range(1, n_tp)]
         else:
+            if small and s == 0:
+                sent[0][0], *_ = lax.optimization_barrier((sent[0][0], totals[2], totals[3]))
             come = [turn(sent[k - 1][s], "tp", k) for k in range(1, n_tp)]
-            total = add([kept[s]] + come)
-            if small and s == 3:
-                total, sent[0][0] = lax.optimization_barrier((total, sent[0][0]))
-            home[s] = [turn(total, "pool", -s) if s else total]
-    if small:
-        home[1], home[0] = lax.optimization_barrier((home[1], home[0]))
+            totals[s] = add([kept[s]] + come)
+            home[s] = [turn(totals[s], "pool", -s) if s else totals[s]]
     layout, parts = [], []
     for s in range(n_pool):
         layout.append((len(home[s]), 0))

time: 50.9 us -> 48.1 us (0.945)
  starting transfers between devices: 25 us -> 19.9 us
  waiting for transfers between devices: 12.2 us -> 14.3 us
  Pallas kernels: 10.7 us -> 11.6 us
  local copies, waits for them, and re-layouts: 2.44 us -> 1.69 us
    ppermute x2 -> x0, starting transfers between devices: 3.86 us -> none  [cross(): return lax.ppermute(x, ('pool', 'tp'), pairs)]
    ppermute x18 -> x20, waiting for transfers between devices: 12.1 us -> 14.3 us  [turn(): return lax.ppermute(x, axis, [(i, (i + shift) % n) for i in range(n)])]
    ppermute x18 -> x20, starting transfers between devices: 21.2 us -> 19.9 us  [turn(): return lax.ppermute(x, axis, [(i, (i + shift) % n) for i in range(n)])]
    pallas_call x7, Pallas kernels: 10.7 us -> 11.6 us  [call(): pl.pallas_call(kernel, out_shape=outs, in_specs=in_specs, out_specs=[VMEM...]
    unnamed x8 -> x6, local copies, waits for them, and re-layouts: 2.42 us -> 1.66 us
  transfers between devices with their start and end apart: 20 -> 20, of which waited for: 6 -> 11; matrix products, arithmetic and copies ran while one was open for 0% -> 0% of each run, Pallas kernels for 14% -> 17%
where the time goes in v4:
time: 48.1 us; the launch traced here: 47.9 us
  starting transfers between devices  19.9 us (41%)
  waiting for transfers between devices  14.3 us (30%)
  Pallas kernels  11.6 us (24%)
  local copies, waits for them, and re-layouts  1.69 us (4%)
    ppermute x20, starting transfers between devices, turn(): return lax.ppermute(x, axis, [(i, (i + shift) % n) for i in range(n)])  19.9 us
    ppermute x20, waiting for transfers between devices, turn(): return lax.ppermute(x, axis, [(i, (i + shift) % n) for i in range(n)])  14.3 us
    pallas_call x7, Pallas kernels, call(): pl.pallas_call(kernel, out_shape=outs, in_specs=in_specs, out_specs=[VMEM...  11.6 us
    unnamed x6, local copies, waits for them, and re-layouts  1.66 us
  transfers between devices with their start and end apart: 20, of which 11 were waited for; matrix products, arithmetic and copies ran while one was open for 0% of the time, Pallas kernels for 17%

profile of v4, /device:TPU:0, one launch (start us, length us, event | category | flops | bytes accessed | tf_op | source)
XLA Modules:
  0.0 47.9 jit_solution(16007084301369302623)
XLA Ops:
  0.6 1.8 %select_own.1 = (bf16[32,2048]{1,0:T(8,128)(2,1)S(1)}, bf16[32,2048]{1,0:T(8,128)(2,1)S(1)}, bf16[32,2048]{1,0:T(8,128)(2,1)S(1)}, bf16[32,2048]{1,0:T(8,128)(2,1)S(1)}) custom-call(s32[3]{0:T(128)S(1)} %pad_add_fusion.pos_ref, s32[8,128]{1,0:T(8,128)} %bitcast.11, bf16[128,2048]{1,0:T(8,128)(2,1)} %tokens.1), custom_call_target="tpu_custom_call" | custom-call | bytes 1048576 | tf_op jit(solution)/shard_map/select_own/pallas_call | solution.py:18
  2.5 0.9 %select_other.1 = (bf16[32,2048]{1,0:T(8,128)(2,1)S(1)}, bf16[32,2048]{1,0:T(8,128)(2,1)S(1)}, bf16[32,2048]{1,0:T(8,128)(2,1)S(1)}, bf16[32,2048]{1,0:T(8,128)(2,1)S(1)}) custom-call(s32[3]{0:T(128)S(1)} %pad_add_fusion.pos_ref, s32[8,128]{1,0:T(8,128)S(1)} %collective-permute-done.refs_0_, ...), custom_call_target="tpu_custom_call", output_to_operand_aliasing={{0}: (3, {}), {1}: (4, {}), {2}: (5, {}), {3}: (6, {})} | custom-call | bytes 1048576 | tf_op jit(solution)/shard_map/select_other/pallas_call | solution.py:18
  3.4 5.1 %collective-permute-start.2 = (bf16[32,2048]{1,0:T(8,128)(2,1)S(1)}, bf16[32,2048]{1,0:T(8,128)(2,1)S(1)}, u32[]{:S(2)}, u32[]{:S(2)}) collective-permute-start(bf16[32,2048]{1,0:T(8,128)(2,1)S(1)} %get-tuple-element.33), channel_id=1, source_target_pairs={{0,12},{4,0},{8,4},{12,8},{1,13},{5,1},{9,5},{13,9},{2,14},{6,2},{... | collective-permute-start | bytes 393224 | tf_op jit(solution)/shard_map/ppermute | solution.py:194
  8.5 1.0 %collective-permute-start.4 = (bf16[32,2048]{1,0:T(8,128)(2,1)S(1)}, bf16[32,2048]{1,0:T(8,128)(2,1)S(1)}, u32[]{:S(2)}, u32[]{:S(2)}) collective-permute-start(bf16[32,2048]{1,0:T(8,128)(2,1)S(1)} %get-tuple-element.37), channel_id=1, source_target_pairs={{0,8},{4,12},{8,0},{12,4},{1,9},{5,13},{9,1},{13,5},{2,10},{6,14},... | collective-permute-start | bytes 393224 | tf_op jit(solution)/shard_map/ppermute | solution.py:194
  9.5 1.5 %collective-permute-start.5 = (bf16[32,2048]{1,0:T(8,128)(2,1)S(1)}, bf16[32,2048]{1,0:T(8,128)(2,1)S(1)}, u32[]{:S(2)}, u32[]{:S(2)}) collective-permute-start(bf16[32,2048]{1,0:T(8,128)(2,1)S(1)} %get-tuple-element.34.after_ref.refs_0_), channel_id=1, source_target_pairs={{0,2},{2,0},{1,3},{3,1},{4,6},{6,4},{5,7},{7,5},{8,10},{10,8},{9,1... | collective-permute-start | bytes 393224 | tf_op jit(solution)/shard_map/ppermute | solution.py:194
  11.0 0.7 %copy-done.1 = s32[128,8]{0,1:T(8,128)S(1)} copy-done((s32[128,8]{0,1:T(8,128)S(1)}, s32[128,8]{0,1:T(8,128)}, u32[]{:S(2)}) %copy-start.1) | copy-done | bytes 4120
  12.4 0.8 %mixing.1.mixing_ref = bf16[128,256]{1,0:T(8,128)(2,1)S(1)} custom-call(s32[3]{0:T(128)S(1)} %pad_add_fusion.pos_ref, bf16[32,2048]{1,0:T(8,128)(2,1)S(1)} %get-tuple-element.34.after_ref.refs_0_, s32[8,128]{1,0:T(8,128)S(1)} %bitcast.12, s32[8,128]{1,0:T(8,128)S(1)} %bitcast.13), custom_call_target="tpu_custom_call" | custom-call | bytes 655360 | tf_op jit(solution)/shard_map/mixing/pallas_call | solution.py:18
  13.2 0.7 %collective-permute-start.8 = (bf16[32,2048]{1,0:T(8,128)(2,1)S(1)}, bf16[32,2048]{1,0:T(8,128)(2,1)S(1)}, u32[]{:S(2)}, u32[]{:S(2)}) collective-permute-start(bf16[32,2048]{1,0:T(8,128)(2,1)S(1)} %collective-permute-done.2.refs_3_), channel_id=1, source_target_pairs={{0,2},{2,0},{1,3},{3,1},{4,6},{6,4},{5,7},{7,5},{8,10},{10,8},{9,1... | collective-permute-start | bytes 393224 | tf_op jit(solution)/shard_map/ppermute | solution.py:194
  13.9 2.8 %collective-permute-done.3.refs_1_ = bf16[32,2048]{1,0:T(8,128)(2,1)S(1)} collective-permute-done((bf16[32,2048]{1,0:T(8,128)(2,1)S(1)}, bf16[32,2048]{1,0:T(8,128)(2,1)S(1)}, u32[]{:S(2)}, u32[]{:S(2)}) %collective-permute-start.3) | collective-permute-done | bytes 131104 | tf_op jit(solution)/shard_map/ppermute | solution.py:194
  16.7 1.5 %collective-permute-start.6 = (bf16[32,2048]{1,0:T(8,128)(2,1)S(1)}, bf16[32,2048]{1,0:T(8,128)(2,1)S(1)}, u32[]{:S(2)}, u32[]{:S(2)}) collective-permute-start(bf16[32,2048]{1,0:T(8,128)(2,1)S(1)} %collective-permute-done.3.refs_1_), channel_id=1, source_target_pairs={{0,2},{2,0},{1,3},{3,1},{4,6},{6,4},{5,7},{7,5},{8,10},{10,8},{9,1... | collective-permute-start | bytes 393224 | tf_op jit(solution)/shard_map/ppermute | solution.py:194
  18.2 1.9 %collective-permute-done.4.refs_2_ = bf16[32,2048]{1,0:T(8,128)(2,1)S(1)} collective-permute-done((bf16[32,2048]{1,0:T(8,128)(2,1)S(1)}, bf16[32,2048]{1,0:T(8,128)(2,1)S(1)}, u32[]{:S(2)}, u32[]{:S(2)}) %collective-permute-start.4) | collective-permute-done | bytes 131104 | tf_op jit(solution)/shard_map/ppermute | solution.py:194
  20.1 1.5 %collective-permute-start.7 = (bf16[32,2048]{1,0:T(8,128)(2,1)S(1)}, bf16[32,2048]{1,0:T(8,128)(2,1)S(1)}, u32[]{:S(2)}, u32[]{:S(2)}) collective-permute-start(bf16[32,2048]{1,0:T(8,128)(2,1)S(1)} %collective-permute-done.4.refs_2_), channel_id=1, source_target_pairs={{0,2},{2,0},{1,3},{3,1},{4,6},{6,4},{5,7},{7,5},{8,10},{10,8},{9,1... | collective-permute-start | bytes 393224 | tf_op jit(solution)/shard_map/ppermute | solution.py:194
  21.6 4.3 %near.1 = (f32[128,512]{1,0:T(8,128)S(1)}, f32[128,512]{1,0:T(8,128)S(1)}, bf16[2048,512]{1,0:T(8,128)(2,1)S(1)}, bf16[2048,512]{1,0:T(8,128)(2,1)S(1)}) custom-call(s32[3]{0:T(128)S(1)} %pad_add_fusion.pos_ref, bf16[4096,512]{1,0:T(8,128)(2,1)} %bitcast.14, bf16[4096,512]{1,0:T(8,128)(2,1)} %bitcast.15, ...), custom_call_target="tpu_custom_call" | custom-call | flops 536870912 | bytes 16777216 | tf_op jit(solution)/shard_map/near/pallas_call | solution.py:18
  26.3 1.6 %far.1 = (bf16[128,512]{1,0:T(8,128)(2,1)S(1)}, bf16[32,2048]{1,0:T(8,128)(2,1)S(1)}, bf16[32,2048]{1,0:T(8,128)(2,1)S(1)}, bf16[32,2048]{1,0:T(8,128)(2,1)S(1)}, bf16[32,2048]{1,0:T(8,128)(2,1)S(1)}) custom-call(s32[3]{0:T(128)S(1)} %pad_add_fusion.pos_ref, bf16[2048,512]{1,0:T(8,128)(2,1)S(1)} %get-tuple-element.39.gate_ref, ...), custom_call_target="tpu_custom_call" | custom-call | flops 805306368 | bytes 8388608 | tf_op jit(solution)/shard_map/far/pallas_call | solution.py:18
  28.5 1.5 %collective-permute-start.10 = (bf16[32,2048]{1,0:T(8,128)(2,1)S(1)}, bf16[32,2048]{1,0:T(8,128)(2,1)S(1)}, u32[]{:S(2)}, u32[]{:S(2)}) collective-permute-start(bf16[32,2048]{1,0:T(8,128)(2,1)S(1)} %get-tuple-element.49), channel_id=1, source_target_pairs={{0,2},{2,0},{1,3},{3,1},{4,6},{6,4},{5,7},{7,5},{8,10},{10,8},{9,1... | collective-permute-start | bytes 393224 | tf_op jit(solution)/shard_map/ppermute | solution.py:194
  30.6 1.0 %keep.1 = (bf16[32,2048]{1,0:T(8,128)(2,1)S(1)}, bf16[32,2048]{1,0:T(8,128)(2,1)S(1)}, bf16[32,2048]{1,0:T(8,128)(2,1)S(1)}, bf16[32,2048]{1,0:T(8,128)(2,1)S(1)}) custom-call(s32[3]{0:T(128)S(1)} %pad_add_fusion.pos_ref, bf16[512,4096]{1,0:T(8,128)(2,1)S(1)} %bitcast.9, bf16[128,512]{1,0:T(8,128)(2,1)S(1)} %get-tuple-element.43.hidden_ref), custom_call_target="tpu_custom_call" | custom-call | flops 268435456 | bytes 2097152 | tf_op jit(solution)/shard_map/keep/pallas_call | solution.py:18
  31.6 2.9 %collective-permute-done.9 = bf16[32,2048]{1,0:T(8,128)(2,1)S(1)} collective-permute-done((bf16[32,2048]{1,0:T(8,128)(2,1)S(1)}, bf16[32,2048]{1,0:T(8,128)(2,1)S(1)}, u32[]{:S(2)}, u32[]{:S(2)}) %collective-permute-start.9) | collective-permute-done | bytes 131104 | tf_op jit(solution)/shard_map/ppermute | solution.py:194
  35.0 1.8 %collective-permute-done.10 = bf16[32,2048]{1,0:T(8,128)(2,1)S(1)} collective-permute-done((bf16[32,2048]{1,0:T(8,128)(2,1)S(1)}, bf16[32,2048]{1,0:T(8,128)(2,1)S(1)}, u32[]{:S(2)}, u32[]{:S(2)}) %collective-permute-start.10) | collective-permute-done | bytes 131104 | tf_op jit(solution)/shard_map/ppermute | solution.py:194
  37.4 1.2 %collective-permute-start.11 = (bf16[32,2048]{1,0:T(8,128)(2,1)S(1)}, bf16[32,2048]{1,0:T(8,128)(2,1)S(1)}, u32[]{:S(2)}, u32[]{:S(2)}) collective-permute-start(bf16[32,2048]{1,0:T(8,128)(2,1)S(1)} %get-tuple-element.50), channel_id=1, source_target_pairs={{0,2},{2,0},{1,3},{3,1},{4,6},{6,4},{5,7},{7,5},{8,10},{10,8},{9,1... | collective-permute-start | bytes 393224 | tf_op jit(solution)/shard_map/ppermute | solution.py:194
  39.3 2.4 %collective-permute-start.13 = (bf16[32,2048]{1,0:T(8,128)(2,1)S(1)}, bf16[32,2048]{1,0:T(8,128)(2,1)S(1)}, u32[]{:S(2)}, u32[]{:S(2)}) collective-permute-start(bf16[32,2048]{1,0:T(8,128)(2,1)S(1)} %add_convert_fusion), channel_id=1, source_target_pairs={{0,12},{4,0},{8,4},{12,8},{1,13},{5,1},{9,5},{13,9},{2,14},{6,2},{... | collective-permute-start | bytes 393224 | tf_op jit(solution)/shard_map/ppermute | solution.py:194
  41.7 0.7 %collective-permute-done.11 = bf16[32,2048]{1,0:T(8,128)(2,1)S(1)} collective-permute-done((bf16[32,2048]{1,0:T(8,128)(2,1)S(1)}, bf16[32,2048]{1,0:T(8,128)(2,1)S(1)}, u32[]{:S(2)}, u32[]{:S(2)}) %collective-permute-start.11) | collective-permute-done | bytes 131104 | tf_op jit(solution)/shard_map/ppermute | solution.py:194
  42.5 1.8 %collective-permute-done.14.refs_2_ = bf16[32,2048]{1,0:T(8,128)(2,1)S(1)} collective-permute-done((bf16[32,2048]{1,0:T(8,128)(2,1)S(1)}, bf16[32,2048]{1,0:T(8,128)(2,1)S(1)}, u32[]{:S(2)}, u32[]{:S(2)}) %collective-permute-start.14) | collective-permute-done | bytes 131104 | tf_op jit(solution)/shard_map/ppermute | solution.py:194
  45.8 0.9 %collective-permute-done.17.refs_5_ = bf16[16,2048]{1,0:T(8,128)(2,1)S(1)} collective-permute-done((bf16[16,2048]{1,0:T(8,128)(2,1)S(1)}, bf16[16,2048]{1,0:T(8,128)(2,1)S(1)}, u32[]{:S(2)}, u32[]{:S(2)}) %collective-permute-start.17) | collective-permute-done | bytes 65568 | tf_op jit(solution)/shard_map/ppermute | solution.py:194
  46.8 1.1 %mix.1 = bf16[128,2048]{1,0:T(8,128)(2,1)} custom-call(bf16[128,256]{1,0:T(8,128)(2,1)S(1)} %mixing.1.mixing_ref, bf16[32,2048]{1,0:T(8,128)(2,1)S(1)} %add_convert_fusion.1.refs_0_, bf16[32,2048]{1,0:T(8,128)(2,1)S(1)} %collective-permute-done.13.refs_1_, bf16[32,2048]{1,0:T(8,128)(2,1)S(1)} %collective-permute-done.14.refs_2_, ...), custom_call_target="tpu_custom_call" | custom-call | bytes 1572864 | tf_op jit(solution)/shard_map/mix/pallas_call | solution.py:18
  (38 shorter events, 6.1 us)
Async XLA Ops:
  0.0 2.5 %collective-permute-start.1 = (bf16[128,2048]{1,0:T(8,128)(2,1)}, bf16[128,2048]{1,0:T(8,128)(2,1)S(1)}, u32[]{:S(2)}, u32[]{:S(2)}) collective-permute-start(bf16[128,2048]{1,0:T(8,128)(2,1)} %tokens.1), channel_id=1, source_target_pairs={{0,1},{1,0},{2,3},{3,2},{4,5},{5,4},{6,7},{7,6},{8,9},{9,8},{10,11... | collective-permute-start | bytes 1572872 | tf_op jit(solution)/shard_map/ppermute | solution.py:194
  0.5 2.0 %collective-permute-start = (s32[8,128]{1,0:T(8,128)}, s32[8,128]{1,0:T(8,128)S(1)}, u32[]{:S(2)}, u32[]{:S(2)}) collective-permute-start(s32[8,128]{1,0:T(8,128)} %bitcast.10), channel_id=1, source_target_pairs={{0,1},{1,0},{2,3},{3,2},{4,5},{5,4},{6,7},{7,6},{8,9},{9,8},{10,11... | collective-permute-start | bytes 12296 | tf_op jit(solution)/shard_map/ppermute | solution.py:194
  3.4 9.8 %collective-permute-start.2 = (bf16[32,2048]{1,0:T(8,128)(2,1)S(1)}, bf16[32,2048]{1,0:T(8,128)(2,1)S(1)}, u32[]{:S(2)}, u32[]{:S(2)}) collective-permute-start(bf16[32,2048]{1,0:T(8,128)(2,1)S(1)} %get-tuple-element.33), channel_id=1, source_target_pairs={{0,12},{4,0},{8,4},{12,8},{1,13},{5,1},{9,5},{13,9},{2,14},{6,2},{... | collective-permute-start | bytes 393224 | tf_op jit(solution)/shard_map/ppermute | solution.py:194
  8.5 8.3 %collective-permute-start.3 = (bf16[32,2048]{1,0:T(8,128)(2,1)S(1)}, bf16[32,2048]{1,0:T(8,128)(2,1)S(1)}, u32[]{:S(2)}, u32[]{:S(2)}) collective-permute-start(bf16[32,2048]{1,0:T(8,128)(2,1)S(1)} %get-tuple-element.36), channel_id=1, source_target_pairs={{0,4},{4,8},{8,12},{12,0},{1,5},{5,9},{9,13},{13,1},{2,6},{6,10},{... | collective-permute-start | bytes 393224 | tf_op jit(solution)/shard_map/ppermute | solution.py:194
  8.5 11.6 %collective-permute-start.4 = (bf16[32,2048]{1,0:T(8,128)(2,1)S(1)}, bf16[32,2048]{1,0:T(8,128)(2,1)S(1)}, u32[]{:S(2)}, u32[]{:S(2)}) collective-permute-start(bf16[32,2048]{1,0:T(8,128)(2,1)S(1)} %get-tuple-element.37), channel_id=1, source_target_pairs={{0,8},{4,12},{8,0},{12,4},{1,9},{5,13},{9,1},{13,5},{2,10},{6,14},... | collective-permute-start | bytes 393224 | tf_op jit(solution)/shard_map/ppermute | solution.py:194
  9.5 16.4 %collective-permute-start.5 = (bf16[32,2048]{1,0:T(8,128)(2,1)S(1)}, bf16[32,2048]{1,0:T(8,128)(2,1)S(1)}, u32[]{:S(2)}, u32[]{:S(2)}) collective-permute-start(bf16[32,2048]{1,0:T(8,128)(2,1)S(1)} %get-tuple-element.34.after_ref.refs_0_), channel_id=1, source_target_pairs={{0,2},{2,0},{1,3},{3,1},{4,6},{6,4},{5,7},{7,5},{8,10},{10,8},{9,1... | collective-permute-start | bytes 393224 | tf_op jit(solution)/shard_map/ppermute | solution.py:194
  11.0 0.7 %copy-start.1 = (s32[128,8]{0,1:T(8,128)S(1)}, s32[128,8]{0,1:T(8,128)}, u32[]{:S(2)}) copy-start(s32[128,8]{0,1:T(8,128)} %param.7) | copy-start | bytes 12292
  11.7 0.7 %copy-start.2 = (s32[128,8]{0,1:T(8,128)S(1)}, s32[128,8]{0,1:T(8,128)}, u32[]{:S(2)}) copy-start(s32[128,8]{0,1:T(8,128)} %param.8) | copy-start | bytes 12292
  13.2 12.8 %collective-permute-start.8 = (bf16[32,2048]{1,0:T(8,128)(2,1)S(1)}, bf16[32,2048]{1,0:T(8,128)(2,1)S(1)}, u32[]{:S(2)}, u32[]{:S(2)}) collective-permute-start(bf16[32,2048]{1,0:T(8,128)(2,1)S(1)} %collective-permute-done.2.refs_3_), channel_id=1, source_target_pairs={{0,2},{2,0},{1,3},{3,1},{4,6},{6,4},{5,7},{7,5},{8,10},{10,8},{9,1... | collective-permute-start | bytes 393224 | tf_op jit(solution)/shard_map/ppermute | solution.py:194
  16.7 9.2 %collective-permute-start.6 = (bf16[32,2048]{1,0:T(8,128)(2,1)S(1)}, bf16[32,2048]{1,0:T(8,128)(2,1)S(1)}, u32[]{:S(2)}, u32[]{:S(2)}) collective-permute-start(bf16[32,2048]{1,0:T(8,128)(2,1)S(1)} %collective-permute-done.3.refs_1_), channel_id=1, source_target_pairs={{0,2},{2,0},{1,3},{3,1},{4,6},{6,4},{5,7},{7,5},{8,10},{10,8},{9,1... | collective-permute-start | bytes 393224 | tf_op jit(solution)/shard_map/ppermute | solution.py:194
  20.1 5.9 %collective-permute-start.7 = (bf16[32,2048]{1,0:T(8,128)(2,1)S(1)}, bf16[32,2048]{1,0:T(8,128)(2,1)S(1)}, u32[]{:S(2)}, u32[]{:S(2)}) collective-permute-start(bf16[32,2048]{1,0:T(8,128)(2,1)S(1)} %collective-permute-done.4.refs_2_), channel_id=1, source_target_pairs={{0,2},{2,0},{1,3},{3,1},{4,6},{6,4},{5,7},{7,5},{8,10},{10,8},{9,1... | collective-permute-start | bytes 393224 | tf_op jit(solution)/shard_map/ppermute | solution.py:194
  21.6 4.7 %copy-start = (bf16[1,512,4096]{2,1,0:T(8,128)(2,1)S(1)}, bf16[1,512,4096]{2,1,0:T(8,128)(2,1)}, u32[]{:S(2)}) copy-start(bf16[1,512,4096]{2,1,0:T(8,128)(2,1)} %param.11) | copy-start | bytes 12582916
  27.9 6.5 %collective-permute-start.9 = (bf16[32,2048]{1,0:T(8,128)(2,1)S(1)}, bf16[32,2048]{1,0:T(8,128)(2,1)S(1)}, u32[]{:S(2)}, u32[]{:S(2)}) collective-permute-start(bf16[32,2048]{1,0:T(8,128)(2,1)S(1)} %get-tuple-element.47), channel_id=1, source_target_pairs={{0,2},{2,0},{1,3},{3,1},{4,6},{6,4},{5,7},{7,5},{8,10},{10,8},{9,1... | collective-permute-start | bytes 393224 | tf_op jit(solution)/shard_map/ppermute | solution.py:194
  28.5 8.2 %collective-permute-start.10 = (bf16[32,2048]{1,0:T(8,128)(2,1)S(1)}, bf16[32,2048]{1,0:T(8,128)(2,1)S(1)}, u32[]{:S(2)}, u32[]{:S(2)}) collective-permute-start(bf16[32,2048]{1,0:T(8,128)(2,1)S(1)} %get-tuple-element.49), channel_id=1, source_target_pairs={{0,2},{2,0},{1,3},{3,1},{4,6},{6,4},{5,7},{7,5},{8,10},{10,8},{9,1... | collective-permute-start | bytes 393224 | tf_op jit(solution)/shard_map/ppermute | solution.py:194
  30.0 9.2 %collective-permute-start.12 = (bf16[32,2048]{1,0:T(8,128)(2,1)S(1)}, bf16[32,2048]{1,0:T(8,128)(2,1)S(1)}, u32[]{:S(2)}, u32[]{:S(2)}) collective-permute-start(bf16[32,2048]{1,0:T(8,128)(2,1)S(1)} %get-tuple-element.52), channel_id=1, source_target_pairs={{0,2},{2,0},{1,3},{3,1},{4,6},{6,4},{5,7},{7,5},{8,10},{10,8},{9,1... | collective-permute-start | bytes 393224 | tf_op jit(solution)/shard_map/ppermute | solution.py:194
  34.5 9.9 %collective-permute-start.14 = (bf16[32,2048]{1,0:T(8,128)(2,1)S(1)}, bf16[32,2048]{1,0:T(8,128)(2,1)S(1)}, u32[]{:S(2)}, u32[]{:S(2)}) collective-permute-start(bf16[32,2048]{1,0:T(8,128)(2,1)S(1)} %add_convert_fusion.3), channel_id=1, source_target_pairs={{0,8},{4,12},{8,0},{12,4},{1,9},{5,13},{9,1},{13,5},{2,10},{6,14},... | collective-permute-start | bytes 393224 | tf_op jit(solution)/shard_map/ppermute | solution.py:194
  36.8 7.6 %collective-permute-start.15 = (bf16[32,2048]{1,0:T(8,128)(2,1)S(1)}, bf16[32,2048]{1,0:T(8,128)(2,1)S(1)}, u32[]{:S(2)}, u32[]{:S(2)}) collective-permute-start(bf16[32,2048]{1,0:T(8,128)(2,1)S(1)} %add_convert_fusion.2), channel_id=1, source_target_pairs={{0,4},{4,8},{8,12},{12,0},{1,5},{5,9},{9,13},{13,1},{2,6},{6,10},{... | collective-permute-start | bytes 393224 | tf_op jit(solution)/shard_map/ppermute | solution.py:194
  37.4 5.0 %collective-permute-start.11 = (bf16[32,2048]{1,0:T(8,128)(2,1)S(1)}, bf16[32,2048]{1,0:T(8,128)(2,1)S(1)}, u32[]{:S(2)}, u32[]{:S(2)}) collective-permute-start(bf16[32,2048]{1,0:T(8,128)(2,1)S(1)} %get-tuple-element.50), channel_id=1, source_target_pairs={{0,2},{2,0},{1,3},{3,1},{4,6},{6,4},{5,7},{7,5},{8,10},{10,8},{9,1... | collective-permute-start | bytes 393224 | tf_op jit(solution)/shard_map/ppermute | solution.py:194
  39.3 6.3 %collective-permute-start.13 = (bf16[32,2048]{1,0:T(8,128)(2,1)S(1)}, bf16[32,2048]{1,0:T(8,128)(2,1)S(1)}, u32[]{:S(2)}, u32[]{:S(2)}) collective-permute-start(bf16[32,2048]{1,0:T(8,128)(2,1)S(1)} %add_convert_fusion), channel_id=1, source_target_pairs={{0,12},{4,0},{8,4},{12,8},{1,13},{5,1},{9,5},{13,9},{2,14},{6,2},{... | collective-permute-start | bytes 393224 | tf_op jit(solution)/shard_map/ppermute | solution.py:194
  42.4 3.1 %collective-permute-start.16 = (bf16[16,2048]{1,0:T(8,128)(2,1)S(1)}, bf16[16,2048]{1,0:T(8,128)(2,1)S(1)}, u32[]{:S(2)}, u32[]{:S(2)}) collective-permute-start(bf16[16,2048]{1,0:T(8,128)(2,1)S(1)} %slice.16), channel_id=1, source_target_pairs={{0,1},{1,0},{2,3},{3,2},{4,5},{5,4},{6,7},{7,6},{8,9},{9,8},{10,11... | collective-permute-start | bytes 196616 | tf_op jit(solution)/shard_map/ppermute | solution.py:194
  44.4 1.3 %collective-permute-start.18 = (bf16[16,2048]{1,0:T(8,128)(2,1)S(1)}, bf16[16,2048]{1,0:T(8,128)(2,1)S(1)}, u32[]{:S(2)}, u32[]{:S(2)}) collective-permute-start(bf16[16,2048]{1,0:T(8,128)(2,1)S(1)} %slice.18), channel_id=1, source_target_pairs={{0,1},{1,0},{2,3},{3,2},{4,5},{5,4},{6,7},{7,6},{8,9},{9,8},{10,11... | collective-permute-start | bytes 196616 | tf_op jit(solution)/shard_map/ppermute | solution.py:194
  44.4 1.5 %collective-permute-start.19 = (bf16[16,2048]{1,0:T(8,128)(2,1)S(1)}, bf16[16,2048]{1,0:T(8,128)(2,1)S(1)}, u32[]{:S(2)}, u32[]{:S(2)}) collective-permute-start(bf16[16,2048]{1,0:T(8,128)(2,1)S(1)} %slice.19), channel_id=1, source_target_pairs={{0,1},{1,0},{2,3},{3,2},{4,5},{5,4},{6,7},{7,6},{8,9},{9,8},{10,11... | collective-permute-start | bytes 196616 | tf_op jit(solution)/shard_map/ppermute | solution.py:194
  45.5 1.3 %collective-permute-start.17 = (bf16[16,2048]{1,0:T(8,128)(2,1)S(1)}, bf16[16,2048]{1,0:T(8,128)(2,1)S(1)}, u32[]{:S(2)}, u32[]{:S(2)}) collective-permute-start(bf16[16,2048]{1,0:T(8,128)(2,1)S(1)} %slice.17), channel_id=1, source_target_pairs={{0,1},{1,0},{2,3},{3,2},{4,5},{5,4},{6,7},{7,6},{8,9},{9,8},{10,11... | collective-permute-start | bytes 196616 | tf_op jit(solution)/shard_map/ppermute | solution.py:194

commit v5 on v4

--- a/solution.py
+++ b/solution.py
@@ -14,12 +14,12 @@
 BF16, F32 = jnp.bfloat16, jnp.float32
 
 
-def call(kernel, name, outs, in_specs, args, nbytes, flops=0, scratch=(), alias=None, vmem=24):
+def call(kernel, name, outs, in_specs, args, nbytes, flops=0, scratch=(), alias=None, vmem=24, to=VMEM):
     return pl.pallas_call(
         kernel,
         out_shape=outs,
         in_specs=in_specs,
-        out_specs=[VMEM] * len(outs),
+        out_specs=[to] * len(outs),
         scratch_shapes=scratch,
         input_output_aliases=alias or {},
         compiler_params=pltpu.CompilerParams(vmem_limit_bytes=vmem * 2**20),
@@ -176,17 +176,22 @@
     put(outs, jnp.dot(hidden_ref[...], down_ref[:, at], preferred_element_type=F32).astype(BF16))
 
 
-def mix_kernel(n_pool, n_pair, layout, mixing_ref, *refs):
-    parts, out = refs[:-1], refs[-1]
-    at, rows = 0, []
-    for n, first in layout:
-        total = parts[at][first : first + CAP, :].astype(F32)
-        for r in parts[at + 1 : at + n]:
-            total += r[first : first + CAP, :].astype(F32)
-        rows.append(total.astype(BF16))
-        at += n
-    rows = jnp.concatenate(rows + rows, axis=0)
-    out[...] = jnp.dot(mixing_ref[...], rows, preferred_element_type=F32).astype(BF16)
+def mix_kernel(tiles, mixing_ref, *refs):
+    parts, out, held, sems = refs[:-3], refs[-3], refs[-2], refs[-1]
+    half = mixing_ref.shape[1] // 2
+    high, low = mixing_ref[:, :half], mixing_ref[:, half:]
+    cut = held.shape[1] // tiles
+    copies = []
+    for j in range(tiles):
+        at = slice(j * cut, (j + 1) * cut)
+        rows = jnp.concatenate([r[:CAP, at] for r in parts], axis=0)
+        total = jnp.dot(high, rows, preferred_element_type=F32)
+        total += jnp.dot(low, rows, preferred_element_type=F32)
+        held[:, at] = total.astype(BF16)
+        copies.append(pltpu.make_async_copy(held.at[:, at], out.at[:, at], sems.at[j]))
+        copies[-1].start()
+    for c in copies:
+        c.wait()
 
 
 def turn(x, axis, shift):
@@ -295,6 +300,11 @@
         2 * slots * width * hidden_units,
     )
 
+    if small:
+        late = [0, 1, 3]
+        held, kept = lax.optimization_barrier(([sent[0][s] for s in late], kept))
+        for s, x in zip(late, held):
+            sent[0][s] = x
     home = [None] * n_pool
     totals = [None] * n_pool
     for s in [2, 3, 1, 0] if small else range(n_pool):
@@ -305,23 +315,20 @@
                 sent[0][0], *_ = lax.optimization_barrier((sent[0][0], totals[2], totals[3]))
             come = [turn(sent[k - 1][s], "tp", k) for k in range(1, n_tp)]
             totals[s] = add([kept[s]] + come)
-            home[s] = [turn(totals[s], "pool", -s) if s else totals[s]]
-    layout, parts = [], []
-    for s in range(n_pool):
-        layout.append((len(home[s]), 0))
-        parts += home[s]
+            home[s] = turn(totals[s], "pool", -s) if s else totals[s]
+    parts = [home[s] for s in range(n_pool)]
     for u in range(1, n_pair):
-        for s in range(n_pool):
-            part = add([h[u * CAP : (u + 1) * CAP] for h in home[s]])
-            layout.append((1, 0))
-            parts.append(turn(part, "pair", u))
+        parts += [turn(home[s][u * CAP : (u + 1) * CAP], "pair", u) for s in range(n_pool)]
+    tiles = 4 if width % 512 == 0 else 1
     (out,) = call(
-        functools.partial(mix_kernel, n_pool, n_pair, layout),
+        functools.partial(mix_kernel, tiles),
         "mix",
         [shape(streams, width)],
         [VMEM] * (1 + len(parts)),
         (mixing, *parts),
         2 * 3 * streams * width,
+        scratch=[pltpu.VMEM((streams, width), BF16), pltpu.SemaphoreType.DMA((tiles,))],
+        to=HBM,
     )
     return out
 

time: 48.1 us -> 47.9 us (level)
  transfers between devices with their start and end apart: 20 -> 20, of which waited for: 11 -> 10; matrix products, arithmetic and copies ran while one was open for 0% -> 0% of each run, Pallas kernels for 17% -> 17%
where the time goes in v5:
time: 47.9 us; the launch traced here: 47.7 us
  starting transfers between devices  20.1 us (42%)
  waiting for transfers between devices  13.9 us (29%)
  Pallas kernels  11.6 us (24%)
  local copies, waits for them, and re-layouts  1.69 us (4%)
    ppermute x20, starting transfers between devices, turn(): return lax.ppermute(x, axis, [(i, (i + shift) % n) for i in range(n)])  20.1 us
    ppermute x20, waiting for transfers between devices, turn(): return lax.ppermute(x, axis, [(i, (i + shift) % n) for i in range(n)])  13.9 us
    pallas_call x7, Pallas kernels, call(): pl.pallas_call(kernel, out_shape=outs, in_specs=in_specs, out_specs=[to]...  11.6 us
    unnamed x6, local copies, waits for them, and re-layouts  1.66 us
  transfers between devices with their start and end apart: 20, of which 10 were waited for; matrix products, arithmetic and copies ran while one was open for 0% of the time, Pallas kernels for 17%

profile of v5, /device:TPU:0, one launch (start us, length us, event | category | flops | bytes accessed | tf_op | source)
XLA Modules:
  0.0 47.7 jit_solution(13561004588299136679)
XLA Ops:
  0.6 1.8 %select_own.1 = (bf16[32,2048]{1,0:T(8,128)(2,1)S(1)}, bf16[32,2048]{1,0:T(8,128)(2,1)S(1)}, bf16[32,2048]{1,0:T(8,128)(2,1)S(1)}, bf16[32,2048]{1,0:T(8,128)(2,1)S(1)}) custom-call(s32[3]{0:T(128)S(1)} %pad_add_fusion.pos_ref, s32[8,128]{1,0:T(8,128)} %bitcast.11, bf16[128,2048]{1,0:T(8,128)(2,1)} %tokens.1), custom_call_target="tpu_custom_call" | custom-call | bytes 1048576 | tf_op jit(solution)/shard_map/select_own/pallas_call | solution.py:18
  2.5 0.9 %select_other.1 = (bf16[32,2048]{1,0:T(8,128)(2,1)S(1)}, bf16[32,2048]{1,0:T(8,128)(2,1)S(1)}, bf16[32,2048]{1,0:T(8,128)(2,1)S(1)}, bf16[32,2048]{1,0:T(8,128)(2,1)S(1)}) custom-call(s32[3]{0:T(128)S(1)} %pad_add_fusion.pos_ref, s32[8,128]{1,0:T(8,128)S(1)} %collective-permute-done.refs_0_, ...), custom_call_target="tpu_custom_call", output_to_operand_aliasing={{0}: (3, {}), {1}: (4, {}), {2}: (5, {}), {3}: (6, {})} | custom-call | bytes 1048576 | tf_op jit(solution)/shard_map/select_other/pallas_call | solution.py:18
  3.4 5.1 %collective-permute-start.2 = (bf16[32,2048]{1,0:T(8,128)(2,1)S(1)}, bf16[32,2048]{1,0:T(8,128)(2,1)S(1)}, u32[]{:S(2)}, u32[]{:S(2)}) collective-permute-start(bf16[32,2048]{1,0:T(8,128)(2,1)S(1)} %get-tuple-element.40), channel_id=1, source_target_pairs={{0,12},{4,0},{8,4},{12,8},{1,13},{5,1},{9,5},{13,9},{2,14},{6,2},{... | collective-permute-start | bytes 393224 | tf_op jit(solution)/shard_map/ppermute | solution.py:199
  8.5 1.0 %collective-permute-start.4 = (bf16[32,2048]{1,0:T(8,128)(2,1)S(1)}, bf16[32,2048]{1,0:T(8,128)(2,1)S(1)}, u32[]{:S(2)}, u32[]{:S(2)}) collective-permute-start(bf16[32,2048]{1,0:T(8,128)(2,1)S(1)} %get-tuple-element.44), channel_id=1, source_target_pairs={{0,8},{4,12},{8,0},{12,4},{1,9},{5,13},{9,1},{13,5},{2,10},{6,14},... | collective-permute-start | bytes 393224 | tf_op jit(solution)/shard_map/ppermute | solution.py:199
  9.5 1.5 %collective-permute-start.5 = (bf16[32,2048]{1,0:T(8,128)(2,1)S(1)}, bf16[32,2048]{1,0:T(8,128)(2,1)S(1)}, u32[]{:S(2)}, u32[]{:S(2)}) collective-permute-start(bf16[32,2048]{1,0:T(8,128)(2,1)S(1)} %get-tuple-element.41.after_ref.refs_0_), channel_id=1, source_target_pairs={{0,2},{2,0},{1,3},{3,1},{4,6},{6,4},{5,7},{7,5},{8,10},{10,8},{9,1... | collective-permute-start | bytes 393224 | tf_op jit(solution)/shard_map/ppermute | solution.py:199
  11.0 0.7 %copy-done.1 = s32[128,8]{0,1:T(8,128)S(1)} copy-done((s32[128,8]{0,1:T(8,128)S(1)}, s32[128,8]{0,1:T(8,128)}, u32[]{:S(2)}) %copy-start.1) | copy-done | bytes 4120
  11.7 0.7 %copy-done.2 = s32[128,8]{0,1:T(8,128)S(1)} copy-done((s32[128,8]{0,1:T(8,128)S(1)}, s32[128,8]{0,1:T(8,128)}, u32[]{:S(2)}) %copy-start.2) | copy-done | bytes 4120
  12.4 0.8 %mixing.1.mixing_ref = bf16[128,256]{1,0:T(8,128)(2,1)S(1)} custom-call(s32[3]{0:T(128)S(1)} %pad_add_fusion.pos_ref, bf16[32,2048]{1,0:T(8,128)(2,1)S(1)} %get-tuple-element.41.after_ref.refs_0_, s32[8,128]{1,0:T(8,128)S(1)} %bitcast.12, s32[8,128]{1,0:T(8,128)S(1)} %bitcast.13), custom_call_target="tpu_custom_call" | custom-call | bytes 655360 | tf_op jit(solution)/shard_map/mixing/pallas_call | solution.py:18
  13.2 0.7 %collective-permute-start.8 = (bf16[32,2048]{1,0:T(8,128)(2,1)S(1)}, bf16[32,2048]{1,0:T(8,128)(2,1)S(1)}, u32[]{:S(2)}, u32[]{:S(2)}) collective-permute-start(bf16[32,2048]{1,0:T(8,128)(2,1)S(1)} %collective-permute-done.2.refs_3_), channel_id=1, source_target_pairs={{0,2},{2,0},{1,3},{3,1},{4,6},{6,4},{5,7},{7,5},{8,10},{10,8},{9,1... | collective-permute-start | bytes 393224 | tf_op jit(solution)/shard_map/ppermute | solution.py:199
  13.9 2.8 %collective-permute-done.3.refs_1_ = bf16[32,2048]{1,0:T(8,128)(2,1)S(1)} collective-permute-done((bf16[32,2048]{1,0:T(8,128)(2,1)S(1)}, bf16[32,2048]{1,0:T(8,128)(2,1)S(1)}, u32[]{:S(2)}, u32[]{:S(2)}) %collective-permute-start.3) | collective-permute-done | bytes 131104 | tf_op jit(solution)/shard_map/ppermute | solution.py:199
  16.7 1.5 %collective-permute-start.6 = (bf16[32,2048]{1,0:T(8,128)(2,1)S(1)}, bf16[32,2048]{1,0:T(8,128)(2,1)S(1)}, u32[]{:S(2)}, u32[]{:S(2)}) collective-permute-start(bf16[32,2048]{1,0:T(8,128)(2,1)S(1)} %collective-permute-done.3.refs_1_), channel_id=1, source_target_pairs={{0,2},{2,0},{1,3},{3,1},{4,6},{6,4},{5,7},{7,5},{8,10},{10,8},{9,1... | collective-permute-start | bytes 393224 | tf_op jit(solution)/shard_map/ppermute | solution.py:199
  18.2 1.9 %collective-permute-done.4.refs_2_ = bf16[32,2048]{1,0:T(8,128)(2,1)S(1)} collective-permute-done((bf16[32,2048]{1,0:T(8,128)(2,1)S(1)}, bf16[32,2048]{1,0:T(8,128)(2,1)S(1)}, u32[]{:S(2)}, u32[]{:S(2)}) %collective-permute-start.4) | collective-permute-done | bytes 131104 | tf_op jit(solution)/shard_map/ppermute | solution.py:199
  20.1 1.5 %collective-permute-start.7 = (bf16[32,2048]{1,0:T(8,128)(2,1)S(1)}, bf16[32,2048]{1,0:T(8,128)(2,1)S(1)}, u32[]{:S(2)}, u32[]{:S(2)}) collective-permute-start(bf16[32,2048]{1,0:T(8,128)(2,1)S(1)} %collective-permute-done.4.refs_2_), channel_id=1, source_target_pairs={{0,2},{2,0},{1,3},{3,1},{4,6},{6,4},{5,7},{7,5},{8,10},{10,8},{9,1... | collective-permute-start | bytes 393224 | tf_op jit(solution)/shard_map/ppermute | solution.py:199
  21.6 4.3 %near.1 = (f32[128,512]{1,0:T(8,128)S(1)}, f32[128,512]{1,0:T(8,128)S(1)}, bf16[2048,512]{1,0:T(8,128)(2,1)S(1)}, bf16[2048,512]{1,0:T(8,128)(2,1)S(1)}) custom-call(s32[3]{0:T(128)S(1)} %pad_add_fusion.pos_ref, bf16[4096,512]{1,0:T(8,128)(2,1)} %bitcast.14, bf16[4096,512]{1,0:T(8,128)(2,1)} %bitcast.15, ...), custom_call_target="tpu_custom_call" | custom-call | flops 536870912 | bytes 16777216 | tf_op jit(solution)/shard_map/near/pallas_call | solution.py:18
  26.3 1.6 %far.1 = (bf16[128,512]{1,0:T(8,128)(2,1)S(1)}, bf16[32,2048]{1,0:T(8,128)(2,1)S(1)}, bf16[32,2048]{1,0:T(8,128)(2,1)S(1)}, bf16[32,2048]{1,0:T(8,128)(2,1)S(1)}, bf16[32,2048]{1,0:T(8,128)(2,1)S(1)}) custom-call(s32[3]{0:T(128)S(1)} %pad_add_fusion.pos_ref, bf16[2048,512]{1,0:T(8,128)(2,1)S(1)} %get-tuple-element.46.gate_ref, ...), custom_call_target="tpu_custom_call" | custom-call | flops 805306368 | bytes 8388608 | tf_op jit(solution)/shard_map/far/pallas_call | solution.py:18
  28.5 1.0 %keep.1 = (bf16[32,2048]{1,0:T(8,128)(2,1)S(1)}, bf16[32,2048]{1,0:T(8,128)(2,1)S(1)}, bf16[32,2048]{1,0:T(8,128)(2,1)S(1)}, bf16[32,2048]{1,0:T(8,128)(2,1)S(1)}) custom-call(s32[3]{0:T(128)S(1)} %pad_add_fusion.pos_ref, bf16[512,4096]{1,0:T(8,128)(2,1)S(1)} %bitcast.9, bf16[128,512]{1,0:T(8,128)(2,1)S(1)} %get-tuple-element.53.hidden_ref), custom_call_target="tpu_custom_call" | custom-call | flops 268435456 | bytes 2097152 | tf_op jit(solution)/shard_map/keep/pallas_call | solution.py:18
  29.5 1.5 %collective-permute-start.10 = (bf16[32,2048]{1,0:T(8,128)(2,1)S(1)}, bf16[32,2048]{1,0:T(8,128)(2,1)S(1)}, u32[]{:S(2)}, u32[]{:S(2)}) collective-permute-start(bf16[32,2048]{1,0:T(8,128)(2,1)S(1)} %get-tuple-element.63), channel_id=1, source_target_pairs={{0,2},{2,0},{1,3},{3,1},{4,6},{6,4},{5,7},{7,5},{8,10},{10,8},{9,1... | collective-permute-start | bytes 393224 | tf_op jit(solution)/shard_map/ppermute | solution.py:199
  31.6 2.8 %collective-permute-done.9 = bf16[32,2048]{1,0:T(8,128)(2,1)S(1)} collective-permute-done((bf16[32,2048]{1,0:T(8,128)(2,1)S(1)}, bf16[32,2048]{1,0:T(8,128)(2,1)S(1)}, u32[]{:S(2)}, u32[]{:S(2)}) %collective-permute-start.9) | collective-permute-done | bytes 131104 | tf_op jit(solution)/shard_map/ppermute | solution.py:199
  34.9 1.5 %collective-permute-done.10 = bf16[32,2048]{1,0:T(8,128)(2,1)S(1)} collective-permute-done((bf16[32,2048]{1,0:T(8,128)(2,1)S(1)}, bf16[32,2048]{1,0:T(8,128)(2,1)S(1)}, u32[]{:S(2)}, u32[]{:S(2)}) %collective-permute-start.10) | collective-permute-done | bytes 131104 | tf_op jit(solution)/shard_map/ppermute | solution.py:199
  36.4 1.0 %collective-permute-start.15 = (bf16[32,2048]{1,0:T(8,128)(2,1)S(1)}, bf16[32,2048]{1,0:T(8,128)(2,1)S(1)}, u32[]{:S(2)}, u32[]{:S(2)}) collective-permute-start(bf16[32,2048]{1,0:T(8,128)(2,1)S(1)} %add_convert_fusion.2), channel_id=1, source_target_pairs={{0,4},{4,8},{8,12},{12,0},{1,5},{5,9},{9,13},{13,1},{2,6},{6,10},{... | collective-permute-start | bytes 393224 | tf_op jit(solution)/shard_map/ppermute | solution.py:199
  37.9 1.1 %collective-permute-done.12 = bf16[32,2048]{1,0:T(8,128)(2,1)S(1)} collective-permute-done((bf16[32,2048]{1,0:T(8,128)(2,1)S(1)}, bf16[32,2048]{1,0:T(8,128)(2,1)S(1)}, u32[]{:S(2)}, u32[]{:S(2)}) %collective-permute-start.12) | collective-permute-done | bytes 131104 | tf_op jit(solution)/shard_map/ppermute | solution.py:199
  39.0 2.6 %collective-permute-start.13 = (bf16[32,2048]{1,0:T(8,128)(2,1)S(1)}, bf16[32,2048]{1,0:T(8,128)(2,1)S(1)}, u32[]{:S(2)}, u32[]{:S(2)}) collective-permute-start(bf16[32,2048]{1,0:T(8,128)(2,1)S(1)} %add_convert_fusion), channel_id=1, source_target_pairs={{0,12},{4,0},{8,4},{12,8},{1,13},{5,1},{9,5},{13,9},{2,14},{6,2},{... | collective-permute-start | bytes 393224 | tf_op jit(solution)/shard_map/ppermute | solution.py:199
  41.6 2.8 %collective-permute-done.14.refs_2_ = bf16[32,2048]{1,0:T(8,128)(2,1)S(1)} collective-permute-done((bf16[32,2048]{1,0:T(8,128)(2,1)S(1)}, bf16[32,2048]{1,0:T(8,128)(2,1)S(1)}, u32[]{:S(2)}, u32[]{:S(2)}) %collective-permute-start.14) | collective-permute-done | bytes 131104 | tf_op jit(solution)/shard_map/ppermute | solution.py:199
  46.6 1.1 %mix.1 = bf16[128,2048]{1,0:T(8,128)(2,1)} custom-call(bf16[128,256]{1,0:T(8,128)(2,1)S(1)} %mixing.1.mixing_ref, bf16[32,2048]{1,0:T(8,128)(2,1)S(1)} %add_convert_fusion.1.refs_0_, bf16[32,2048]{1,0:T(8,128)(2,1)S(1)} %collective-permute-done.13.refs_1_, bf16[32,2048]{1,0:T(8,128)(2,1)S(1)} %collective-permute-done.14.refs_2_, ...), custom_call_target="tpu_custom_call" | custom-call | bytes 1572864 | tf_op jit(solution)/shard_map/mix/pallas_call | solution.py:18
  (38 shorter events, 5.3 us)
Async XLA Ops:
  0.0 2.5 %collective-permute-start.1 = (bf16[128,2048]{1,0:T(8,128)(2,1)}, bf16[128,2048]{1,0:T(8,128)(2,1)S(1)}, u32[]{:S(2)}, u32[]{:S(2)}) collective-permute-start(bf16[128,2048]{1,0:T(8,128)(2,1)} %tokens.1), channel_id=1, source_target_pairs={{0,1},{1,0},{2,3},{3,2},{4,5},{5,4},{6,7},{7,6},{8,9},{9,8},{10,11... | collective-permute-start | bytes 1572872 | tf_op jit(solution)/shard_map/ppermute | solution.py:199
  0.5 2.0 %collective-permute-start = (s32[8,128]{1,0:T(8,128)}, s32[8,128]{1,0:T(8,128)S(1)}, u32[]{:S(2)}, u32[]{:S(2)}) collective-permute-start(s32[8,128]{1,0:T(8,128)} %bitcast.10), channel_id=1, source_target_pairs={{0,1},{1,0},{2,3},{3,2},{4,5},{5,4},{6,7},{7,6},{8,9},{9,8},{10,11... | collective-permute-start | bytes 12296 | tf_op jit(solution)/shard_map/ppermute | solution.py:199
  3.4 9.8 %collective-permute-start.2 = (bf16[32,2048]{1,0:T(8,128)(2,1)S(1)}, bf16[32,2048]{1,0:T(8,128)(2,1)S(1)}, u32[]{:S(2)}, u32[]{:S(2)}) collective-permute-start(bf16[32,2048]{1,0:T(8,128)(2,1)S(1)} %get-tuple-element.40), channel_id=1, source_target_pairs={{0,12},{4,0},{8,4},{12,8},{1,13},{5,1},{9,5},{13,9},{2,14},{6,2},{... | collective-permute-start | bytes 393224 | tf_op jit(solution)/shard_map/ppermute | solution.py:199
  8.5 8.3 %collective-permute-start.3 = (bf16[32,2048]{1,0:T(8,128)(2,1)S(1)}, bf16[32,2048]{1,0:T(8,128)(2,1)S(1)}, u32[]{:S(2)}, u32[]{:S(2)}) collective-permute-start(bf16[32,2048]{1,0:T(8,128)(2,1)S(1)} %get-tuple-element.43), channel_id=1, source_target_pairs={{0,4},{4,8},{8,12},{12,0},{1,5},{5,9},{9,13},{13,1},{2,6},{6,10},{... | collective-permute-start | bytes 393224 | tf_op jit(solution)/shard_map/ppermute | solution.py:199
  8.5 11.6 %collective-permute-start.4 = (bf16[32,2048]{1,0:T(8,128)(2,1)S(1)}, bf16[32,2048]{1,0:T(8,128)(2,1)S(1)}, u32[]{:S(2)}, u32[]{:S(2)}) collective-permute-start(bf16[32,2048]{1,0:T(8,128)(2,1)S(1)} %get-tuple-element.44), channel_id=1, source_target_pairs={{0,8},{4,12},{8,0},{12,4},{1,9},{5,13},{9,1},{13,5},{2,10},{6,14},... | collective-permute-start | bytes 393224 | tf_op jit(solution)/shard_map/ppermute | solution.py:199
  9.5 16.4 %collective-permute-start.5 = (bf16[32,2048]{1,0:T(8,128)(2,1)S(1)}, bf16[32,2048]{1,0:T(8,128)(2,1)S(1)}, u32[]{:S(2)}, u32[]{:S(2)}) collective-permute-start(bf16[32,2048]{1,0:T(8,128)(2,1)S(1)} %get-tuple-element.41.after_ref.refs_0_), channel_id=1, source_target_pairs={{0,2},{2,0},{1,3},{3,1},{4,6},{6,4},{5,7},{7,5},{8,10},{10,8},{9,1... | collective-permute-start | bytes 393224 | tf_op jit(solution)/shard_map/ppermute | solution.py:199
  11.0 0.7 %copy-start.1 = (s32[128,8]{0,1:T(8,128)S(1)}, s32[128,8]{0,1:T(8,128)}, u32[]{:S(2)}) copy-start(s32[128,8]{0,1:T(8,128)} %param.7) | copy-start | bytes 12292
  11.7 0.7 %copy-start.2 = (s32[128,8]{0,1:T(8,128)S(1)}, s32[128,8]{0,1:T(8,128)}, u32[]{:S(2)}) copy-start(s32[128,8]{0,1:T(8,128)} %param.8) | copy-start | bytes 12292
  13.2 12.8 %collective-permute-start.8 = (bf16[32,2048]{1,0:T(8,128)(2,1)S(1)}, bf16[32,2048]{1,0:T(8,128)(2,1)S(1)}, u32[]{:S(2)}, u32[]{:S(2)}) collective-permute-start(bf16[32,2048]{1,0:T(8,128)(2,1)S(1)} %collective-permute-done.2.refs_3_), channel_id=1, source_target_pairs={{0,2},{2,0},{1,3},{3,1},{4,6},{6,4},{5,7},{7,5},{8,10},{10,8},{9,1... | collective-permute-start | bytes 393224 | tf_op jit(solution)/shard_map/ppermute | solution.py:199
  16.7 9.2 %collective-permute-start.6 = (bf16[32,2048]{1,0:T(8,128)(2,1)S(1)}, bf16[32,2048]{1,0:T(8,128)(2,1)S(1)}, u32[]{:S(2)}, u32[]{:S(2)}) collective-permute-start(bf16[32,2048]{1,0:T(8,128)(2,1)S(1)} %collective-permute-done.3.refs_1_), channel_id=1, source_target_pairs={{0,2},{2,0},{1,3},{3,1},{4,6},{6,4},{5,7},{7,5},{8,10},{10,8},{9,1... | collective-permute-start | bytes 393224 | tf_op jit(solution)/shard_map/ppermute | solution.py:199
  20.1 5.9 %collective-permute-start.7 = (bf16[32,2048]{1,0:T(8,128)(2,1)S(1)}, bf16[32,2048]{1,0:T(8,128)(2,1)S(1)}, u32[]{:S(2)}, u32[]{:S(2)}) collective-permute-start(bf16[32,2048]{1,0:T(8,128)(2,1)S(1)} %collective-permute-done.4.refs_2_), channel_id=1, source_target_pairs={{0,2},{2,0},{1,3},{3,1},{4,6},{6,4},{5,7},{7,5},{8,10},{10,8},{9,1... | collective-permute-start | bytes 393224 | tf_op jit(solution)/shard_map/ppermute | solution.py:199
  21.6 4.7 %copy-start = (bf16[1,512,4096]{2,1,0:T(8,128)(2,1)S(1)}, bf16[1,512,4096]{2,1,0:T(8,128)(2,1)}, u32[]{:S(2)}) copy-start(bf16[1,512,4096]{2,1,0:T(8,128)(2,1)} %param.11) | copy-start | bytes 12582916
  27.9 6.5 %collective-permute-start.9 = (bf16[32,2048]{1,0:T(8,128)(2,1)S(1)}, bf16[32,2048]{1,0:T(8,128)(2,1)S(1)}, u32[]{:S(2)}, u32[]{:S(2)}) collective-permute-start(bf16[32,2048]{1,0:T(8,128)(2,1)S(1)} %get-tuple-element.61), channel_id=1, source_target_pairs={{0,2},{2,0},{1,3},{3,1},{4,6},{6,4},{5,7},{7,5},{8,10},{10,8},{9,1... | collective-permute-start | bytes 393224 | tf_op jit(solution)/shard_map/ppermute | solution.py:199
  29.5 6.9 %collective-permute-start.10 = (bf16[32,2048]{1,0:T(8,128)(2,1)S(1)}, bf16[32,2048]{1,0:T(8,128)(2,1)S(1)}, u32[]{:S(2)}, u32[]{:S(2)}) collective-permute-start(bf16[32,2048]{1,0:T(8,128)(2,1)S(1)} %get-tuple-element.63), channel_id=1, source_target_pairs={{0,2},{2,0},{1,3},{3,1},{4,6},{6,4},{5,7},{7,5},{8,10},{10,8},{9,1... | collective-permute-start | bytes 393224 | tf_op jit(solution)/shard_map/ppermute | solution.py:199
  31.1 7.9 %collective-permute-start.12 = (bf16[32,2048]{1,0:T(8,128)(2,1)S(1)}, bf16[32,2048]{1,0:T(8,128)(2,1)S(1)}, u32[]{:S(2)}, u32[]{:S(2)}) collective-permute-start(bf16[32,2048]{1,0:T(8,128)(2,1)S(1)} %get-tuple-element.66), channel_id=1, source_target_pairs={{0,2},{2,0},{1,3},{3,1},{4,6},{6,4},{5,7},{7,5},{8,10},{10,8},{9,1... | collective-permute-start | bytes 393224 | tf_op jit(solution)/shard_map/ppermute | solution.py:199
  34.5 9.9 %collective-permute-start.14 = (bf16[32,2048]{1,0:T(8,128)(2,1)S(1)}, bf16[32,2048]{1,0:T(8,128)(2,1)S(1)}, u32[]{:S(2)}, u32[]{:S(2)}) collective-permute-start(bf16[32,2048]{1,0:T(8,128)(2,1)S(1)} %add_convert_fusion.3), channel_id=1, source_target_pairs={{0,8},{4,12},{8,0},{12,4},{1,9},{5,13},{9,1},{13,5},{2,10},{6,14},... | collective-permute-start | bytes 393224 | tf_op jit(solution)/shard_map/ppermute | solution.py:199
  36.4 8.6 %collective-permute-start.15 = (bf16[32,2048]{1,0:T(8,128)(2,1)S(1)}, bf16[32,2048]{1,0:T(8,128)(2,1)S(1)}, u32[]{:S(2)}, u32[]{:S(2)}) collective-permute-start(bf16[32,2048]{1,0:T(8,128)(2,1)S(1)} %add_convert_fusion.2), channel_id=1, source_target_pairs={{0,4},{4,8},{8,12},{12,0},{1,5},{5,9},{9,13},{13,1},{2,6},{6,10},{... | collective-permute-start | bytes 393224 | tf_op jit(solution)/shard_map/ppermute | solution.py:199
  37.4 7.0 %collective-permute-start.11 = (bf16[32,2048]{1,0:T(8,128)(2,1)S(1)}, bf16[32,2048]{1,0:T(8,128)(2,1)S(1)}, u32[]{:S(2)}, u32[]{:S(2)}) collective-permute-start(bf16[32,2048]{1,0:T(8,128)(2,1)S(1)} %get-tuple-element.64), channel_id=1, source_target_pairs={{0,2},{2,0},{1,3},{3,1},{4,6},{6,4},{5,7},{7,5},{8,10},{10,8},{9,1... | collective-permute-start | bytes 393224 | tf_op jit(solution)/shard_map/ppermute | solution.py:199
  39.0 6.3 %collective-permute-start.13 = (bf16[32,2048]{1,0:T(8,128)(2,1)S(1)}, bf16[32,2048]{1,0:T(8,128)(2,1)S(1)}, u32[]{:S(2)}, u32[]{:S(2)}) collective-permute-start(bf16[32,2048]{1,0:T(8,128)(2,1)S(1)} %add_convert_fusion), channel_id=1, source_target_pairs={{0,12},{4,0},{8,4},{12,8},{1,13},{5,1},{9,5},{13,9},{2,14},{6,2},{... | collective-permute-start | bytes 393224 | tf_op jit(solution)/shard_map/ppermute | solution.py:199
  44.4 1.3 %collective-permute-start.18 = (bf16[16,2048]{1,0:T(8,128)(2,1)S(1)}, bf16[16,2048]{1,0:T(8,128)(2,1)S(1)}, u32[]{:S(2)}, u32[]{:S(2)}) collective-permute-start(bf16[16,2048]{1,0:T(8,128)(2,1)S(1)} %slice.18), channel_id=1, source_target_pairs={{0,1},{1,0},{2,3},{3,2},{4,5},{5,4},{6,7},{7,6},{8,9},{9,8},{10,11... | collective-permute-start | bytes 196616 | tf_op jit(solution)/shard_map/ppermute | solution.py:199
  44.5 1.5 %collective-permute-start.16 = (bf16[16,2048]{1,0:T(8,128)(2,1)S(1)}, bf16[16,2048]{1,0:T(8,128)(2,1)S(1)}, u32[]{:S(2)}, u32[]{:S(2)}) collective-permute-start(bf16[16,2048]{1,0:T(8,128)(2,1)S(1)} %slice.16), channel_id=1, source_target_pairs={{0,1},{1,0},{2,3},{3,2},{4,5},{5,4},{6,7},{7,6},{8,9},{9,8},{10,11... | collective-permute-start | bytes 196616 | tf_op jit(solution)/shard_map/ppermute | solution.py:199
  45.0 1.3 %collective-permute-start.19 = (bf16[16,2048]{1,0:T(8,128)(2,1)S(1)}, bf16[16,2048]{1,0:T(8,128)(2,1)S(1)}, u32[]{:S(2)}, u32[]{:S(2)}) collective-permute-start(bf16[16,2048]{1,0:T(8,128)(2,1)S(1)} %slice.19), channel_id=1, source_target_pairs={{0,1},{1,0},{2,3},{3,2},{4,5},{5,4},{6,7},{7,6},{8,9},{9,8},{10,11... | collective-permute-start | bytes 196616 | tf_op jit(solution)/shard_map/ppermute | solution.py:199
  45.3 1.3 %collective-permute-start.17 = (bf16[16,2048]{1,0:T(8,128)(2,1)S(1)}, bf16[16,2048]{1,0:T(8,128)(2,1)S(1)}, u32[]{:S(2)}, u32[]{:S(2)}) collective-permute-start(bf16[16,2048]{1,0:T(8,128)(2,1)S(1)} %slice.17), channel_id=1, source_target_pairs={{0,1},{1,0},{2,3},{3,2},{4,5},{5,4},{6,7},{7,6},{8,9},{9,8},{10,11... | collective-permute-start | bytes 196616 | tf_op jit(solution)/shard_map/ppermute | solution.py:199

commit v6 on v5

--- a/solution.py
+++ b/solution.py
@@ -9,7 +9,6 @@
 
 CAP = 16
 VMEM = pl.BlockSpec(memory_space=pltpu.VMEM)
-SMEM = pl.BlockSpec(memory_space=pltpu.SMEM)
 HBM = pl.BlockSpec(memory_space=pltpu.HBM)
 BF16, F32 = jnp.bfloat16, jnp.float32
 
@@ -47,8 +46,8 @@
     return jnp.where((slots[row : row + 1] == slot) & (hits[row : row + 1] > 0), 1.0, 0.0)
 
 
-def select(pos_ref, routes, tokens, outs, n_pool, n_pair, u, copy=None):
-    pool, pair = pos_ref[0], pos_ref[1]
+def select(routes, tokens, outs, n_pool, n_pair, u, copy=None):
+    pool, pair = lax.axis_index("pool"), lax.axis_index("pair")
     experts = [lax.rem(pool + s, n_pool) * n_pair + pair for s in range(n_pool)]
     hits, slots = picks(routes[...], experts)
     sel = jnp.concatenate([one_hot(hits, slots, s) for s in range(n_pool)], axis=0)
@@ -59,17 +58,17 @@
         outs[s][u * CAP : (u + 1) * CAP, :] = rows[s * CAP : (s + 1) * CAP]
 
 
-def select_own_kernel(n_pool, n_pair, pos_ref, routes, tokens, *refs):
+def select_own_kernel(n_pool, n_pair, routes, tokens, *refs):
     outs, held, held_routes, sems = refs[:n_pool], refs[n_pool], refs[n_pool + 1], refs[n_pool + 2]
     first = pltpu.make_async_copy(routes, held_routes, sems.at[0])
     second = pltpu.make_async_copy(tokens, held, sems.at[1])
     first.start()
     second.start()
     first.wait()
-    select(pos_ref, held_routes, held, outs, n_pool, n_pair, 0, second)
-
-
-def select_other_kernel(n_pool, n_pair, pos_ref, *refs):
+    select(held_routes, held, outs, n_pool, n_pair, 0, second)
+
+
+def select_other_kernel(n_pool, n_pair, *refs):
     others = n_pair - 1
     routes, tokens = refs[:others], refs[others : 2 * others]
     outs = refs[2 * others + n_pool :]
@@ -77,11 +76,11 @@
     for s in range(n_pool):
         outs[s][:CAP, :] = held[s][:CAP, :]
     for u in range(1, n_pair):
-        select(pos_ref, routes[u - 1], tokens[u - 1], outs, n_pool, n_pair, u)
-
-
-def mixing_kernel(n_pool, n_pair, pos_ref, after_ref, routes_ref, weights_ref, out_ref):
-    pool, pair = pos_ref[0], pos_ref[1]
+        select(routes[u - 1], tokens[u - 1], outs, n_pool, n_pair, u)
+
+
+def mixing_kernel(n_pool, n_pair, after_ref, routes_ref, weights_ref, out_ref):
+    pool, pair = lax.axis_index("pool"), lax.axis_index("pair")
     routes, weights = routes_ref[...], weights_ref[...]
     totals = jnp.sum(weights.astype(F32), axis=0, keepdims=True)
     experts = [
@@ -106,11 +105,11 @@
     return jnp.concatenate([r[...] for r in refs], axis=0)
 
 
-def near_kernel(n_tp, tiles, pos_ref, gate_ref, up_ref, *refs):
+def near_kernel(n_tp, tiles, gate_ref, up_ref, *refs):
     rows = refs[:-7]
     gate_out, up_out, gate_far, up_far, gate_near, up_near, sems = refs[-7:]
     width = rows[0].shape[1]
-    tp = pos_ref[2]
+    tp = lax.axis_index("tp")
     depth = width // tiles
     pairs = ((gate_ref, gate_near, gate_far), (up_ref, up_near, up_far))
     near, far = [], []
@@ -143,12 +142,12 @@
         c.wait()
 
 
-def far_kernel(n_tp, n_chunks, pos_ref, gate_ref, up_ref, down_ref, gate_in, up_in, *refs):
+def far_kernel(n_tp, n_chunks, gate_ref, up_ref, down_ref, gate_in, up_in, *refs):
     far = n_tp - 1
     rows = [refs[k * n_chunks : (k + 1) * n_chunks] for k in range(far)]
     hidden_ref, outs = refs[far * n_chunks], refs[far * n_chunks + 1 :]
     width = down_ref.shape[1] // n_tp
-    tp = pos_ref[2]
+    tp = lax.axis_index("tp")
     gate, up = gate_in[...], up_in[...]
     for k in range(1, n_tp):
         at = pl.ds((k - 1) * width, width)
@@ -170,9 +169,9 @@
         at += o.shape[0]
 
 
-def keep_kernel(n_tp, pos_ref, down_ref, hidden_ref, *outs):
+def keep_kernel(n_tp, down_ref, hidden_ref, *outs):
     width = outs[0].shape[1]
-    at = pl.ds(pl.multiple_of(pos_ref[2] * width, width), width)
+    at = pl.ds(pl.multiple_of(lax.axis_index("tp") * width, width), width)
     put(outs, jnp.dot(hidden_ref[...], down_ref[:, at], preferred_element_type=F32).astype(BF16))
 
 
@@ -216,7 +215,6 @@
     n_pool, n_tp, n_pair = (lax.axis_size(a) for a in ("pool", "tp", "pair"))
     streams, width = tokens.shape
     hidden_units = w_gate.shape[2]
-    pos = jnp.stack([lax.axis_index(a) for a in ("pool", "pair", "tp")]).astype(jnp.int32)
     routes_t, weights_t = routes.T, gate_weights.T
     rows = n_pair * CAP
     small = n_pool == 4 and n_tp == 2
@@ -231,8 +229,8 @@
         functools.partial(select_own_kernel, n_pool, n_pair),
         "select_own",
         [shape(rows, width)] * n_pool,
-        [SMEM, HBM, HBM],
-        (pos, pltpu.with_memory_space_constraint(routes_t, pltpu.HBM), pltpu.with_memory_space_constraint(tokens, pltpu.HBM)),
+        [HBM, HBM],
+        (pltpu.with_memory_space_constraint(routes_t, pltpu.HBM), pltpu.with_memory_space_constraint(tokens, pltpu.HBM)),
         2 * 2 * streams * width,
         scratch=[
             pltpu.VMEM((streams, width), BF16),
@@ -244,10 +242,10 @@
         functools.partial(select_other_kernel, n_pool, n_pair),
         "select_other",
         [shape(rows, width)] * n_pool,
-        [SMEM] + [VMEM] * (2 * (n_pair - 1) + n_pool),
-        (pos, *far_routes, *far_tokens, *leaving),
+        [VMEM] * (2 * (n_pair - 1) + n_pool),
+        (*far_routes, *far_tokens, *leaving),
         2 * 2 * streams * width,
-        alias={1 + 2 * (n_pair - 1) + s: s for s in range(n_pool)},
+        alias={2 * (n_pair - 1) + s: s for s in range(n_pool)},
     )
     gate_mat, up_mat, down_mat = w_gate[0], w_up[0], w_down[0]
     slots = n_pool * rows
@@ -255,8 +253,8 @@
         functools.partial(mixing_kernel, n_pool, n_pair),
         "mixing",
         [shape(streams, 2 * slots)],
-        [SMEM, VMEM, VMEM, VMEM],
-        (pos, leaving[0], routes_t, weights_t),
+        [VMEM, VMEM, VMEM],
+        (leaving[0], routes_t, weights_t),
         4 * 10 * streams * slots,
     )
 
@@ -272,8 +270,8 @@
         functools.partial(near_kernel, n_tp, tiles),
         "near",
         [shape(slots, hidden_units, F32)] * 2 + [shape(rest, hidden_units)] * 2,
-        [SMEM] + [HBM] * 2 + [VMEM] * n_pool,
-        (pos, gate_mat, up_mat, *near),
+        [HBM] * 2 + [VMEM] * n_pool,
+        (gate_mat, up_mat, *near),
         2 * 2 * (w_gate.size + w_up.size),
         4 * slots * width * hidden_units,
         scratch=[pltpu.VMEM((width, hidden_units), BF16)] * 2
@@ -284,8 +282,8 @@
         functools.partial(far_kernel, n_tp, n_pool),
         "far",
         [shape(slots, hidden_units)] + [shape(rows, width)] * (n_pool * (n_tp - 1)),
-        [SMEM] + [VMEM] * (5 + n_pool * (n_tp - 1)),
-        (pos, gate_far, up_far, down_mat, gate, up, *sum(far, [])),
+        [VMEM] * (5 + n_pool * (n_tp - 1)),
+        (gate_far, up_far, down_mat, gate, up, *sum(far, [])),
         8 * width * hidden_units,
         6 * slots * width * hidden_units,
     )
@@ -294,8 +292,8 @@
         functools.partial(keep_kernel, n_tp),
         "keep",
         [shape(rows, width)] * n_pool,
-        [SMEM] + [VMEM] * 2,
-        (pos, down_mat, hidden),
+        [VMEM] * 2,
+        (down_mat, hidden),
         2 * width * hidden_units,
         2 * slots * width * hidden_units,
     )

time: 47.9 us -> 46.7 us (0.975)
  Pallas kernels: 11.6 us -> 8.22 us
  waiting for transfers between devices: 13.9 us -> 15.5 us
  local copies, waits for them, and re-layouts: 1.69 us -> 2.34 us
    pallas_call x7, Pallas kernels: 11.6 us -> 8.22 us  [call(): pl.pallas_call(kernel, out_shape=outs, in_specs=in_specs, out_specs=[to]...]
    ppermute x20, waiting for transfers between devices: 13.9 us -> 15.5 us  [turn(): return lax.ppermute(x, axis, [(i, (i + shift) % n) for i in range(n)])]
    unnamed x6, local copies, waits for them, and re-layouts: 1.66 us -> 2.31 us
  transfers between devices with their start and end apart: 20 -> 20, of which waited for: 10 -> 11; matrix products, arithmetic and copies ran while one was open for 0% -> 0% of each run, Pallas kernels for 17% -> 12%
where the time goes in v6:
time: 46.7 us; the launch traced here: 46.5 us
  starting transfers between devices  20.1 us (43%)
  waiting for transfers between devices  15.5 us (33%)
  Pallas kernels  8.22 us (18%)
  local copies, waits for them, and re-layouts  2.34 us (5%)
    ppermute x20, starting transfers between devices, turn(): return lax.ppermute(x, axis, [(i, (i + shift) % n) for i in range(n)])  20.1 us
    ppermute x20, waiting for transfers between devices, turn(): return lax.ppermute(x, axis, [(i, (i + shift) % n) for i in range(n)])  15.5 us
    pallas_call x7, Pallas kernels, call(): pl.pallas_call(kernel, out_shape=outs, in_specs=in_specs, out_specs=[to]...  8.22 us
    unnamed x6, local copies, waits for them, and re-layouts  2.31 us
  transfers between devices with their start and end apart: 20, of which 11 were waited for; matrix products, arithmetic and copies ran while one was open for 0% of the time, Pallas kernels for 12%

profile of v6, /device:TPU:0, one launch (start us, length us, event | category | flops | bytes accessed | tf_op | source)
XLA Modules:
  0.0 46.5 jit_solution(12910882818273270662)
XLA Ops:
  0.5 1.3 %select_own.1 = (bf16[32,2048]{1,0:T(8,128)(2,1)S(1)}, bf16[32,2048]{1,0:T(8,128)(2,1)S(1)}, bf16[32,2048]{1,0:T(8,128)(2,1)S(1)}, bf16[32,2048]{1,0:T(8,128)(2,1)S(1)}) custom-call(s32[8,128]{1,0:T(8,128)} %bitcast.8, bf16[128,2048]{1,0:T(8,128)(2,1)} %tokens.1), custom_call_target="tpu_custom_call" | custom-call | bytes 1048576 | tf_op jit(solution)/shard_map/select_own/pallas_call | solution.py:17
  2.6 5.0 %collective-permute-start.2 = (bf16[32,2048]{1,0:T(8,128)(2,1)S(1)}, bf16[32,2048]{1,0:T(8,128)(2,1)S(1)}, u32[]{:S(2)}, u32[]{:S(2)}) collective-permute-start(bf16[32,2048]{1,0:T(8,128)(2,1)S(1)} %get-tuple-element.40), channel_id=1, source_target_pairs={{0,12},{4,0},{8,4},{12,8},{1,13},{5,1},{9,5},{13,9},{2,14},{6,2},{... | collective-permute-start | bytes 393224 | tf_op jit(solution)/shard_map/ppermute | solution.py:198
  7.6 1.0 %collective-permute-start.4 = (bf16[32,2048]{1,0:T(8,128)(2,1)S(1)}, bf16[32,2048]{1,0:T(8,128)(2,1)S(1)}, u32[]{:S(2)}, u32[]{:S(2)}) collective-permute-start(bf16[32,2048]{1,0:T(8,128)(2,1)S(1)} %get-tuple-element.44), channel_id=1, source_target_pairs={{0,8},{4,12},{8,0},{12,4},{1,9},{5,13},{9,1},{13,5},{2,10},{6,14},... | collective-permute-start | bytes 393224 | tf_op jit(solution)/shard_map/ppermute | solution.py:198
  8.6 1.5 %collective-permute-start.5 = (bf16[32,2048]{1,0:T(8,128)(2,1)S(1)}, bf16[32,2048]{1,0:T(8,128)(2,1)S(1)}, u32[]{:S(2)}, u32[]{:S(2)}) collective-permute-start(bf16[32,2048]{1,0:T(8,128)(2,1)S(1)} %get-tuple-element.41.after_ref.refs_0_), channel_id=1, source_target_pairs={{0,2},{2,0},{1,3},{3,1},{4,6},{6,4},{5,7},{7,5},{8,10},{10,8},{9,1... | collective-permute-start | bytes 393224 | tf_op jit(solution)/shard_map/ppermute | solution.py:198
  10.1 0.7 %copy-done.1 = s32[128,8]{0,1:T(8,128)S(1)} copy-done((s32[128,8]{0,1:T(8,128)S(1)}, s32[128,8]{0,1:T(8,128)}, u32[]{:S(2)}) %copy-start.1) | copy-done | bytes 4120
  10.8 0.7 %copy-done.2 = s32[128,8]{0,1:T(8,128)S(1)} copy-done((s32[128,8]{0,1:T(8,128)S(1)}, s32[128,8]{0,1:T(8,128)}, u32[]{:S(2)}) %copy-start.2) | copy-done | bytes 4120
  11.7 1.3 %collective-permute-start.8 = (bf16[32,2048]{1,0:T(8,128)(2,1)S(1)}, bf16[32,2048]{1,0:T(8,128)(2,1)S(1)}, u32[]{:S(2)}, u32[]{:S(2)}) collective-permute-start(bf16[32,2048]{1,0:T(8,128)(2,1)S(1)} %collective-permute-done.2.refs_3_), channel_id=1, source_target_pairs={{0,2},{2,0},{1,3},{3,1},{4,6},{6,4},{5,7},{7,5},{8,10},{10,8},{9,1... | collective-permute-start | bytes 393224 | tf_op jit(solution)/shard_map/ppermute | solution.py:198
  13.0 2.8 %collective-permute-done.3.refs_1_ = bf16[32,2048]{1,0:T(8,128)(2,1)S(1)} collective-permute-done((bf16[32,2048]{1,0:T(8,128)(2,1)S(1)}, bf16[32,2048]{1,0:T(8,128)(2,1)S(1)}, u32[]{:S(2)}, u32[]{:S(2)}) %collective-permute-start.3) | collective-permute-done | bytes 131104 | tf_op jit(solution)/shard_map/ppermute | solution.py:198
  15.8 1.5 %collective-permute-start.6 = (bf16[32,2048]{1,0:T(8,128)(2,1)S(1)}, bf16[32,2048]{1,0:T(8,128)(2,1)S(1)}, u32[]{:S(2)}, u32[]{:S(2)}) collective-permute-start(bf16[32,2048]{1,0:T(8,128)(2,1)S(1)} %collective-permute-done.3.refs_1_), channel_id=1, source_target_pairs={{0,2},{2,0},{1,3},{3,1},{4,6},{6,4},{5,7},{7,5},{8,10},{10,8},{9,1... | collective-permute-start | bytes 393224 | tf_op jit(solution)/shard_map/ppermute | solution.py:198
  17.3 2.1 %collective-permute-done.4.refs_2_ = bf16[32,2048]{1,0:T(8,128)(2,1)S(1)} collective-permute-done((bf16[32,2048]{1,0:T(8,128)(2,1)S(1)}, bf16[32,2048]{1,0:T(8,128)(2,1)S(1)}, u32[]{:S(2)}, u32[]{:S(2)}) %collective-permute-start.4) | collective-permute-done | bytes 131104 | tf_op jit(solution)/shard_map/ppermute | solution.py:198
  19.4 1.5 %collective-permute-start.7 = (bf16[32,2048]{1,0:T(8,128)(2,1)S(1)}, bf16[32,2048]{1,0:T(8,128)(2,1)S(1)}, u32[]{:S(2)}, u32[]{:S(2)}) collective-permute-start(bf16[32,2048]{1,0:T(8,128)(2,1)S(1)} %collective-permute-done.4.refs_2_), channel_id=1, source_target_pairs={{0,2},{2,0},{1,3},{3,1},{4,6},{6,4},{5,7},{7,5},{8,10},{10,8},{9,1... | collective-permute-start | bytes 393224 | tf_op jit(solution)/shard_map/ppermute | solution.py:198
  20.9 3.7 %near.1 = (f32[128,512]{1,0:T(8,128)S(1)}, f32[128,512]{1,0:T(8,128)S(1)}, bf16[2048,512]{1,0:T(8,128)(2,1)S(1)}, bf16[2048,512]{1,0:T(8,128)(2,1)S(1)}) custom-call(bf16[4096,512]{1,0:T(8,128)(2,1)} %bitcast.11, bf16[4096,512]{1,0:T(8,128)(2,1)} %bitcast.12, bf16[32,2048]{1,0:T(8,128)(2,1)S(1)} %get-tuple-element.41.after_ref.refs_0_, ...), custom_call_target="tpu_custom_call" | custom-call | flops 536870912 | bytes 16777216 | tf_op jit(solution)/shard_map/near/pallas_call | solution.py:17
  24.6 0.9 %copy-done = bf16[1,512,4096]{2,1,0:T(8,128)(2,1)S(1)} copy-done((bf16[1,512,4096]{2,1,0:T(8,128)(2,1)S(1)}, bf16[1,512,4096]{2,1,0:T(8,128)(2,1)}, u32[]{:S(2)}) %copy-start) | copy-done | bytes 4194328
  25.5 1.1 %far.1 = (bf16[128,512]{1,0:T(8,128)(2,1)S(1)}, bf16[32,2048]{1,0:T(8,128)(2,1)S(1)}, bf16[32,2048]{1,0:T(8,128)(2,1)S(1)}, bf16[32,2048]{1,0:T(8,128)(2,1)S(1)}, bf16[32,2048]{1,0:T(8,128)(2,1)S(1)}) custom-call(bf16[2048,512]{1,0:T(8,128)(2,1)S(1)} %get-tuple-element.46.gate_ref, bf16[2048,512]{1,0:T(8,128)(2,1)S(1)} %get-tuple-element.47.up_ref, ...), custom_call_target="tpu_custom_call" | custom-call | flops 805306368 | bytes 8388608 | tf_op jit(solution)/shard_map/far/pallas_call | solution.py:17
  26.6 0.6 %collective-permute-start.9 = (bf16[32,2048]{1,0:T(8,128)(2,1)S(1)}, bf16[32,2048]{1,0:T(8,128)(2,1)S(1)}, u32[]{:S(2)}, u32[]{:S(2)}) collective-permute-start(bf16[32,2048]{1,0:T(8,128)(2,1)S(1)} %get-tuple-element.61), channel_id=1, source_target_pairs={{0,2},{2,0},{1,3},{3,1},{4,6},{6,4},{5,7},{7,5},{8,10},{10,8},{9,1... | collective-permute-start | bytes 393224 | tf_op jit(solution)/shard_map/ppermute | solution.py:198
  27.7 1.6 %collective-permute-start.10 = (bf16[32,2048]{1,0:T(8,128)(2,1)S(1)}, bf16[32,2048]{1,0:T(8,128)(2,1)S(1)}, u32[]{:S(2)}, u32[]{:S(2)}) collective-permute-start(bf16[32,2048]{1,0:T(8,128)(2,1)S(1)} %get-tuple-element.63), channel_id=1, source_target_pairs={{0,2},{2,0},{1,3},{3,1},{4,6},{6,4},{5,7},{7,5},{8,10},{10,8},{9,1... | collective-permute-start | bytes 393224 | tf_op jit(solution)/shard_map/ppermute | solution.py:198
  29.8 3.3 %collective-permute-done.9 = bf16[32,2048]{1,0:T(8,128)(2,1)S(1)} collective-permute-done((bf16[32,2048]{1,0:T(8,128)(2,1)S(1)}, bf16[32,2048]{1,0:T(8,128)(2,1)S(1)}, u32[]{:S(2)}, u32[]{:S(2)}) %collective-permute-start.9) | collective-permute-done | bytes 131104 | tf_op jit(solution)/shard_map/ppermute | solution.py:198
  33.7 1.6 %collective-permute-done.10 = bf16[32,2048]{1,0:T(8,128)(2,1)S(1)} collective-permute-done((bf16[32,2048]{1,0:T(8,128)(2,1)S(1)}, bf16[32,2048]{1,0:T(8,128)(2,1)S(1)}, u32[]{:S(2)}, u32[]{:S(2)}) %collective-permute-start.10) | collective-permute-done | bytes 131104 | tf_op jit(solution)/shard_map/ppermute | solution.py:198
  35.3 0.8 %collective-permute-start.15 = (bf16[32,2048]{1,0:T(8,128)(2,1)S(1)}, bf16[32,2048]{1,0:T(8,128)(2,1)S(1)}, u32[]{:S(2)}, u32[]{:S(2)}) collective-permute-start(bf16[32,2048]{1,0:T(8,128)(2,1)S(1)} %add_convert_fusion.2), channel_id=1, source_target_pairs={{0,4},{4,8},{8,12},{12,0},{1,5},{5,9},{9,13},{13,1},{2,6},{6,10},{... | collective-permute-start | bytes 393224 | tf_op jit(solution)/shard_map/ppermute | solution.py:198
  36.1 0.6 %collective-permute-start.11 = (bf16[32,2048]{1,0:T(8,128)(2,1)S(1)}, bf16[32,2048]{1,0:T(8,128)(2,1)S(1)}, u32[]{:S(2)}, u32[]{:S(2)}) collective-permute-start(bf16[32,2048]{1,0:T(8,128)(2,1)S(1)} %get-tuple-element.64), channel_id=1, source_target_pairs={{0,2},{2,0},{1,3},{3,1},{4,6},{6,4},{5,7},{7,5},{8,10},{10,8},{9,1... | collective-permute-start | bytes 393224 | tf_op jit(solution)/shard_map/ppermute | solution.py:198
  36.8 1.2 %collective-permute-done.12 = bf16[32,2048]{1,0:T(8,128)(2,1)S(1)} collective-permute-done((bf16[32,2048]{1,0:T(8,128)(2,1)S(1)}, bf16[32,2048]{1,0:T(8,128)(2,1)S(1)}, u32[]{:S(2)}, u32[]{:S(2)}) %collective-permute-start.12) | collective-permute-done | bytes 131104 | tf_op jit(solution)/shard_map/ppermute | solution.py:198
  38.0 2.2 %collective-permute-start.13 = (bf16[32,2048]{1,0:T(8,128)(2,1)S(1)}, bf16[32,2048]{1,0:T(8,128)(2,1)S(1)}, u32[]{:S(2)}, u32[]{:S(2)}) collective-permute-start(bf16[32,2048]{1,0:T(8,128)(2,1)S(1)} %add_convert_fusion), channel_id=1, source_target_pairs={{0,12},{4,0},{8,4},{12,8},{1,13},{5,1},{9,5},{13,9},{2,14},{6,2},{... | collective-permute-start | bytes 393224 | tf_op jit(solution)/shard_map/ppermute | solution.py:198
  40.2 2.9 %collective-permute-done.14.refs_2_ = bf16[32,2048]{1,0:T(8,128)(2,1)S(1)} collective-permute-done((bf16[32,2048]{1,0:T(8,128)(2,1)S(1)}, bf16[32,2048]{1,0:T(8,128)(2,1)S(1)}, u32[]{:S(2)}, u32[]{:S(2)}) %collective-permute-start.14) | collective-permute-done | bytes 131104 | tf_op jit(solution)/shard_map/ppermute | solution.py:198
  45.3 1.1 %mix.1 = bf16[128,2048]{1,0:T(8,128)(2,1)} custom-call(bf16[128,256]{1,0:T(8,128)(2,1)S(1)} %mixing.1.mixing_ref, bf16[32,2048]{1,0:T(8,128)(2,1)S(1)} %add_convert_fusion.1.refs_0_, bf16[32,2048]{1,0:T(8,128)(2,1)S(1)} %collective-permute-done.13.refs_1_, bf16[32,2048]{1,0:T(8,128)(2,1)S(1)} %collective-permute-done.14.refs_2_, ...), custom_call_target="tpu_custom_call" | custom-call | bytes 1572864 | tf_op jit(solution)/shard_map/mix/pallas_call | solution.py:17
  (37 shorter events, 5.3 us)
Async XLA Ops:
  0.0 2.2 %collective-permute-start.1 = (bf16[128,2048]{1,0:T(8,128)(2,1)}, bf16[128,2048]{1,0:T(8,128)(2,1)S(1)}, u32[]{:S(2)}, u32[]{:S(2)}) collective-permute-start(bf16[128,2048]{1,0:T(8,128)(2,1)} %tokens.1), channel_id=1, source_target_pairs={{0,1},{1,0},{2,3},{3,2},{4,5},{5,4},{6,7},{7,6},{8,9},{9,8},{10,11... | collective-permute-start | bytes 1572872 | tf_op jit(solution)/shard_map/ppermute | solution.py:198
  0.5 1.8 %collective-permute-start = (s32[8,128]{1,0:T(8,128)}, s32[8,128]{1,0:T(8,128)S(1)}, u32[]{:S(2)}, u32[]{:S(2)}) collective-permute-start(s32[8,128]{1,0:T(8,128)} %bitcast.7), channel_id=1, source_target_pairs={{0,1},{1,0},{2,3},{3,2},{4,5},{5,4},{6,7},{7,6},{8,9},{9,8},{10,11... | collective-permute-start | bytes 12296 | tf_op jit(solution)/shard_map/ppermute | solution.py:198
  2.6 9.2 %collective-permute-start.2 = (bf16[32,2048]{1,0:T(8,128)(2,1)S(1)}, bf16[32,2048]{1,0:T(8,128)(2,1)S(1)}, u32[]{:S(2)}, u32[]{:S(2)}) collective-permute-start(bf16[32,2048]{1,0:T(8,128)(2,1)S(1)} %get-tuple-element.40), channel_id=1, source_target_pairs={{0,12},{4,0},{8,4},{12,8},{1,13},{5,1},{9,5},{13,9},{2,14},{6,2},{... | collective-permute-start | bytes 393224 | tf_op jit(solution)/shard_map/ppermute | solution.py:198
  7.6 8.2 %collective-permute-start.3 = (bf16[32,2048]{1,0:T(8,128)(2,1)S(1)}, bf16[32,2048]{1,0:T(8,128)(2,1)S(1)}, u32[]{:S(2)}, u32[]{:S(2)}) collective-permute-start(bf16[32,2048]{1,0:T(8,128)(2,1)S(1)} %get-tuple-element.43), channel_id=1, source_target_pairs={{0,4},{4,8},{8,12},{12,0},{1,5},{5,9},{9,13},{13,1},{2,6},{6,10},{... | collective-permute-start | bytes 393224 | tf_op jit(solution)/shard_map/ppermute | solution.py:198
  7.6 11.8 %collective-permute-start.4 = (bf16[32,2048]{1,0:T(8,128)(2,1)S(1)}, bf16[32,2048]{1,0:T(8,128)(2,1)S(1)}, u32[]{:S(2)}, u32[]{:S(2)}) collective-permute-start(bf16[32,2048]{1,0:T(8,128)(2,1)S(1)} %get-tuple-element.44), channel_id=1, source_target_pairs={{0,8},{4,12},{8,0},{12,4},{1,9},{5,13},{9,1},{13,5},{2,10},{6,14},... | collective-permute-start | bytes 393224 | tf_op jit(solution)/shard_map/ppermute | solution.py:198
  8.6 15.9 %collective-permute-start.5 = (bf16[32,2048]{1,0:T(8,128)(2,1)S(1)}, bf16[32,2048]{1,0:T(8,128)(2,1)S(1)}, u32[]{:S(2)}, u32[]{:S(2)}) collective-permute-start(bf16[32,2048]{1,0:T(8,128)(2,1)S(1)} %get-tuple-element.41.after_ref.refs_0_), channel_id=1, source_target_pairs={{0,2},{2,0},{1,3},{3,1},{4,6},{6,4},{5,7},{7,5},{8,10},{10,8},{9,1... | collective-permute-start | bytes 393224 | tf_op jit(solution)/shard_map/ppermute | solution.py:198
  10.1 0.7 %copy-start.1 = (s32[128,8]{0,1:T(8,128)S(1)}, s32[128,8]{0,1:T(8,128)}, u32[]{:S(2)}) copy-start(s32[128,8]{0,1:T(8,128)} %param.7) | copy-start | bytes 12292
  10.8 0.7 %copy-start.2 = (s32[128,8]{0,1:T(8,128)S(1)}, s32[128,8]{0,1:T(8,128)}, u32[]{:S(2)}) copy-start(s32[128,8]{0,1:T(8,128)} %param.8) | copy-start | bytes 12292
  11.7 12.8 %collective-permute-start.8 = (bf16[32,2048]{1,0:T(8,128)(2,1)S(1)}, bf16[32,2048]{1,0:T(8,128)(2,1)S(1)}, u32[]{:S(2)}, u32[]{:S(2)}) collective-permute-start(bf16[32,2048]{1,0:T(8,128)(2,1)S(1)} %collective-permute-done.2.refs_3_), channel_id=1, source_target_pairs={{0,2},{2,0},{1,3},{3,1},{4,6},{6,4},{5,7},{7,5},{8,10},{10,8},{9,1... | collective-permute-start | bytes 393224 | tf_op jit(solution)/shard_map/ppermute | solution.py:198
  15.8 8.7 %collective-permute-start.6 = (bf16[32,2048]{1,0:T(8,128)(2,1)S(1)}, bf16[32,2048]{1,0:T(8,128)(2,1)S(1)}, u32[]{:S(2)}, u32[]{:S(2)}) collective-permute-start(bf16[32,2048]{1,0:T(8,128)(2,1)S(1)} %collective-permute-done.3.refs_1_), channel_id=1, source_target_pairs={{0,2},{2,0},{1,3},{3,1},{4,6},{6,4},{5,7},{7,5},{8,10},{10,8},{9,1... | collective-permute-start | bytes 393224 | tf_op jit(solution)/shard_map/ppermute | solution.py:198
  19.4 5.2 %collective-permute-start.7 = (bf16[32,2048]{1,0:T(8,128)(2,1)S(1)}, bf16[32,2048]{1,0:T(8,128)(2,1)S(1)}, u32[]{:S(2)}, u32[]{:S(2)}) collective-permute-start(bf16[32,2048]{1,0:T(8,128)(2,1)S(1)} %collective-permute-done.4.refs_2_), channel_id=1, source_target_pairs={{0,2},{2,0},{1,3},{3,1},{4,6},{6,4},{5,7},{7,5},{8,10},{10,8},{9,1... | collective-permute-start | bytes 393224 | tf_op jit(solution)/shard_map/ppermute | solution.py:198
  20.9 4.7 %copy-start = (bf16[1,512,4096]{2,1,0:T(8,128)(2,1)S(1)}, bf16[1,512,4096]{2,1,0:T(8,128)(2,1)}, u32[]{:S(2)}) copy-start(bf16[1,512,4096]{2,1,0:T(8,128)(2,1)} %param.11) | copy-start | bytes 12582916
  26.6 6.5 %collective-permute-start.9 = (bf16[32,2048]{1,0:T(8,128)(2,1)S(1)}, bf16[32,2048]{1,0:T(8,128)(2,1)S(1)}, u32[]{:S(2)}, u32[]{:S(2)}) collective-permute-start(bf16[32,2048]{1,0:T(8,128)(2,1)S(1)} %get-tuple-element.61), channel_id=1, source_target_pairs={{0,2},{2,0},{1,3},{3,1},{4,6},{6,4},{5,7},{7,5},{8,10},{10,8},{9,1... | collective-permute-start | bytes 393224 | tf_op jit(solution)/shard_map/ppermute | solution.py:198
  27.7 7.6 %collective-permute-start.10 = (bf16[32,2048]{1,0:T(8,128)(2,1)S(1)}, bf16[32,2048]{1,0:T(8,128)(2,1)S(1)}, u32[]{:S(2)}, u32[]{:S(2)}) collective-permute-start(bf16[32,2048]{1,0:T(8,128)(2,1)S(1)} %get-tuple-element.63), channel_id=1, source_target_pairs={{0,2},{2,0},{1,3},{3,1},{4,6},{6,4},{5,7},{7,5},{8,10},{10,8},{9,1... | collective-permute-start | bytes 393224 | tf_op jit(solution)/shard_map/ppermute | solution.py:198
  29.2 8.7 %collective-permute-start.12 = (bf16[32,2048]{1,0:T(8,128)(2,1)S(1)}, bf16[32,2048]{1,0:T(8,128)(2,1)S(1)}, u32[]{:S(2)}, u32[]{:S(2)}) collective-permute-start(bf16[32,2048]{1,0:T(8,128)(2,1)S(1)} %get-tuple-element.66), channel_id=1, source_target_pairs={{0,2},{2,0},{1,3},{3,1},{4,6},{6,4},{5,7},{7,5},{8,10},{10,8},{9,1... | collective-permute-start | bytes 393224 | tf_op jit(solution)/shard_map/ppermute | solution.py:198
  33.2 10.0 %collective-permute-start.14 = (bf16[32,2048]{1,0:T(8,128)(2,1)S(1)}, bf16[32,2048]{1,0:T(8,128)(2,1)S(1)}, u32[]{:S(2)}, u32[]{:S(2)}) collective-permute-start(bf16[32,2048]{1,0:T(8,128)(2,1)S(1)} %add_convert_fusion.3), channel_id=1, source_target_pairs={{0,8},{4,12},{8,0},{12,4},{1,9},{5,13},{9,1},{13,5},{2,10},{6,14},... | collective-permute-start | bytes 393224 | tf_op jit(solution)/shard_map/ppermute | solution.py:198
  35.3 8.5 %collective-permute-start.15 = (bf16[32,2048]{1,0:T(8,128)(2,1)S(1)}, bf16[32,2048]{1,0:T(8,128)(2,1)S(1)}, u32[]{:S(2)}, u32[]{:S(2)}) collective-permute-start(bf16[32,2048]{1,0:T(8,128)(2,1)S(1)} %add_convert_fusion.2), channel_id=1, source_target_pairs={{0,4},{4,8},{8,12},{12,0},{1,5},{5,9},{9,13},{13,1},{2,6},{6,10},{... | collective-permute-start | bytes 393224 | tf_op jit(solution)/shard_map/ppermute | solution.py:198
  36.1 7.0 %collective-permute-start.11 = (bf16[32,2048]{1,0:T(8,128)(2,1)S(1)}, bf16[32,2048]{1,0:T(8,128)(2,1)S(1)}, u32[]{:S(2)}, u32[]{:S(2)}) collective-permute-start(bf16[32,2048]{1,0:T(8,128)(2,1)S(1)} %get-tuple-element.64), channel_id=1, source_target_pairs={{0,2},{2,0},{1,3},{3,1},{4,6},{6,4},{5,7},{7,5},{8,10},{10,8},{9,1... | collective-permute-start | bytes 393224 | tf_op jit(solution)/shard_map/ppermute | solution.py:198
  38.0 6.1 %collective-permute-start.13 = (bf16[32,2048]{1,0:T(8,128)(2,1)S(1)}, bf16[32,2048]{1,0:T(8,128)(2,1)S(1)}, u32[]{:S(2)}, u32[]{:S(2)}) collective-permute-start(bf16[32,2048]{1,0:T(8,128)(2,1)S(1)} %add_convert_fusion), channel_id=1, source_target_pairs={{0,12},{4,0},{8,4},{12,8},{1,13},{5,1},{9,5},{13,9},{2,14},{6,2},{... | collective-permute-start | bytes 393224 | tf_op jit(solution)/shard_map/ppermute | solution.py:198
  43.1 1.3 %collective-permute-start.18 = (bf16[16,2048]{1,0:T(8,128)(2,1)S(1)}, bf16[16,2048]{1,0:T(8,128)(2,1)S(1)}, u32[]{:S(2)}, u32[]{:S(2)}) collective-permute-start(bf16[16,2048]{1,0:T(8,128)(2,1)S(1)} %slice.18), channel_id=1, source_target_pairs={{0,1},{1,0},{2,3},{3,2},{4,5},{5,4},{6,7},{7,6},{8,9},{9,8},{10,11... | collective-permute-start | bytes 196616 | tf_op jit(solution)/shard_map/ppermute | solution.py:198
  43.2 1.5 %collective-permute-start.16 = (bf16[16,2048]{1,0:T(8,128)(2,1)S(1)}, bf16[16,2048]{1,0:T(8,128)(2,1)S(1)}, u32[]{:S(2)}, u32[]{:S(2)}) collective-permute-start(bf16[16,2048]{1,0:T(8,128)(2,1)S(1)} %slice.16), channel_id=1, source_target_pairs={{0,1},{1,0},{2,3},{3,2},{4,5},{5,4},{6,7},{7,6},{8,9},{9,8},{10,11... | collective-permute-start | bytes 196616 | tf_op jit(solution)/shard_map/ppermute | solution.py:198
  43.8 1.3 %collective-permute-start.19 = (bf16[16,2048]{1,0:T(8,128)(2,1)S(1)}, bf16[16,2048]{1,0:T(8,128)(2,1)S(1)}, u32[]{:S(2)}, u32[]{:S(2)}) collective-permute-start(bf16[16,2048]{1,0:T(8,128)(2,1)S(1)} %slice.19), channel_id=1, source_target_pairs={{0,1},{1,0},{2,3},{3,2},{4,5},{5,4},{6,7},{7,6},{8,9},{9,8},{10,11... | collective-permute-start | bytes 196616 | tf_op jit(solution)/shard_map/ppermute | solution.py:198
  44.1 1.3 %collective-permute-start.17 = (bf16[16,2048]{1,0:T(8,128)(2,1)S(1)}, bf16[16,2048]{1,0:T(8,128)(2,1)S(1)}, u32[]{:S(2)}, u32[]{:S(2)}) collective-permute-start(bf16[16,2048]{1,0:T(8,128)(2,1)S(1)} %slice.17), channel_id=1, source_target_pairs={{0,1},{1,0},{2,3},{3,2},{4,5},{5,4},{6,7},{7,6},{8,9},{9,8},{10,11... | collective-permute-start | bytes 196616 | tf_op jit(solution)/shard_map/ppermute | solution.py:198

commit v7 on v6

--- a/solution.py
+++ b/solution.py
@@ -58,14 +58,17 @@
         outs[s][u * CAP : (u + 1) * CAP, :] = rows[s * CAP : (s + 1) * CAP]
 
 
-def select_own_kernel(n_pool, n_pair, routes, tokens, *refs):
-    outs, held, held_routes, sems = refs[:n_pool], refs[n_pool], refs[n_pool + 1], refs[n_pool + 2]
+def select_own_kernel(n_pool, n_pair, routes, weights, tokens, *refs):
+    outs, held_routes, held_weights, held, sems = refs[:n_pool], *refs[n_pool:]
     first = pltpu.make_async_copy(routes, held_routes, sems.at[0])
     second = pltpu.make_async_copy(tokens, held, sems.at[1])
+    third = pltpu.make_async_copy(weights, held_weights, sems.at[2])
     first.start()
     second.start()
+    third.start()
     first.wait()
     select(held_routes, held, outs, n_pool, n_pair, 0, second)
+    third.wait()
 
 
 def select_other_kernel(n_pool, n_pair, *refs):
@@ -105,9 +108,9 @@
     return jnp.concatenate([r[...] for r in refs], axis=0)
 
 
-def near_kernel(n_tp, tiles, gate_ref, up_ref, *refs):
-    rows = refs[:-7]
-    gate_out, up_out, gate_far, up_far, gate_near, up_near, sems = refs[-7:]
+def near_kernel(n_tp, tiles, gate_ref, up_ref, down_ref, *refs):
+    rows = refs[:-8]
+    gate_out, up_out, gate_far, up_far, down_out, gate_near, up_near, sems = refs[-8:]
     width = rows[0].shape[1]
     tp = lax.axis_index("tp")
     depth = width // tiles
@@ -125,6 +128,11 @@
             for j, (ref, _, out) in enumerate(pairs):
                 sem = sems.at[2 * tiles + ((k - 1) * 2 + i) * 2 + j]
                 far.append(pltpu.make_async_copy(ref.at[at, :], out.at[to, :], sem))
+    for k in range(1, n_tp):
+        at = pl.ds(pl.multiple_of(lax.rem(tp + k, n_tp) * width, width), width)
+        to = pl.ds((k - 1) * width, width)
+        sem = sems.at[2 * tiles + 4 * (n_tp - 1) + k - 1]
+        far.append(pltpu.make_async_copy(down_ref.at[:, at], down_out.at[:, to], sem))
     for c in near + far:
         c.start()
     block = stacked(rows)
@@ -146,8 +154,7 @@
     far = n_tp - 1
     rows = [refs[k * n_chunks : (k + 1) * n_chunks] for k in range(far)]
     hidden_ref, outs = refs[far * n_chunks], refs[far * n_chunks + 1 :]
-    width = down_ref.shape[1] // n_tp
-    tp = lax.axis_index("tp")
+    width = down_ref.shape[1] // far
     gate, up = gate_in[...], up_in[...]
     for k in range(1, n_tp):
         at = pl.ds((k - 1) * width, width)
@@ -157,7 +164,7 @@
     hidden = (gate / (1.0 + jnp.exp(-gate)) * up).astype(BF16)
     hidden_ref[...] = hidden
     for k in range(1, n_tp):
-        at = pl.ds(pl.multiple_of(lax.rem(tp + k, n_tp) * width, width), width)
+        at = pl.ds((k - 1) * width, width)
         part = jnp.dot(hidden, down_ref[:, at], preferred_element_type=F32).astype(BF16)
         put(outs[(k - 1) * n_chunks : k * n_chunks], part)
 
@@ -225,18 +232,14 @@
 
     far_tokens = [turn(tokens, "pair", -u) for u in range(1, n_pair)]
     far_routes = [turn(routes_t, "pair", -u) for u in range(1, n_pair)]
-    leaving = call(
+    *leaving, near_routes, near_weights = call(
         functools.partial(select_own_kernel, n_pool, n_pair),
         "select_own",
-        [shape(rows, width)] * n_pool,
-        [HBM, HBM],
-        (pltpu.with_memory_space_constraint(routes_t, pltpu.HBM), pltpu.with_memory_space_constraint(tokens, pltpu.HBM)),
+        [shape(rows, width)] * n_pool + [shape(*x.shape, x.dtype) for x in (routes_t, weights_t)],
+        [HBM] * 3,
+        [pltpu.with_memory_space_constraint(x, pltpu.HBM) for x in (routes_t, weights_t, tokens)],
         2 * 2 * streams * width,
-        scratch=[
-            pltpu.VMEM((streams, width), BF16),
-            pltpu.VMEM(routes_t.shape, routes.dtype),
-            pltpu.SemaphoreType.DMA((2,)),
-        ],
+        scratch=[pltpu.VMEM((streams, width), BF16), pltpu.SemaphoreType.DMA((3,))],
     )
     leaving = call(
         functools.partial(select_other_kernel, n_pool, n_pair),
@@ -254,7 +257,7 @@
         "mixing",
         [shape(streams, 2 * slots)],
         [VMEM, VMEM, VMEM],
-        (leaving[0], routes_t, weights_t),
+        (leaving[0], near_routes, near_weights),
         4 * 10 * streams * slots,
     )
 
@@ -266,24 +269,24 @@
     far = [[turn(b, "tp", k) for b in near] for k in range(1, n_tp)]
     tiles = 4 if width % 1024 == 0 else 1
     rest = (n_tp - 1) * width
-    gate, up, gate_far, up_far = call(
+    gate, up, gate_far, up_far, down_far = call(
         functools.partial(near_kernel, n_tp, tiles),
         "near",
-        [shape(slots, hidden_units, F32)] * 2 + [shape(rest, hidden_units)] * 2,
-        [HBM] * 2 + [VMEM] * n_pool,
-        (gate_mat, up_mat, *near),
+        [shape(slots, hidden_units, F32)] * 2 + [shape(rest, hidden_units)] * 2 + [shape(hidden_units, rest)],
+        [HBM] * 3 + [VMEM] * n_pool,
+        (*[pltpu.with_memory_space_constraint(w, pltpu.HBM) for w in (gate_mat, up_mat, down_mat)], *near),
         2 * 2 * (w_gate.size + w_up.size),
         4 * slots * width * hidden_units,
         scratch=[pltpu.VMEM((width, hidden_units), BF16)] * 2
-        + [pltpu.SemaphoreType.DMA((2 * tiles + 4 * (n_tp - 1),))],
-        vmem=48,
+        + [pltpu.SemaphoreType.DMA((2 * tiles + 5 * (n_tp - 1),))],
+        vmem=24,
     )
     hidden, *sent = call(
         functools.partial(far_kernel, n_tp, n_pool),
         "far",
         [shape(slots, hidden_units)] + [shape(rows, width)] * (n_pool * (n_tp - 1)),
         [VMEM] * (5 + n_pool * (n_tp - 1)),
-        (gate_far, up_far, down_mat, gate, up, *sum(far, [])),
+        (gate_far, up_far, down_far, gate, up, *sum(far, [])),
         8 * width * hidden_units,
         6 * slots * width * hidden_units,
     )

time: 46.7 us -> 46.6 us (level)
  local copies, waits for them, and re-layouts: 2.34 us -> 0.3 us
  waiting for transfers between devices: 15.5 us -> 17.1 us
  Pallas kernels: 8.22 us -> 8.8 us
    unnamed x6 -> x2, local copies, waits for them, and re-layouts: 2.31 us -> 0.28 us
    ppermute x20, waiting for transfers between devices: 15.5 us -> 17.1 us  [turn(): return lax.ppermute(x, axis, [(i, (i + shift) % n) for i in range(n)])]
    pallas_call x7, Pallas kernels: 8.22 us -> 8.8 us  [call(): pl.pallas_call(kernel, out_shape=outs, in_specs=in_specs, out_specs=[to]...]
  transfers between devices with their start and end apart: 20 -> 20, of which waited for: 11 -> 12; matrix products, arithmetic and copies ran while one was open for 0% -> 0% of each run, Pallas kernels for 12% -> 13%
where the time goes in v7:
time: 46.6 us; the launch traced here: 46.5 us
  starting transfers between devices  20 us (43%)
  waiting for transfers between devices  17.1 us (37%)
  Pallas kernels  8.8 us (19%)
    ppermute x20, starting transfers between devices, turn(): return lax.ppermute(x, axis, [(i, (i + shift) % n) for i in range(n)])  20 us
    ppermute x20, waiting for transfers between devices, turn(): return lax.ppermute(x, axis, [(i, (i + shift) % n) for i in range(n)])  17.1 us
    pallas_call x7, Pallas kernels, call(): pl.pallas_call(kernel, out_shape=outs, in_specs=in_specs, out_specs=[to]...  8.8 us
  transfers between devices with their start and end apart: 20, of which 12 were waited for; matrix products, arithmetic and copies ran while one was open for 0% of the time, Pallas kernels for 13%

profile of v7, /device:TPU:0, one launch (start us, length us, event | category | flops | bytes accessed | tf_op | source)
XLA Modules:
  0.0 46.5 jit_solution(10533126765283085634)
XLA Ops:
  0.5 1.3 %select_own.1 = (bf16[32,2048]{1,0:T(8,128)(2,1)S(1)}, bf16[32,2048]{1,0:T(8,128)(2,1)S(1)}, bf16[32,2048]{1,0:T(8,128)(2,1)S(1)}, bf16[32,2048]{1,0:T(8,128)(2,...) custom-call(s32[8,128]{1,0:T(8,128)} %bitcast.11, s32[8,128]{1,0:T(8,128)} %bitcast.9, bf16[128,2048]{1,0:T(8,128)(2,1)} %tokens.1), custom_call_target="tpu_custom_call" | custom-call | bytes 1048576 | tf_op jit(solution)/shard_map/select_own/pallas_call | solution.py:17
  2.6 5.0 %collective-permute-start.2 = (bf16[32,2048]{1,0:T(8,128)(2,1)S(1)}, bf16[32,2048]{1,0:T(8,128)(2,1)S(1)}, u32[]{:S(2)}, u32[]{:S(2)}) collective-permute-start(bf16[32,2048]{1,0:T(8,128)(2,1)S(1)} %get-tuple-element.43), channel_id=1, source_target_pairs={{0,12},{4,0},{8,4},{12,8},{1,13},{5,1},{9,5},{13,9},{2,14},{6,2},{... | collective-permute-start | bytes 393224 | tf_op jit(solution)/shard_map/ppermute | solution.py:205
  7.6 1.0 %collective-permute-start.4 = (bf16[32,2048]{1,0:T(8,128)(2,1)S(1)}, bf16[32,2048]{1,0:T(8,128)(2,1)S(1)}, u32[]{:S(2)}, u32[]{:S(2)}) collective-permute-start(bf16[32,2048]{1,0:T(8,128)(2,1)S(1)} %get-tuple-element.49), channel_id=1, source_target_pairs={{0,8},{4,12},{8,0},{12,4},{1,9},{5,13},{9,1},{13,5},{2,10},{6,14},... | collective-permute-start | bytes 393224 | tf_op jit(solution)/shard_map/ppermute | solution.py:205
  8.6 1.5 %collective-permute-start.5 = (bf16[32,2048]{1,0:T(8,128)(2,1)S(1)}, bf16[32,2048]{1,0:T(8,128)(2,1)S(1)}, u32[]{:S(2)}, u32[]{:S(2)}) collective-permute-start(bf16[32,2048]{1,0:T(8,128)(2,1)S(1)} %get-tuple-element.44.after_ref.refs_0_), channel_id=1, source_target_pairs={{0,2},{2,0},{1,3},{3,1},{4,6},{6,4},{5,7},{7,5},{8,10},{10,8},{9,1... | collective-permute-start | bytes 393224 | tf_op jit(solution)/shard_map/ppermute | solution.py:205
  10.3 1.1 %collective-permute-done.2.refs_3_ = bf16[32,2048]{1,0:T(8,128)(2,1)S(1)} collective-permute-done((bf16[32,2048]{1,0:T(8,128)(2,1)S(1)}, bf16[32,2048]{1,0:T(8,128)(2,1)S(1)}, u32[]{:S(2)}, u32[]{:S(2)}) %collective-permute-start.2) | collective-permute-done | bytes 131104 | tf_op jit(solution)/shard_map/ppermute | solution.py:205
  11.5 1.5 %collective-permute-start.8 = (bf16[32,2048]{1,0:T(8,128)(2,1)S(1)}, bf16[32,2048]{1,0:T(8,128)(2,1)S(1)}, u32[]{:S(2)}, u32[]{:S(2)}) collective-permute-start(bf16[32,2048]{1,0:T(8,128)(2,1)S(1)} %collective-permute-done.2.refs_3_), channel_id=1, source_target_pairs={{0,2},{2,0},{1,3},{3,1},{4,6},{6,4},{5,7},{7,5},{8,10},{10,8},{9,1... | collective-permute-start | bytes 393224 | tf_op jit(solution)/shard_map/ppermute | solution.py:205
  13.0 2.8 %collective-permute-done.3.refs_1_ = bf16[32,2048]{1,0:T(8,128)(2,1)S(1)} collective-permute-done((bf16[32,2048]{1,0:T(8,128)(2,1)S(1)}, bf16[32,2048]{1,0:T(8,128)(2,1)S(1)}, u32[]{:S(2)}, u32[]{:S(2)}) %collective-permute-start.3) | collective-permute-done | bytes 131104 | tf_op jit(solution)/shard_map/ppermute | solution.py:205
  15.8 1.5 %collective-permute-start.6 = (bf16[32,2048]{1,0:T(8,128)(2,1)S(1)}, bf16[32,2048]{1,0:T(8,128)(2,1)S(1)}, u32[]{:S(2)}, u32[]{:S(2)}) collective-permute-start(bf16[32,2048]{1,0:T(8,128)(2,1)S(1)} %collective-permute-done.3.refs_1_), channel_id=1, source_target_pairs={{0,2},{2,0},{1,3},{3,1},{4,6},{6,4},{5,7},{7,5},{8,10},{10,8},{9,1... | collective-permute-start | bytes 393224 | tf_op jit(solution)/shard_map/ppermute | solution.py:205
  17.3 2.1 %collective-permute-done.4.refs_2_ = bf16[32,2048]{1,0:T(8,128)(2,1)S(1)} collective-permute-done((bf16[32,2048]{1,0:T(8,128)(2,1)S(1)}, bf16[32,2048]{1,0:T(8,128)(2,1)S(1)}, u32[]{:S(2)}, u32[]{:S(2)}) %collective-permute-start.4) | collective-permute-done | bytes 131104 | tf_op jit(solution)/shard_map/ppermute | solution.py:205
  19.4 1.5 %collective-permute-start.7 = (bf16[32,2048]{1,0:T(8,128)(2,1)S(1)}, bf16[32,2048]{1,0:T(8,128)(2,1)S(1)}, u32[]{:S(2)}, u32[]{:S(2)}) collective-permute-start(bf16[32,2048]{1,0:T(8,128)(2,1)S(1)} %collective-permute-done.4.refs_2_), channel_id=1, source_target_pairs={{0,2},{2,0},{1,3},{3,1},{4,6},{6,4},{5,7},{7,5},{8,10},{10,8},{9,1... | collective-permute-start | bytes 393224 | tf_op jit(solution)/shard_map/ppermute | solution.py:205
  20.9 4.2 %near.1 = (f32[128,512]{1,0:T(8,128)S(1)}, f32[128,512]{1,0:T(8,128)S(1)}, bf16[2048,512]{1,0:T(8,128)(2,1)S(1)}, bf16[2048,512]{1,0:T(8,128)(2,1)S(1)}, bf16[512,2048]{1,0:T(8,128)(2,1)S(1)}) custom-call(bf16[4096,512]{1,0:T(8,128)(2,1)} %bitcast.7, bf16[4096,512]{1,0:T(8,128)(2,1)} %bitcast.8, bf16[512,4096]{1,0:T(8,128)(2,1)} %bitcast.5, ...), custom_call_target="tpu_custom_call" | custom-call | flops 536870912 | bytes 16777216 | tf_op jit(solution)/shard_map/near/pallas_call | solution.py:17
  25.1 1.1 %far.1 = (bf16[128,512]{1,0:T(8,128)(2,1)S(1)}, bf16[32,2048]{1,0:T(8,128)(2,1)S(1)}, bf16[32,2048]{1,0:T(8,128)(2,1)S(1)}, bf16[32,2048]{1,0:T(8,128)(2,1)S(1)}, bf16[32,2048]{1,0:T(8,128)(2,1)S(1)}) custom-call(bf16[2048,512]{1,0:T(8,128)(2,1)S(1)} %get-tuple-element.51.gate_ref, bf16[2048,512]{1,0:T(8,128)(2,1)S(1)} %get-tuple-element.52.up_ref, ...), custom_call_target="tpu_custom_call" | custom-call | flops 805306368 | bytes 8388608 | tf_op jit(solution)/shard_map/far/pallas_call | solution.py:17
  26.3 0.7 %collective-permute-start.9 = (bf16[32,2048]{1,0:T(8,128)(2,1)S(1)}, bf16[32,2048]{1,0:T(8,128)(2,1)S(1)}, u32[]{:S(2)}, u32[]{:S(2)}) collective-permute-start(bf16[32,2048]{1,0:T(8,128)(2,1)S(1)} %get-tuple-element.67), channel_id=1, source_target_pairs={{0,2},{2,0},{1,3},{3,1},{4,6},{6,4},{5,7},{7,5},{8,10},{10,8},{9,1... | collective-permute-start | bytes 393224 | tf_op jit(solution)/shard_map/ppermute | solution.py:205
  27.7 1.1 %collective-permute-start.10 = (bf16[32,2048]{1,0:T(8,128)(2,1)S(1)}, bf16[32,2048]{1,0:T(8,128)(2,1)S(1)}, u32[]{:S(2)}, u32[]{:S(2)}) collective-permute-start(bf16[32,2048]{1,0:T(8,128)(2,1)S(1)} %get-tuple-element.69), channel_id=1, source_target_pairs={{0,2},{2,0},{1,3},{3,1},{4,6},{6,4},{5,7},{7,5},{8,10},{10,8},{9,1... | collective-permute-start | bytes 393224 | tf_op jit(solution)/shard_map/ppermute | solution.py:205
  28.9 1.0 %collective-permute-start.12 = (bf16[32,2048]{1,0:T(8,128)(2,1)S(1)}, bf16[32,2048]{1,0:T(8,128)(2,1)S(1)}, u32[]{:S(2)}, u32[]{:S(2)}) collective-permute-start(bf16[32,2048]{1,0:T(8,128)(2,1)S(1)} %get-tuple-element.72), channel_id=1, source_target_pairs={{0,2},{2,0},{1,3},{3,1},{4,6},{6,4},{5,7},{7,5},{8,10},{10,8},{9,1... | collective-permute-start | bytes 393224 | tf_op jit(solution)/shard_map/ppermute | solution.py:205
  29.8 2.8 %collective-permute-done.9 = bf16[32,2048]{1,0:T(8,128)(2,1)S(1)} collective-permute-done((bf16[32,2048]{1,0:T(8,128)(2,1)S(1)}, bf16[32,2048]{1,0:T(8,128)(2,1)S(1)}, u32[]{:S(2)}, u32[]{:S(2)}) %collective-permute-start.9) | collective-permute-done | bytes 131104 | tf_op jit(solution)/shard_map/ppermute | solution.py:205
  32.7 0.5 %collective-permute-start.14 = (bf16[32,2048]{1,0:T(8,128)(2,1)S(1)}, bf16[32,2048]{1,0:T(8,128)(2,1)S(1)}, u32[]{:S(2)}, u32[]{:S(2)}) collective-permute-start(bf16[32,2048]{1,0:T(8,128)(2,1)S(1)} %add_convert_fusion.3), channel_id=1, source_target_pairs={{0,8},{4,12},{8,0},{12,4},{1,9},{5,13},{9,1},{13,5},{2,10},{6,14},... | collective-permute-start | bytes 393224 | tf_op jit(solution)/shard_map/ppermute | solution.py:205
  33.1 2.2 %collective-permute-done.10 = bf16[32,2048]{1,0:T(8,128)(2,1)S(1)} collective-permute-done((bf16[32,2048]{1,0:T(8,128)(2,1)S(1)}, bf16[32,2048]{1,0:T(8,128)(2,1)S(1)}, u32[]{:S(2)}, u32[]{:S(2)}) %collective-permute-start.10) | collective-permute-done | bytes 131104 | tf_op jit(solution)/shard_map/ppermute | solution.py:205
  35.6 0.8 %collective-permute-start.11 = (bf16[32,2048]{1,0:T(8,128)(2,1)S(1)}, bf16[32,2048]{1,0:T(8,128)(2,1)S(1)}, u32[]{:S(2)}, u32[]{:S(2)}) collective-permute-start(bf16[32,2048]{1,0:T(8,128)(2,1)S(1)} %get-tuple-element.70), channel_id=1, source_target_pairs={{0,2},{2,0},{1,3},{3,1},{4,6},{6,4},{5,7},{7,5},{8,10},{10,8},{9,1... | collective-permute-start | bytes 393224 | tf_op jit(solution)/shard_map/ppermute | solution.py:205
  36.4 1.3 %collective-permute-done.12 = bf16[32,2048]{1,0:T(8,128)(2,1)S(1)} collective-permute-done((bf16[32,2048]{1,0:T(8,128)(2,1)S(1)}, bf16[32,2048]{1,0:T(8,128)(2,1)S(1)}, u32[]{:S(2)}, u32[]{:S(2)}) %collective-permute-start.12) | collective-permute-done | bytes 131104 | tf_op jit(solution)/shard_map/ppermute | solution.py:205
  37.7 2.3 %collective-permute-start.13 = (bf16[32,2048]{1,0:T(8,128)(2,1)S(1)}, bf16[32,2048]{1,0:T(8,128)(2,1)S(1)}, u32[]{:S(2)}, u32[]{:S(2)}) collective-permute-start(bf16[32,2048]{1,0:T(8,128)(2,1)S(1)} %add_convert_fusion), channel_id=1, source_target_pairs={{0,12},{4,0},{8,4},{12,8},{1,13},{5,1},{9,5},{13,9},{2,14},{6,2},{... | collective-permute-start | bytes 393224 | tf_op jit(solution)/shard_map/ppermute | solution.py:205
  40.0 3.0 %collective-permute-done.14.refs_2_ = bf16[32,2048]{1,0:T(8,128)(2,1)S(1)} collective-permute-done((bf16[32,2048]{1,0:T(8,128)(2,1)S(1)}, bf16[32,2048]{1,0:T(8,128)(2,1)S(1)}, u32[]{:S(2)}, u32[]{:S(2)}) %collective-permute-start.14) | collective-permute-done | bytes 131104 | tf_op jit(solution)/shard_map/ppermute | solution.py:205
  43.1 0.6 %collective-permute-start.16 = (bf16[16,2048]{1,0:T(8,128)(2,1)S(1)}, bf16[16,2048]{1,0:T(8,128)(2,1)S(1)}, u32[]{:S(2)}, u32[]{:S(2)}) collective-permute-start(bf16[16,2048]{1,0:T(8,128)(2,1)S(1)} %slice.16), channel_id=1, source_target_pairs={{0,1},{1,0},{2,3},{3,2},{4,5},{5,4},{6,7},{7,6},{8,9},{9,8},{10,11... | collective-permute-start | bytes 196616 | tf_op jit(solution)/shard_map/ppermute | solution.py:205
  45.4 1.1 %mix.1 = bf16[128,2048]{1,0:T(8,128)(2,1)} custom-call(bf16[128,256]{1,0:T(8,128)(2,1)S(1)} %mixing.1.mixing_ref, bf16[32,2048]{1,0:T(8,128)(2,1)S(1)} %add_convert_fusion.1.refs_0_, bf16[32,2048]{1,0:T(8,128)(2,1)S(1)} %collective-permute-done.13.refs_1_, bf16[32,2048]{1,0:T(8,128)(2,1)S(1)} %collective-permute-done.14.refs_2_, ...), custom_call_target="tpu_custom_call" | custom-call | bytes 1572864 | tf_op jit(solution)/shard_map/mix/pallas_call | solution.py:17
  (33 shorter events, 4.3 us)
Async XLA Ops:
  0.0 2.2 %collective-permute-start.1 = (bf16[128,2048]{1,0:T(8,128)(2,1)}, bf16[128,2048]{1,0:T(8,128)(2,1)S(1)}, u32[]{:S(2)}, u32[]{:S(2)}) collective-permute-start(bf16[128,2048]{1,0:T(8,128)(2,1)} %tokens.1), channel_id=1, source_target_pairs={{0,1},{1,0},{2,3},{3,2},{4,5},{5,4},{6,7},{7,6},{8,9},{9,8},{10,11... | collective-permute-start | bytes 1572872 | tf_op jit(solution)/shard_map/ppermute | solution.py:205
  0.5 1.8 %collective-permute-start = (s32[8,128]{1,0:T(8,128)}, s32[8,128]{1,0:T(8,128)S(1)}, u32[]{:S(2)}, u32[]{:S(2)}) collective-permute-start(s32[8,128]{1,0:T(8,128)} %bitcast.10), channel_id=1, source_target_pairs={{0,1},{1,0},{2,3},{3,2},{4,5},{5,4},{6,7},{7,6},{8,9},{9,8},{10,11... | collective-permute-start | bytes 12296 | tf_op jit(solution)/shard_map/ppermute | solution.py:205
  2.6 8.9 %collective-permute-start.2 = (bf16[32,2048]{1,0:T(8,128)(2,1)S(1)}, bf16[32,2048]{1,0:T(8,128)(2,1)S(1)}, u32[]{:S(2)}, u32[]{:S(2)}) collective-permute-start(bf16[32,2048]{1,0:T(8,128)(2,1)S(1)} %get-tuple-element.43), channel_id=1, source_target_pairs={{0,12},{4,0},{8,4},{12,8},{1,13},{5,1},{9,5},{13,9},{2,14},{6,2},{... | collective-permute-start | bytes 393224 | tf_op jit(solution)/shard_map/ppermute | solution.py:205
  7.6 8.2 %collective-permute-start.3 = (bf16[32,2048]{1,0:T(8,128)(2,1)S(1)}, bf16[32,2048]{1,0:T(8,128)(2,1)S(1)}, u32[]{:S(2)}, u32[]{:S(2)}) collective-permute-start(bf16[32,2048]{1,0:T(8,128)(2,1)S(1)} %get-tuple-element.48), channel_id=1, source_target_pairs={{0,4},{4,8},{8,12},{12,0},{1,5},{5,9},{9,13},{13,1},{2,6},{6,10},{... | collective-permute-start | bytes 393224 | tf_op jit(solution)/shard_map/ppermute | solution.py:205
  7.6 11.8 %collective-permute-start.4 = (bf16[32,2048]{1,0:T(8,128)(2,1)S(1)}, bf16[32,2048]{1,0:T(8,128)(2,1)S(1)}, u32[]{:S(2)}, u32[]{:S(2)}) collective-permute-start(bf16[32,2048]{1,0:T(8,128)(2,1)S(1)} %get-tuple-element.49), channel_id=1, source_target_pairs={{0,8},{4,12},{8,0},{12,4},{1,9},{5,13},{9,1},{13,5},{2,10},{6,14},... | collective-permute-start | bytes 393224 | tf_op jit(solution)/shard_map/ppermute | solution.py:205
  8.6 16.5 %collective-permute-start.5 = (bf16[32,2048]{1,0:T(8,128)(2,1)S(1)}, bf16[32,2048]{1,0:T(8,128)(2,1)S(1)}, u32[]{:S(2)}, u32[]{:S(2)}) collective-permute-start(bf16[32,2048]{1,0:T(8,128)(2,1)S(1)} %get-tuple-element.44.after_ref.refs_0_), channel_id=1, source_target_pairs={{0,2},{2,0},{1,3},{3,1},{4,6},{6,4},{5,7},{7,5},{8,10},{10,8},{9,1... | collective-permute-start | bytes 393224 | tf_op jit(solution)/shard_map/ppermute | solution.py:205
  11.5 13.6 %collective-permute-start.8 = (bf16[32,2048]{1,0:T(8,128)(2,1)S(1)}, bf16[32,2048]{1,0:T(8,128)(2,1)S(1)}, u32[]{:S(2)}, u32[]{:S(2)}) collective-permute-start(bf16[32,2048]{1,0:T(8,128)(2,1)S(1)} %collective-permute-done.2.refs_3_), channel_id=1, source_target_pairs={{0,2},{2,0},{1,3},{3,1},{4,6},{6,4},{5,7},{7,5},{8,10},{10,8},{9,1... | collective-permute-start | bytes 393224 | tf_op jit(solution)/shard_map/ppermute | solution.py:205
  15.8 9.3 %collective-permute-start.6 = (bf16[32,2048]{1,0:T(8,128)(2,1)S(1)}, bf16[32,2048]{1,0:T(8,128)(2,1)S(1)}, u32[]{:S(2)}, u32[]{:S(2)}) collective-permute-start(bf16[32,2048]{1,0:T(8,128)(2,1)S(1)} %collective-permute-done.3.refs_1_), channel_id=1, source_target_pairs={{0,2},{2,0},{1,3},{3,1},{4,6},{6,4},{5,7},{7,5},{8,10},{10,8},{9,1... | collective-permute-start | bytes 393224 | tf_op jit(solution)/shard_map/ppermute | solution.py:205
  19.4 5.8 %collective-permute-start.7 = (bf16[32,2048]{1,0:T(8,128)(2,1)S(1)}, bf16[32,2048]{1,0:T(8,128)(2,1)S(1)}, u32[]{:S(2)}, u32[]{:S(2)}) collective-permute-start(bf16[32,2048]{1,0:T(8,128)(2,1)S(1)} %collective-permute-done.4.refs_2_), channel_id=1, source_target_pairs={{0,2},{2,0},{1,3},{3,1},{4,6},{6,4},{5,7},{7,5},{8,10},{10,8},{9,1... | collective-permute-start | bytes 393224 | tf_op jit(solution)/shard_map/ppermute | solution.py:205
  25.1 2.2 %copy-start = (bf16[1,512,4096]{2,1,0:T(8,128)(2,1)S(1)}, bf16[1,512,4096]{2,1,0:T(8,128)(2,1)}, u32[]{:S(2)}) copy-start(bf16[1,512,4096]{2,1,0:T(8,128)(2,1)} %param.11) | copy-start | bytes 12582916
  26.3 6.4 %collective-permute-start.9 = (bf16[32,2048]{1,0:T(8,128)(2,1)S(1)}, bf16[32,2048]{1,0:T(8,128)(2,1)S(1)}, u32[]{:S(2)}, u32[]{:S(2)}) collective-permute-start(bf16[32,2048]{1,0:T(8,128)(2,1)S(1)} %get-tuple-element.67), channel_id=1, source_target_pairs={{0,2},{2,0},{1,3},{3,1},{4,6},{6,4},{5,7},{7,5},{8,10},{10,8},{9,1... | collective-permute-start | bytes 393224 | tf_op jit(solution)/shard_map/ppermute | solution.py:205
  27.7 7.6 %collective-permute-start.10 = (bf16[32,2048]{1,0:T(8,128)(2,1)S(1)}, bf16[32,2048]{1,0:T(8,128)(2,1)S(1)}, u32[]{:S(2)}, u32[]{:S(2)}) collective-permute-start(bf16[32,2048]{1,0:T(8,128)(2,1)S(1)} %get-tuple-element.69), channel_id=1, source_target_pairs={{0,2},{2,0},{1,3},{3,1},{4,6},{6,4},{5,7},{7,5},{8,10},{10,8},{9,1... | collective-permute-start | bytes 393224 | tf_op jit(solution)/shard_map/ppermute | solution.py:205
  28.9 8.8 %collective-permute-start.12 = (bf16[32,2048]{1,0:T(8,128)(2,1)S(1)}, bf16[32,2048]{1,0:T(8,128)(2,1)S(1)}, u32[]{:S(2)}, u32[]{:S(2)}) collective-permute-start(bf16[32,2048]{1,0:T(8,128)(2,1)S(1)} %get-tuple-element.72), channel_id=1, source_target_pairs={{0,2},{2,0},{1,3},{3,1},{4,6},{6,4},{5,7},{7,5},{8,10},{10,8},{9,1... | collective-permute-start | bytes 393224 | tf_op jit(solution)/shard_map/ppermute | solution.py:205
  32.7 10.4 %collective-permute-start.14 = (bf16[32,2048]{1,0:T(8,128)(2,1)S(1)}, bf16[32,2048]{1,0:T(8,128)(2,1)S(1)}, u32[]{:S(2)}, u32[]{:S(2)}) collective-permute-start(bf16[32,2048]{1,0:T(8,128)(2,1)S(1)} %add_convert_fusion.3), channel_id=1, source_target_pairs={{0,8},{4,12},{8,0},{12,4},{1,9},{5,13},{9,1},{13,5},{2,10},{6,14},... | collective-permute-start | bytes 393224 | tf_op jit(solution)/shard_map/ppermute | solution.py:205
  35.4 8.3 %collective-permute-start.15 = (bf16[32,2048]{1,0:T(8,128)(2,1)S(1)}, bf16[32,2048]{1,0:T(8,128)(2,1)S(1)}, u32[]{:S(2)}, u32[]{:S(2)}) collective-permute-start(bf16[32,2048]{1,0:T(8,128)(2,1)S(1)} %add_convert_fusion.2), channel_id=1, source_target_pairs={{0,4},{4,8},{8,12},{12,0},{1,5},{5,9},{9,13},{13,1},{2,6},{6,10},{... | collective-permute-start | bytes 393224 | tf_op jit(solution)/shard_map/ppermute | solution.py:205
  35.6 7.4 %collective-permute-start.11 = (bf16[32,2048]{1,0:T(8,128)(2,1)S(1)}, bf16[32,2048]{1,0:T(8,128)(2,1)S(1)}, u32[]{:S(2)}, u32[]{:S(2)}) collective-permute-start(bf16[32,2048]{1,0:T(8,128)(2,1)S(1)} %get-tuple-element.70), channel_id=1, source_target_pairs={{0,2},{2,0},{1,3},{3,1},{4,6},{6,4},{5,7},{7,5},{8,10},{10,8},{9,1... | collective-permute-start | bytes 393224 | tf_op jit(solution)/shard_map/ppermute | solution.py:205
  37.7 6.4 %collective-permute-start.13 = (bf16[32,2048]{1,0:T(8,128)(2,1)S(1)}, bf16[32,2048]{1,0:T(8,128)(2,1)S(1)}, u32[]{:S(2)}, u32[]{:S(2)}) collective-permute-start(bf16[32,2048]{1,0:T(8,128)(2,1)S(1)} %add_convert_fusion), channel_id=1, source_target_pairs={{0,12},{4,0},{8,4},{12,8},{1,13},{5,1},{9,5},{13,9},{2,14},{6,2},{... | collective-permute-start | bytes 393224 | tf_op jit(solution)/shard_map/ppermute | solution.py:205
  43.1 1.3 %collective-permute-start.18 = (bf16[16,2048]{1,0:T(8,128)(2,1)S(1)}, bf16[16,2048]{1,0:T(8,128)(2,1)S(1)}, u32[]{:S(2)}, u32[]{:S(2)}) collective-permute-start(bf16[16,2048]{1,0:T(8,128)(2,1)S(1)} %slice.18), channel_id=1, source_target_pairs={{0,1},{1,0},{2,3},{3,2},{4,5},{5,4},{6,7},{7,6},{8,9},{9,8},{10,11... | collective-permute-start | bytes 196616 | tf_op jit(solution)/shard_map/ppermute | solution.py:205
  43.1 1.5 %collective-permute-start.16 = (bf16[16,2048]{1,0:T(8,128)(2,1)S(1)}, bf16[16,2048]{1,0:T(8,128)(2,1)S(1)}, u32[]{:S(2)}, u32[]{:S(2)}) collective-permute-start(bf16[16,2048]{1,0:T(8,128)(2,1)S(1)} %slice.16), channel_id=1, source_target_pairs={{0,1},{1,0},{2,3},{3,2},{4,5},{5,4},{6,7},{7,6},{8,9},{9,8},{10,11... | collective-permute-start | bytes 196616 | tf_op jit(solution)/shard_map/ppermute | solution.py:205
  43.7 1.3 %collective-permute-start.19 = (bf16[16,2048]{1,0:T(8,128)(2,1)S(1)}, bf16[16,2048]{1,0:T(8,128)(2,1)S(1)}, u32[]{:S(2)}, u32[]{:S(2)}) collective-permute-start(bf16[16,2048]{1,0:T(8,128)(2,1)S(1)} %slice.19), channel_id=1, source_target_pairs={{0,1},{1,0},{2,3},{3,2},{4,5},{5,4},{6,7},{7,6},{8,9},{9,8},{10,11... | collective-permute-start | bytes 196616 | tf_op jit(solution)/shard_map/ppermute | solution.py:205
  44.1 1.3 %collective-permute-start.17 = (bf16[16,2048]{1,0:T(8,128)(2,1)S(1)}, bf16[16,2048]{1,0:T(8,128)(2,1)S(1)}, u32[]{:S(2)}, u32[]{:S(2)}) collective-permute-start(bf16[16,2048]{1,0:T(8,128)(2,1)S(1)} %slice.17), channel_id=1, source_target_pairs={{0,1},{1,0},{2,3},{3,2},{4,5},{5,4},{6,7},{7,6},{8,9},{9,8},{10,11... | collective-permute-start | bytes 196616 | tf_op jit(solution)/shard_map/ppermute | solution.py:205
